TPU v7x, 32 devices: a whole 2x2x4 slice. The times are simulated.
32 devices in a mesh: dp: 4 (over x, core), fsdp: 8 (over z, y).
Axes of the slice: x: 2, y: 2, z: 4, core: 2. Of those that a mesh axis runs over, the one named last changes fastest.
Arguments:
- tokens: bfloat16 [65536, 768], P(('dp', 'fsdp')), may hold values from -12 to 12
- cotangent: bfloat16 [65536, 768], P(('dp', 'fsdp')), may hold values from -6 to 6
- seg_counts: int32 [512], P(('dp', 'fsdp')), may hold values from 1 to 128, as said below
- w_qkv: float32 [768, 2304], P(('dp', 'fsdp')), may hold values from -0.109375 to 0.109375
- w_out: float32 [768, 768], P(('dp', 'fsdp')), may hold values from -0.875 to 0.875
- w_up: float32 [768, 3072], P(('dp', 'fsdp')), may hold values from -0.21875 to 0.21875
- w_down: float32 [768, 3072], P(('dp', 'fsdp')), may hold values from -0.109375 to 0.109375
- small_params: float32 [9216], P(('dp', 'fsdp')), may hold values from -1 to 6
- first_qkv: float32 [768, 2304], P(('dp', 'fsdp')), may hold values from -0.00024414062 to 0.00024414062
- second_qkv: float32 [768, 2304], P(('dp', 'fsdp')), may hold values from 1.4128508e-10 to 5.651403e-10
- first_out: float32 [768, 768], P(('dp', 'fsdp')), may hold values from -0.00024414062 to 0.00024414062
- second_out: float32 [768, 768], P(('dp', 'fsdp')), may hold values from 1.4128508e-10 to 5.651403e-10
- first_up: float32 [768, 3072], P(('dp', 'fsdp')), may hold values from -0.00024414062 to 0.00024414062
- second_up: float32 [768, 3072], P(('dp', 'fsdp')), may hold values from 1.4128508e-10 to 5.651403e-10
- first_down: float32 [768, 3072], P(('dp', 'fsdp')), may hold values from -0.00024414062 to 0.00024414062
- second_down: float32 [768, 3072], P(('dp', 'fsdp')), may hold values from 1.4128508e-10 to 5.651403e-10
- first_small: float32 [9216], P(('dp', 'fsdp')), may hold values from -0.00048828125 to 0.00048828125
- second_small: float32 [9216], P(('dp', 'fsdp')), may hold values from 5.651403e-10 to 2.2605613e-09
Outputs:
- layer_out: bfloat16 [65536, 768], P(('dp', 'fsdp'))
- grad_tokens: bfloat16 [65536, 768], P(('dp', 'fsdp'))
- grad_norm: float32 [], replicated
- new_qkv: float32 [768, 2304], P(('dp', 'fsdp'))
- moment_qkv: float32 [768, 2304], P(('dp', 'fsdp'))
- square_qkv: float32 [768, 2304], P(('dp', 'fsdp'))
- copy_qkv: bfloat16 [768, 2304], P(('dp', 'fsdp'))
- new_out: float32 [768, 768], P(('dp', 'fsdp'))
- moment_out: float32 [768, 768], P(('dp', 'fsdp'))
- square_out: float32 [768, 768], P(('dp', 'fsdp'))
- copy_out: bfloat16 [768, 768], P(('dp', 'fsdp'))
- new_up: float32 [768, 3072], P(('dp', 'fsdp'))
- moment_up: float32 [768, 3072], P(('dp', 'fsdp'))
- square_up: float32 [768, 3072], P(('dp', 'fsdp'))
- copy_up: bfloat16 [768, 3072], P(('dp', 'fsdp'))
- new_down: float32 [768, 3072], P(('dp', 'fsdp'))
- moment_down: float32 [768, 3072], P(('dp', 'fsdp'))
- square_down: float32 [768, 3072], P(('dp', 'fsdp'))
- copy_down: bfloat16 [768, 3072], P(('dp', 'fsdp'))
- new_small: float32 [9216], P(('dp', 'fsdp'))
- moment_small: float32 [9216], P(('dp', 'fsdp'))
- square_small: float32 [9216], P(('dp', 'fsdp'))
- copy_small: bfloat16 [9216], P(('dp', 'fsdp'))
Inputs may be any that keep to these rules, and one draw needn't show every extreme that they name: `seg_counts`: each device's 16 segments hold one document: every segment is full (128 tokens) except the device's last, which holds 1 to 128.
All inputs are finite; a program needn't handle non-finite values.
Results may differ from a plain program's by a relative error of at most 0.014.
The roundings to bfloat16 on the way count: a program that leaves them out, or rounds other values in their place, can miss the bound.
Values may be sent and summed in bfloat16 or wider, within the bound.
No kernel may reach another device: no remote copies, remote signals or barrier semaphores. Data moves between devices by JAX's collectives and lax.ppermute only.
A program may use at most 256 MiB of HBM per device.

v0:
```python
import jax
import jax.numpy as jnp
from jax import lax
from jax.sharding import PartitionSpec as P

HEAD_DIM = 64
SEG_LEN = 128
MICRO = 2
STEP = 10


NEG_FILL = -1e30
SCALE_QK = 0.125
LN_EPS = 1e-05
BETA_ONE = 0.9
BETA_TWO = 0.999
ADAM_EPS = 1e-08
RATE_MATRIX = 0.03
RATE_SMALL = 0.3
DECAY = 0.01
CLIP_LIMIT = 1.0


def split_small(vector, width, hidden_units):
    front = 3 * width + hidden_units
    return (
        vector[0:width],
        vector[width : 2 * width],
        vector[2 * width : 3 * width],
        vector[3 * width : front],
        vector[front : front + width],
        vector[front + width : front + 2 * width],
        vector[front + 2 * width : front + 3 * width],
        vector[front + 3 * width : front + 4 * width],
        vector[front + 4 * width : front + 5 * width],
    )


def normalize(values):
    row_mean = jnp.mean(values, axis=-1, keepdims=True)
    centred = values - row_mean
    variance = jnp.mean(centred * centred, axis=-1, keepdims=True)
    inverse = lax.rsqrt(variance + LN_EPS)
    return (centred * inverse, inverse)


def norm_back(grad_in, normed, inverse, gain):
    scaled = grad_in * gain
    return inverse * (
        scaled
        - jnp.mean(scaled, axis=-1, keepdims=True)
        - normed * jnp.mean(scaled * normed, axis=-1, keepdims=True)
    )


def plain_dot(left, right):
    return jnp.dot(left, right, preferred_element_type=jnp.float32)


def contract_rows(left, right):
    return lax.dot_general(
        left, right, (((0,), (0,)), ((), ())), preferred_element_type=jnp.float32
    )


def contract_cols(left, right):
    return lax.dot_general(
        left, right, (((1,), (1,)), ((), ())), preferred_element_type=jnp.float32
    )


def gelu_exact(values):
    return jax.nn.gelu(values, approximate=False)


def split_heads(joined_low, seg_count, heads):
    shaped = joined_low.reshape(seg_count, SEG_LEN, 3, heads, HEAD_DIM)
    return (shaped[:, :, 0], shaped[:, :, 1], shaped[:, :, 2])


def seg_scores(query, keyed, visible):
    raw = jnp.einsum("sqhd,skhd->shqk", query, keyed, preferred_element_type=jnp.float32)
    return jnp.where(visible[:, None, None, :], raw * SCALE_QK, NEG_FILL)


def forward(inputs, counts, weights):
    w_qkv, w_out, w_up, w_down, small_low = weights
    row_count, width = inputs.shape
    hidden_units = w_up.shape[1]
    seg_count = counts.shape[0]
    heads = width // HEAD_DIM
    bias_q, bias_v, bias_o, bias_up, bias_down, gain_one, shift_one, gain_two, shift_two = (
        split_small(small_low.astype(jnp.float32), width, hidden_units)
    )
    places = jnp.arange(SEG_LEN, dtype=jnp.int32)
    visible = places[None, :] < counts[:, None]
    live_rows = visible.reshape(row_count, 1).astype(jnp.float32)
    joined = plain_dot(inputs, w_qkv) + jnp.concatenate([bias_q, jnp.zeros_like(bias_q), bias_v])
    joined_low = joined.astype(jnp.bfloat16)
    query, keyed, valued = split_heads(joined_low, seg_count, heads)
    scores = seg_scores(query, keyed, visible)
    highest = jnp.max(scores, axis=-1, keepdims=True)
    totals = jnp.sum(jnp.exp(scores - highest), axis=-1, keepdims=True)
    log_total = highest + jnp.log(totals)
    probs_low = jnp.exp(scores - log_total).astype(jnp.bfloat16)
    mixed = jnp.einsum("shqk,skhd->sqhd", probs_low, valued, preferred_element_type=jnp.float32)
    mixed = mixed.reshape(row_count, width).astype(jnp.bfloat16)
    attended = contract_cols(mixed, w_out) + bias_o
    first = inputs.astype(jnp.float32) + attended
    normed_one, inverse_one = normalize(first)
    hidden = normed_one * gain_one + shift_one
    hidden_low = hidden.astype(jnp.bfloat16)
    pre_act = plain_dot(hidden_low, w_up) + bias_up
    active_low = gelu_exact(pre_act).astype(jnp.bfloat16)
    second = hidden + contract_cols(active_low, w_down) + bias_down
    normed_two, inverse_two = normalize(second)
    result = (normed_two * gain_two + shift_two) * live_rows
    stored = (
        joined_low,
        log_total,
        mixed,
        normed_one,
        inverse_one,
        hidden_low,
        pre_act,
        active_low,
        normed_two,
        inverse_two,
        live_rows,
        visible,
    )
    return (result.astype(jnp.bfloat16), stored)


def backward(inputs, grad_rows, weights, stored):
    w_qkv, w_out, w_up, w_down, small_low = weights
    row_count, width = inputs.shape
    hidden_units = w_up.shape[1]
    heads = width // HEAD_DIM
    seg_count = row_count // SEG_LEN
    bias_q, bias_v, bias_o, bias_up, bias_down, gain_one, shift_one, gain_two, shift_two = (
        split_small(small_low.astype(jnp.float32), width, hidden_units)
    )
    (
        joined_low,
        log_total,
        mixed,
        normed_one,
        inverse_one,
        hidden_low,
        pre_act,
        active_low,
        normed_two,
        inverse_two,
        live_rows,
        visible,
    ) = stored
    grad_result = grad_rows.astype(jnp.float32) * live_rows
    grad_gain_two = jnp.sum(grad_result * normed_two, axis=0)
    grad_shift_two = jnp.sum(grad_result, axis=0)
    grad_second = norm_back(grad_result, normed_two, inverse_two, gain_two)
    grad_bias_down = jnp.sum(grad_second, axis=0)
    second_low = grad_second.astype(jnp.bfloat16)
    grad_down = contract_rows(second_low, active_low)
    grad_active = plain_dot(second_low, w_down)
    grad_pre = jax.vjp(gelu_exact, pre_act)[1](grad_active)[0]
    grad_bias_up = jnp.sum(grad_pre, axis=0)
    pre_low = grad_pre.astype(jnp.bfloat16)
    grad_up = contract_rows(hidden_low, pre_low)
    grad_hidden = contract_cols(pre_low, w_up) + grad_second
    grad_gain_one = jnp.sum(grad_hidden * normed_one, axis=0)
    grad_shift_one = jnp.sum(grad_hidden, axis=0)
    grad_first = norm_back(grad_hidden, normed_one, inverse_one, gain_one)
    grad_bias_o = jnp.sum(grad_first, axis=0)
    first_low = grad_first.astype(jnp.bfloat16)
    grad_outproj = contract_rows(first_low, mixed)
    grad_mixed = (
        plain_dot(first_low, w_out)
        .astype(jnp.bfloat16)
        .reshape(seg_count, SEG_LEN, heads, HEAD_DIM)
    )
    query, keyed, valued = split_heads(joined_low, seg_count, heads)
    probs = jnp.exp(seg_scores(query, keyed, visible) - log_total)
    probs_low = probs.astype(jnp.bfloat16)
    grad_valued = jnp.einsum(
        "shqk,sqhd->skhd", probs_low, grad_mixed, preferred_element_type=jnp.float32
    )
    grad_probs = jnp.einsum(
        "sqhd,skhd->shqk", grad_mixed, valued, preferred_element_type=jnp.float32
    )
    grad_scores = probs * (grad_probs - jnp.sum(probs * grad_probs, axis=-1, keepdims=True))
    scores_low = (grad_scores * SCALE_QK).astype(jnp.bfloat16)
    grad_query = jnp.einsum(
        "shqk,skhd->sqhd", scores_low, keyed, preferred_element_type=jnp.float32
    )
    grad_keyed = jnp.einsum(
        "shqk,sqhd->skhd", scores_low, query, preferred_element_type=jnp.float32
    )
    grad_joined = jnp.stack([grad_query, grad_keyed, grad_valued], axis=2).reshape(
        row_count, 3 * width
    )
    grad_bias_q = jnp.sum(grad_query.reshape(row_count, width), axis=0)
    grad_bias_v = jnp.sum(grad_valued.reshape(row_count, width), axis=0)
    joined_grad = grad_joined.astype(jnp.bfloat16)
    grad_qkv = contract_rows(inputs, joined_grad)
    grad_inputs = contract_cols(joined_grad, w_qkv) + grad_first
    grad_small = jnp.concatenate(
        [
            grad_bias_q,
            grad_bias_v,
            grad_bias_o,
            grad_bias_up,
            grad_bias_down,
            grad_gain_one,
            grad_shift_one,
            grad_gain_two,
            grad_shift_two,
        ]
    )
    return (
        grad_inputs.astype(jnp.bfloat16),
        (grad_qkv, grad_outproj, grad_up, grad_down, grad_small),
    )


def adam_update(weight, first_moment, second_moment, grad_clip, rate, decay):
    fresh_one = BETA_ONE * first_moment + (1.0 - BETA_ONE) * grad_clip
    fresh_two = BETA_TWO * second_moment + (1.0 - BETA_TWO) * grad_clip * grad_clip
    correct_one = 1.0 - BETA_ONE**STEP
    correct_two = 1.0 - BETA_TWO**STEP
    stepped = fresh_one / correct_one / (jnp.sqrt(fresh_two / correct_two) + ADAM_EPS)
    updated = weight - rate * (stepped + decay * weight)
    return (updated, fresh_one, fresh_two, updated.astype(jnp.bfloat16))


def body(
    tokens,
    cotangent,
    seg_counts,
    w_qkv,
    w_out,
    w_up,
    w_down,
    small_params,
    first_qkv,
    second_qkv,
    first_out,
    second_out,
    first_up,
    second_up,
    first_down,
    second_down,
    first_small,
    second_small,
):
    masters = (w_qkv, w_out, w_up, w_down, small_params)
    low_qkv = w_qkv.astype(jnp.bfloat16)
    low_out = w_out.astype(jnp.bfloat16)
    low_up = w_up.astype(jnp.bfloat16)
    low_down = w_down.astype(jnp.bfloat16)
    low_small = small_params.astype(jnp.bfloat16)
    row_count = tokens.shape[0] // MICRO
    seg_count = seg_counts.shape[0] // MICRO
    out_parts = []
    grad_parts = []
    summed = None
    for micro_index in range(MICRO):
        lower = micro_index * row_count
        inputs = tokens[lower : lower + row_count]
        grad_rows = cotangent[lower : lower + row_count]
        counts = seg_counts[micro_index * seg_count : (micro_index + 1) * seg_count]
        forward_weights = (
            lax.all_gather(low_qkv, ("dp", "fsdp"), axis=0, tiled=True),
            lax.all_gather(low_out, ("dp", "fsdp"), axis=0, tiled=True),
            lax.all_gather(low_up, ("dp", "fsdp"), axis=0, tiled=True),
            lax.all_gather(low_down, ("dp", "fsdp"), axis=0, tiled=True),
            lax.all_gather(low_small, ("dp", "fsdp"), axis=0, tiled=True),
        )
        result, stored = forward(inputs, counts, forward_weights)
        backward_weights = (
            lax.all_gather(low_qkv, ("dp", "fsdp"), axis=0, tiled=True),
            lax.all_gather(low_out, ("dp", "fsdp"), axis=0, tiled=True),
            lax.all_gather(low_up, ("dp", "fsdp"), axis=0, tiled=True),
            lax.all_gather(low_down, ("dp", "fsdp"), axis=0, tiled=True),
            lax.all_gather(low_small, ("dp", "fsdp"), axis=0, tiled=True),
        )
        grad_inputs, grads = backward(inputs, grad_rows, backward_weights, stored)
        out_parts.append(result)
        grad_parts.append(grad_inputs)
        if summed is None:
            summed = tuple(grads)
        else:
            summed = tuple((earlier + fresh for earlier, fresh in zip(summed, grads)))
    summed = (
        lax.psum_scatter(summed[0], ("dp", "fsdp"), scatter_dimension=0, tiled=True),
        lax.psum_scatter(summed[1], ("dp", "fsdp"), scatter_dimension=0, tiled=True),
        lax.psum_scatter(summed[2], ("dp", "fsdp"), scatter_dimension=0, tiled=True),
        lax.psum_scatter(summed[3], ("dp", "fsdp"), scatter_dimension=0, tiled=True),
        lax.psum_scatter(summed[4], ("dp", "fsdp"), scatter_dimension=0, tiled=True),
    )
    squares = jnp.float32(0.0)
    for piece in summed:
        squares = squares + jnp.sum(piece * piece)
    total = lax.psum(squares, ("dp", "fsdp"))
    grad_norm = jnp.sqrt(total)
    factor = CLIP_LIMIT / jnp.maximum(grad_norm, CLIP_LIMIT)
    firsts = (first_qkv, first_out, first_up, first_down, first_small)
    seconds = (second_qkv, second_out, second_up, second_down, second_small)
    results = []
    for place in range(5):
        rate = RATE_SMALL if place == 4 else RATE_MATRIX
        decay = 0.0 if place == 4 else DECAY
        results.extend(
            adam_update(
                masters[place], firsts[place], seconds[place], summed[place] * factor, rate, decay
            )
        )
    return (
        jnp.concatenate(out_parts, axis=0),
        jnp.concatenate(grad_parts, axis=0),
        grad_norm,
        results[0],
        results[1],
        results[2],
        results[3],
        results[4],
        results[5],
        results[6],
        results[7],
        results[8],
        results[9],
        results[10],
        results[11],
        results[12],
        results[13],
        results[14],
        results[15],
        results[16],
        results[17],
        results[18],
        results[19],
    )


def solution(mesh):
    return jax.shard_map(
        body,
        mesh=mesh,
        in_specs=(
            P(("dp", "fsdp"), None),
            P(("dp", "fsdp"), None),
            P(("dp", "fsdp")),
            P(("dp", "fsdp"), None),
            P(("dp", "fsdp"), None),
            P(("dp", "fsdp"), None),
            P(("dp", "fsdp"), None),
            P(("dp", "fsdp")),
            P(("dp", "fsdp"), None),
            P(("dp", "fsdp"), None),
            P(("dp", "fsdp"), None),
            P(("dp", "fsdp"), None),
            P(("dp", "fsdp"), None),
            P(("dp", "fsdp"), None),
            P(("dp", "fsdp"), None),
            P(("dp", "fsdp"), None),
            P(("dp", "fsdp")),
            P(("dp", "fsdp")),
        ),
        out_specs=(
            P(("dp", "fsdp"), None),
            P(("dp", "fsdp"), None),
            P(),
            P(("dp", "fsdp"), None),
            P(("dp", "fsdp"), None),
            P(("dp", "fsdp"), None),
            P(("dp", "fsdp"), None),
            P(("dp", "fsdp"), None),
            P(("dp", "fsdp"), None),
            P(("dp", "fsdp"), None),
            P(("dp", "fsdp"), None),
            P(("dp", "fsdp"), None),
            P(("dp", "fsdp"), None),
            P(("dp", "fsdp"), None),
            P(("dp", "fsdp"), None),
            P(("dp", "fsdp"), None),
            P(("dp", "fsdp"), None),
            P(("dp", "fsdp"), None),
            P(("dp", "fsdp"), None),
            P(("dp", "fsdp")),
            P(("dp", "fsdp")),
            P(("dp", "fsdp")),
            P(("dp", "fsdp")),
        ),
        check_vma=False,
    )
```

profile of v0, /device:TPU:0, one launch (start us, length us, event | category | flops | bytes accessed | tf_op | source)
XLA Modules:
  0.0 1028.2 jit_solution(6805795564405574427)
XLA Ops:
  14.8 42.2 %all-reduce = bf16[9216]{0:T(1024)(128)(2,1)S(1)} all-reduce(bf16[9216]{0:T(1024)(128)(2,1)S(1)} %dynamic-update-slice), channel_id=1, replica_groups=mesh['dp'=4,'fsdp'=8] {'dp','fsdp'}, use_global_device_ids=true, to_apply=%add | all-reduce | flops 9216 | bytes 36864
  59.1 15.5 %all-gather.5.cloned.1.call-done = bf16[768,2304]{1,0:T(8,128)(2,1)} async-done(((bf16[24,2304]{1,0:T(8,128)(2,1)}), bf16[768,2304]{1,0:T(8,128)(2,1)}) %all-gather.5.cloned.1.call-update) | async-done | bytes 3538960 | tf_op jit(solution)/shard_map/all_gather | solution.py:273
  74.6 8.4 add_convert_fusion.1
  83.1 6.7 copy.135
  89.8 3.6 copy.178
  101.7 29.5 %all-gather.7.cloned.1.call-done = bf16[768,768]{1,0:T(8,128)(2,1)} async-done(((bf16[24,768]{1,0:T(8,128)(2,1)}), bf16[768,768]{1,0:T(8,128)(2,1)}) %all-gather.7.cloned.1.call-update) | async-done | bytes 1179664 | tf_op jit(solution)/shard_map/all_gather | solution.py:274
  131.1 4.0 fusion.193
  135.7 5.6 add_convert_fusion
  141.3 6.7 copy.141
  148.0 3.6 copy.180
  161.0 36.2 %all-gather.9.cloned.1.call-done = bf16[768,3072]{1,0:T(8,128)(2,1)} async-done(((bf16[24,3072]{1,0:T(8,128)(2,1)}), bf16[768,3072]{1,0:T(8,128)(2,1)}) %all-gather.9.cloned.1.call-update) | async-done | bytes 4718608 | tf_op jit(solution)/shard_map/all_gather | solution.py:275
  197.2 7.4 fusion.168
  204.6 4.6 copy-done.84
  209.2 63.6 %multiply_convert_fusion.1 = (bf16[1024,3072]{1,0:T(8,128)(2,1)}, f32[1024,3072]{1,0:T(8,128)}, bf16[1024,3072]{1,0:T(8,128)(2,1)}, f32[1024,3072]{1,0:T(8,128)}, f32[1024,3072]{1,0:T(8,128)}) fusion(f32[3072]{0:T(1024)S(1)} %slice.111, f32[1024,3072]{1,0:T(8,128)S(1)} %fusion.168, bf16[768,3072]{1,0:T(8,128)(2,1)S(1)} %copy-done.74, ...), kind=kOutput, calls=%fused_computation.21 | convolution fusion | flops 5251006464 | bytes 70805504 | tf_op jit(solution)/shard_map/dot_general | solution.py:57
  272.8 9.7 fusion.196
  283.2 5.4 fusion.195
  290.5 4.2 multiply_reduce_fusion.2
  294.7 5.9 fusion.183
  300.6 19.4 %fusion.199 = (f32[3072]{0:T(1024)}, bf16[1024,3072]{1,0:T(8,128)(2,1)}) fusion(f32[1024,3072]{1,0:T(8,128)} %get-tuple-element.140, bf16[768,3072]{1,0:T(8,128)(2,1)} %all-gather.11.cloned.1.call-done, f32[1024,768]{1,0:T(8,128)} %get-tuple-element.153, f32[1024,3072]{1,0:T(8,128)} %get-tuple-element.182, f32[3072]{0:T(1024)S(1)} %slice.111), kind=kOutput, calls=%fused_computation.298 | convolution fusion | flops 4882953216 | bytes 39346176 | tf_op jit(solution)/shard_map/dot_general | solution.py:57
  320.0 11.8 %multiply_reduce_fusion.5 = (f32[768]{0:T(1024)}, f32[1024]{0:T(1024)S(1)}, f32[1024]{0:T(1024)S(1)}, f32[768]{0:T(1024)}, f32[1024,768]{1,0:T(8,128)}) fusion(f32[1024,768]{1,0:T(8,128)S(1)} %copy-done.4, f32[1024]{0:T(1024)S(1)} %add_rsqrt_fusion.3, f32[1024]{0:T(1024)S(1)} %broadcast_multiply_fusion.11, f32[768]{0:T(1024)S(1)} %get-tuple-element.157, ...), kind=kOutput, calls=%fused_computation.85 | convolution fusion | flops 4839698432 | bytes 20472832 | tf_op jit(solution)/shard_map/dot_general | solution.py:67
  331.8 18.6 %fusion.202 = (f32[3072]{0:T(1024)S(1)}, bf16[1024,3072]{1,0:T(8,128)(2,1)}) fusion(f32[1024,3072]{1,0:T(8,128)} %get-tuple-element.163, bf16[768,3072]{1,0:T(8,128)(2,1)} %all-gather.11.cloned.1.call-done, f32[1024,768]{1,0:T(8,128)} %get-tuple-element.132, f32[1024,3072]{1,0:T(8,128)} %copy-done.84, f32[3072]{0:T(1024)S(1)} %slice.111), kind=kOutput, calls=%fused_computation.299 | convolution fusion | flops 4882953216 | bytes 39346176 | tf_op jit(solution)/shard_map/dot_general | solution.py:57
  350.4 12.7 %fusion.186 = (f32[768]{0:T(1024)S(1)}, f32[1024,768]{1,0:T(8,128)S(1)}, f32[768]{0:T(1024)S(1)}, f32[1024]{0:T(1024)S(1)}, f32[1024]{0:T(1024)S(1)}, /*index=5*/f32[768]{0:T(1024)S(1)}, f32[1024,768]{1,0:T(8,128)}) fusion(f32[1024]{0:T(1024)S(1)} %broadcast_multiply_fusion.4, f32[1024,768]{1,0:T(8,128)S(1)} %copy-done.4, ...), kind=kOutput, calls=%fused_computation.289 | convolution fusion | flops 4845988864 | bytes 29929472 | tf_op jit(solution)/shard_map/dot_general | solution.py:67
  367.3 3.0 copy.147
  372.3 3.8 fusion.103
  376.1 6.4 bitcast_reduce_fusion.2
  382.4 14.1 %bitcast_reduce_fusion.3 = (f32[12,64]{1,0:T(8,128)S(1)}, bf16[8,12,64,128]{3,2,1,0:T(8,128)(2,1)}) fusion(f32[8,12,128,128]{2,3,1,0:T(8,128)} %fusion.103, f32[8,12,128]{2,1,0:T(8,128)S(1)} %copy-done.52, f32[8,12,128,128]{2,3,1,0:T(8,128)} %copy-done.17, pred[8,128]{1,0:T(8,128)(4,1)S(1)} %copy-done.71, bf16[8,128,1,12,64]{1,0,4,3,2:T(8,128)(2,1)} %copy-done.25), kind=kOutput, calls=%fused_computation.80 | convolution fusion | flops 220212608 | bytes 15781888 | tf_op jit(solution)/shard_map/shqk,skhd->sqhd/dot_general | solution.py:193
  396.6 13.7 %fusion.95 = bf16[8,128,1,12,64]{1,4,3,0,2:T(8,128)(2,1)} fusion(f32[8,12,128,128]{2,3,1,0:T(8,128)} %fusion.103, f32[8,12,128]{2,1,0:T(8,128)S(1)} %copy-done.52, f32[8,12,128,128]{2,3,1,0:T(8,128)} %copy-done.17, pred[8,128]{1,0:T(8,128)(4,1)S(1)} %copy-done.71, bf16[8,128,1,12,64]{1,0,4,3,2:T(8,128)(2,1)} %copy-done.24), kind=kOutput, calls=%fused_computation.162 | convolution fusion | flops 219426944 | bytes 15778816 | tf_op jit(solution)/shard_map/shqk,sqhd->skhd/dot_general | solution.py:196
  413.0 3.0 fusion.86
  424.4 3.8 fusion.105
  428.2 14.2 %bitcast_reduce_fusion.1 = (f32[12,64]{1,0:T(8,128)S(1)}, bf16[8,12,64,128]{3,2,1,0:T(8,128)(2,1)}) fusion(f32[8,12,128,128]{2,3,1,0:T(8,128)} %fusion.105, f32[8,12,128]{2,1,0:T(8,128)S(1)} %copy-done.50, f32[8,12,128,128]{2,3,1,0:T(8,128)} %copy-done.16, pred[8,128]{1,0:T(8,128)(4,1)S(1)} %copy-done.69, bf16[8,128,1,12,64]{1,0,4,3,2:T(8,128)(2,1)} %copy-done.27), kind=kOutput, calls=%fused_computation.76 | convolution fusion | flops 220212608 | bytes 15781888 | tf_op jit(solution)/shard_map/shqk,skhd->sqhd/dot_general | solution.py:193
  442.5 13.9 %fusion.98 = bf16[8,128,1,12,64]{1,4,3,0,2:T(8,128)(2,1)} fusion(f32[8,12,128,128]{2,3,1,0:T(8,128)} %fusion.105, f32[8,12,128]{2,1,0:T(8,128)S(1)} %copy-done.50, f32[8,12,128,128]{2,3,1,0:T(8,128)} %copy-done.16, pred[8,128]{1,0:T(8,128)(4,1)S(1)} %copy-done.69, bf16[8,128,1,12,64]{1,0,4,3,2:T(8,128)(2,1)} %copy-done.26), kind=kOutput, calls=%fused_computation.163 | convolution fusion | flops 219426944 | bytes 15778816 | tf_op jit(solution)/shard_map/shqk,sqhd->skhd/dot_general | solution.py:196
  456.3 6.1 fusion.92
  465.6 9.3 copy.153
  480.3 9.3 copy.160
  489.6 5.9 fusion.21
  495.5 8.1 add_bitcast_fusion
  503.6 8.0 copy.170
  512.3 9.0 fusion.51
  521.3 11.1 %convolution_add_fusion.1 = f32[768,3072]{1,0:T(8,128)} fusion(f32[768,3072]{1,0:T(8,128)S(1)} %fusion.51, bf16[1024,3072]{1,0:T(8,128)(2,1)} %get-tuple-element.200, f32[1024,768]{1,0:T(8,128)S(1)} %copy-done.1, f32[1024]{0:T(1024)S(1)} %copy-done.44, f32[1024]{0:T(1024)S(1)} %copy-done.40, f32[768]{0:T(1024)S(1)} %copy-done.38, ...), kind=kOutput, calls=%fused_computation.52 | convolution fusion | flops 4838129664 | bytes 28325888 | tf_op jit(solution)/shard_map/dot_general | solution.py:61
  532.5 8.3 fusion.127
  540.8 10.4 %convolution_add_fusion = f32[768,3072]{1,0:T(8,128)} fusion(f32[768,3072]{1,0:T(8,128)S(1)} %fusion.127, bf16[1024,3072]{1,0:T(8,128)(2,1)} %get-tuple-element.162, f32[1024,768]{1,0:T(8,128)S(1)} %copy-done.6), kind=kOutput, calls=%fused_computation.51 | convolution fusion | flops 4834983936 | bytes 28311552 | tf_op jit(solution)/shard_map/dot_general | solution.py:61
  552.1 40.2 %all-reduce.1 = f32[9216]{0:T(1024)S(1)} all-reduce(f32[9216]{0:T(1024)S(1)} %add.307), channel_id=6, replica_groups=mesh['dp'=4,'fsdp'=8] {'dp','fsdp'}, use_global_device_ids=true, to_apply=%region_48.49.clone | all-reduce | flops 9216 | bytes 73728
  593.1 7.8 add_convert_fusion.3
  600.8 6.5 add_convert_fusion.2
  610.9 74.1 %reduce-scatter.13.cloned.1.call-done = f32[24,2304]{1,0:T(8,128)} async-done(((f32[768,2304]{1,0:T(8,128)}), f32[24,2304]{1,0:T(8,128)}) %reduce-scatter.13.cloned.1.call-update) | async-done | bytes 221200 | tf_op jit(solution)/shard_map/reduce_scatter | solution.py:295
  690.9 134.7 %reduce-scatter.9.cloned.1.call-done = f32[24,3072]{1,0:T(8,128)} async-done(((f32[768,3072]{1,0:T(8,128)}), f32[24,3072]{1,0:T(8,128)}) %reduce-scatter.9.cloned.1.call-update) | async-done | bytes 294928 | tf_op jit(solution)/shard_map/reduce_scatter | solution.py:297
  827.9 139.5 %reduce-scatter.11.cloned.1.call-done = f32[24,3072]{1,0:T(8,128)} async-done(((f32[768,3072]{1,0:T(8,128)}), f32[24,3072]{1,0:T(8,128)}) %reduce-scatter.11.cloned.1.call-update) | async-done | bytes 294928 | tf_op jit(solution)/shard_map/reduce_scatter | solution.py:298
  972.3 39.8 %psum.7 = f32[]{:T(128)} all-reduce(f32[]{:T(128)S(6)} %add.308), channel_id=1, replica_groups=mesh['dp'=4,'fsdp'=8] {'dp','fsdp'}, use_global_device_ids=true, to_apply=%region_50.51 | all-reduce | flops 1 | bytes 8 | tf_op jit(solution)/shard_map/psum | solution.py:304
  (289 shorter events, 78.0 us)
Async XLA Ops:
  7.2 67.4 %all-gather.5.cloned.1.call-start = ((), (), s32[]{:S(2)}) async-start(), calls=%async_computation.4 | async-start | bytes 3649536 | tf_op jit(solution)/shard_map/all_gather | solution.py:273
  8.9 122.3 %all-gather.7.cloned.1.call-start = ((), (), s32[]{:S(2)}) async-start(), calls=%async_computation.5 | async-start | bytes 1216512 | tf_op jit(solution)/shard_map/all_gather | solution.py:274
  10.4 186.8 %all-gather.9.cloned.1.call-start = ((), (), s32[]{:S(2)}) async-start(), calls=%async_computation.6 | async-start | bytes 4866048 | tf_op jit(solution)/shard_map/all_gather | solution.py:275
  12.2 260.6 %all-gather.11.cloned.1.call-start = ((), (), s32[]{:S(2)}) async-start(), calls=%async_computation.7 | async-start | bytes 4866048 | tf_op jit(solution)/shard_map/all_gather | solution.py:276
  13.9 595.3 %reduce-scatter.7.cloned.1.call-start = ((), (), s32[]{:S(2)}) async-start(), calls=%async_computation.8 | async-start | bytes 2433024 | tf_op jit(solution)/shard_map/reduce_scatter | solution.py:296
  57.6 225.5 %copy-start.37 = (f32[768]{0:T(1024)}, f32[768]{0:T(1024)S(1)}, u32[]{:S(2)}) copy-start(f32[768]{0:T(1024)S(1)} %get-tuple-element.158) | copy-start | bytes 9220
  59.1 38.3 %copy-start.70 = (pred[8,128]{1,0:T(8,128)(4,1)}, pred[8,128]{1,0:T(8,128)(4,1)S(1)}, u32[]{:S(2)}) copy-start(pred[8,128]{1,0:T(8,128)(4,1)S(1)} %get-tuple-element.201) | copy-start | bytes 3076
  59.1 96.5 %copy-start.68 = (pred[8,128]{1,0:T(8,128)(4,1)}, pred[8,128]{1,0:T(8,128)(4,1)S(1)}, u32[]{:S(2)}) copy-start(pred[8,128]{1,0:T(8,128)(4,1)S(1)} %get-tuple-element.173) | copy-start | bytes 3076
  160.4 44.1 %copy-start = (f32[1024,768]{1,0:T(8,128)}, f32[1024,768]{1,0:T(8,128)S(1)}, u32[]{:S(2)}) copy-start(f32[1024,768]{1,0:T(8,128)S(1)} %get-tuple-element.181) | copy-start | bytes 9437188
  160.4 44.1 %copy-start.39 = (f32[1024]{0:T(1024)}, f32[1024]{0:T(1024)S(1)}, u32[]{:S(2)}) copy-start(f32[1024]{0:T(1024)S(1)} %broadcast_multiply_fusion.9) | copy-start | bytes 12292
  161.0 43.6 %copy-start.43 = (f32[1024]{0:T(1024)}, f32[1024]{0:T(1024)S(1)}, u32[]{:S(2)}) copy-start(f32[1024]{0:T(1024)S(1)} %add_rsqrt_fusion.1) | copy-start | bytes 12292
  197.2 12.0 %copy-start.3 = (f32[1024,768]{1,0:T(8,128)S(1)}, f32[1024,768]{1,0:T(8,128)}, u32[]{:S(2)}) copy-start(f32[1024,768]{1,0:T(8,128)} %copy-done.2) | copy-start | bytes 9437188
  197.2 12.0 %copy-start.74 = (bf16[768,3072]{1,0:T(8,128)(2,1)S(1)}, bf16[768,3072]{1,0:T(8,128)(2,1)}, u32[]{:S(2)}) copy-start(bf16[768,3072]{1,0:T(8,128)(2,1)} %all-gather.9.cloned.1.call-done) | copy-start | bytes 14155780
  209.2 63.6 %copy-start.65 = (f32[768]{0:T(1024)S(1)}, f32[768]{0:T(1024)}, u32[]{:S(2)}) copy-start(f32[768]{0:T(1024)} %get-tuple-element.156) | copy-start | bytes 9220
  272.8 10.3 %copy-start.1 = (f32[1024,768]{1,0:T(8,128)S(1)}, f32[1024,768]{1,0:T(8,128)}, u32[]{:S(2)}) copy-start(f32[1024,768]{1,0:T(8,128)} %copy-done) | copy-start | bytes 9437188
  272.8 10.3 %copy-start.7 = (bf16[1024,3072]{1,0:T(8,128)(2,1)S(1)}, bf16[1024,3072]{1,0:T(8,128)(2,1)}, u32[]{:S(2)}) copy-start(bf16[1024,3072]{1,0:T(8,128)(2,1)} %get-tuple-element.162) | copy-start | bytes 18874372
  272.8 10.3 %copy-start.40 = (f32[1024]{0:T(1024)S(1)}, f32[1024]{0:T(1024)}, u32[]{:S(2)}) copy-start(f32[1024]{0:T(1024)} %copy-done.39) | copy-start | bytes 12292
  272.8 10.3 %copy-start.44 = (f32[1024]{0:T(1024)S(1)}, f32[1024]{0:T(1024)}, u32[]{:S(2)}) copy-start(f32[1024]{0:T(1024)} %copy-done.43) | copy-start | bytes 12292
  272.8 10.3 %copy-start.75 = (bf16[768,3072]{1,0:T(8,128)(2,1)S(1)}, bf16[768,3072]{1,0:T(8,128)(2,1)}, u32[]{:S(2)}) copy-start(bf16[768,3072]{1,0:T(8,128)(2,1)} %all-gather.11.cloned.1.call-done) | copy-start | bytes 14155780
  300.6 19.4 %copy-start.4 = (f32[1024,768]{1,0:T(8,128)S(1)}, f32[1024,768]{1,0:T(8,128)}, u32[]{:S(2)}) copy-start(f32[1024,768]{1,0:T(8,128)} %copy-done.2) | copy-start | bytes 9437188
  350.4 14.3 %copy-start.82 = (bf16[768,768]{1,0:T(8,128)(2,1)S(1)}, bf16[768,768]{1,0:T(8,128)(2,1)}, u32[]{:S(2)}) copy-start(bf16[768,768]{1,0:T(8,128)(2,1)} %all-gather.7.cloned.1.call-done) | copy-start | bytes 3538948
  462.5 222.6 %reduce-scatter.13.cloned.1.call-start = ((), (), s32[]{:S(2)}) async-start(), calls=%async_computation.11 | async-start | bytes 7299072 | tf_op jit(solution)/shard_map/reduce_scatter | solution.py:295
  464.9 10.2 slice-start
  465.6 9.4 copy-start.33
  465.6 9.5 copy-start.15
  465.6 9.5 slice-start.1
  475.0 14.7 %copy-start.18 = (bf16[8,128,3,12,64]{1,0,4,3,2:T(8,128)(2,1)}, bf16[8,128,3,12,64]{1,0,4,3,2:T(8,128)(2,1)S(1)}, u32[]{:S(2)}) copy-start(bf16[8,128,3,12,64]{1,0,4,3,2:T(8,128)(2,1)S(1)} %copy.153) | copy-start | bytes 14155780
  480.3 9.3 copy-start.80
  511.7 314.0 %reduce-scatter.9.cloned.1.call-start = ((), (), s32[]{:S(2)}) async-start(), calls=%async_computation.9 | async-start | bytes 9732096 | tf_op jit(solution)/shard_map/reduce_scatter | solution.py:297
  532.4 8.4 copy-start.6
  532.4 435.0 %reduce-scatter.11.cloned.1.call-start = ((), (), s32[]{:S(2)}) async-start(), calls=%async_computation.10 | async-start | bytes 9732096 | tf_op jit(solution)/shard_map/reduce_scatter | solution.py:298
  551.3 41.8 %copy-start.21 = (f32[1024,768]{1,0:T(8,128)S(1)}, f32[1024,768]{1,0:T(8,128)}, u32[]{:S(2)}) copy-start(f32[1024,768]{1,0:T(8,128)} %copy-done.20) | copy-start | bytes 9437188
  593.0 7.8 copy-start.23
  593.1 7.8 copy-start.77
  607.3 363.1 %copy-start.12 = (bf16[1024,768]{1,0:T(8,128)(2,1)S(1)}, bf16[1024,768]{1,0:T(8,128)(2,1)}, u32[]{:S(2)}) copy-start(bf16[1024,768]{1,0:T(8,128)(2,1)} %get-tuple-element.150) | copy-start | bytes 4718596
  607.3 363.1 %copy-start.13 = (bf16[1024,768]{1,0:T(8,128)(2,1)S(1)}, bf16[1024,768]{1,0:T(8,128)(2,1)}, u32[]{:S(2)}) copy-start(bf16[1024,768]{1,0:T(8,128)(2,1)} %get-tuple-element.151) | copy-start | bytes 4718596
  689.5 323.3 %copy-start.64 = (f32[288]{0:T(512)S(1)}, f32[288]{0:T(512)}, u32[]{:S(2)}) copy-start(f32[288]{0:T(512)} %param.25) | copy-start | bytes 3460
  689.5 323.3 %copy-start.72 = (f32[288]{0:T(512)S(1)}, f32[288]{0:T(512)}, u32[]{:S(2)}) copy-start(f32[288]{0:T(512)} %param.34) | copy-start | bytes 3460
  689.5 323.3 %copy-start.73 = (f32[288]{0:T(512)S(1)}, f32[288]{0:T(512)}, u32[]{:S(2)}) copy-start(f32[288]{0:T(512)} %param.35) | copy-start | bytes 3460
  689.5 324.0 %copy-start.34 = (f32[24,3072]{1,0:T(8,128)S(1)}, f32[24,3072]{1,0:T(8,128)}, u32[]{:S(2)}) copy-start(f32[24,3072]{1,0:T(8,128)} %param.24) | copy-start | bytes 884740
  972.3 45.9 %copy-start.41 = (f32[24,768]{1,0:T(8,128)S(1)}, f32[24,768]{1,0:T(8,128)}, u32[]{:S(2)}) copy-start(f32[24,768]{1,0:T(8,128)} %param.22) | copy-start | bytes 221188
  972.3 45.9 %copy-start.42 = (f32[24,768]{1,0:T(8,128)S(1)}, f32[24,768]{1,0:T(8,128)}, u32[]{:S(2)}) copy-start(f32[24,768]{1,0:T(8,128)} %reduce-scatter.7.cloned.1.call-done) | copy-start | bytes 221188
  972.3 45.9 %copy-start.47 = (f32[24,768]{1,0:T(8,128)S(1)}, f32[24,768]{1,0:T(8,128)}, u32[]{:S(2)}) copy-start(f32[24,768]{1,0:T(8,128)} %param.28) | copy-start | bytes 221188
  972.3 45.9 %copy-start.48 = (f32[24,768]{1,0:T(8,128)S(1)}, f32[24,768]{1,0:T(8,128)}, u32[]{:S(2)}) copy-start(f32[24,768]{1,0:T(8,128)} %param.29) | copy-start | bytes 221188
  972.3 46.6 %copy-start.35 = (f32[24,2304]{1,0:T(8,128)S(1)}, f32[24,2304]{1,0:T(8,128)}, u32[]{:S(2)}) copy-start(f32[24,2304]{1,0:T(8,128)} %param.21) | copy-start | bytes 663556
  972.3 46.6 %copy-start.36 = (f32[24,2304]{1,0:T(8,128)S(1)}, f32[24,2304]{1,0:T(8,128)}, u32[]{:S(2)}) copy-start(f32[24,2304]{1,0:T(8,128)} %reduce-scatter.13.cloned.1.call-done) | copy-start | bytes 663556
  972.3 46.6 %copy-start.45 = (f32[24,2304]{1,0:T(8,128)S(1)}, f32[24,2304]{1,0:T(8,128)}, u32[]{:S(2)}) copy-start(f32[24,2304]{1,0:T(8,128)} %param.26) | copy-start | bytes 663556
  972.3 46.6 %copy-start.46 = (f32[24,2304]{1,0:T(8,128)S(1)}, f32[24,2304]{1,0:T(8,128)}, u32[]{:S(2)}) copy-start(f32[24,2304]{1,0:T(8,128)} %param.27) | copy-start | bytes 663556
  (47 other events, 129.6 us)
Sparse Core Ops, SparseCore 0:
  11.5 63.0 all-gather.4
  78.1 52.9 all-gather.6
  134.6 62.5 all-gather.8
  200.5 62.4 all-gather.10
  462.6 97.8 reduce-scatter.6
  567.0 118.0 reduce-scatter.12
  690.9 134.6 reduce-scatter.8
  832.5 134.8 reduce-scatter.10
where the time goes:
time: 1040 us; the launch traced here: 1030 us
  waiting for transfers between devices  430 us (41%)
  matrix products  330 us (32%)
  blocking collectives  122 us (12%)
  local copies, waits for them, and re-layouts  79.1 us (8%)
  other arithmetic  45.8 us (4%)
  between operations  21.2 us (2%)
    reduce_scatter x1, waiting for transfers between devices, body(): lax.psum_scatter(summed[3], ('dp', 'fsdp'), scatter_dimension=0, tiled=True)  140 us
    reduce_scatter x1, waiting for transfers between devices, body(): lax.psum_scatter(summed[2], ('dp', 'fsdp'), scatter_dimension=0, tiled=True)  135 us
    dot_general x8, matrix products, plain_dot(): return jnp.dot(left, right, preferred_element_type=jnp.float32)  128 us
    unnamed x2, blocking collectives  82.4 us
    reduce_scatter x1, waiting for transfers between devices, body(): lax.psum_scatter(summed[0], ('dp', 'fsdp'), scatter_dimension=0, tiled=True)  74.1 us
    dot_general x8, matrix products, contract_rows(): lax.dot_general(left, right, (((0,), (0,)), ((), ())), preferred_element_...  61.8 us
    dot_general x8, matrix products, contract_cols(): lax.dot_general(left, right, (((1,), (1,)), ((), ())), preferred_element_...  59.4 us
    psum x1, blocking collectives, body(): total = lax.psum(squares, ('dp', 'fsdp'))  39.8 us
  transfers between devices with their start and end apart: 8, of which 6 were waited for; matrix products, arithmetic and copies ran while one was open for 24% of the time, Pallas kernels for 0%

commit v1 on v0

v1 whole, which is shorter than its diff:
```python
import functools
import math

import jax
import jax.numpy as jnp
from jax import lax
from jax.experimental import pallas as pl
from jax.experimental.pallas import tpu as pltpu
from jax.sharding import Mesh
from jax.sharding import PartitionSpec as P

HEAD_DIM = 64
SEG_LEN = 128
STEP = 10
NEG_FILL = -1e30
SCALE_QK = 0.125
LN_EPS = 1e-05
BETA_ONE = 0.9
BETA_TWO = 0.999
ADAM_EPS = 1e-08
RATE_MATRIX = 0.03
RATE_SMALL = 0.3
DECAY = 0.01
CLIP_LIMIT = 1.0

LANES = 128
VMEM_LIMIT = 60 * 1024 * 1024
F32 = jnp.float32
BF16 = jnp.bfloat16
ALL = ("hi", "core", "fsdp")
PEERS = ("hi", "fsdp")


def dot_nn(left, right):
    return jnp.dot(left, right, preferred_element_type=F32)


def dot_nt(left, right):
    return lax.dot_general(left, right, (((1,), (1,)), ((), ())), preferred_element_type=F32)


def dot_tn(left, right):
    return lax.dot_general(left, right, (((0,), (0,)), ((), ())), preferred_element_type=F32)


def small_places(width, hidden):
    front = 3 * width + hidden
    return {
        "bq": (0, width),
        "bv": (width, 2 * width),
        "bo": (2 * width, 3 * width),
        "b1": (3 * width, front),
        "b2": (front, front + width),
        "g1": (front + width, front + 2 * width),
        "s1": (front + 2 * width, front + 3 * width),
        "g2": (front + 3 * width, front + 4 * width),
        "s2": (front + 4 * width, front + 5 * width),
    }


def normalize(values):
    row_mean = jnp.mean(values, axis=-1, keepdims=True)
    centred = values - row_mean
    variance = jnp.mean(centred * centred, axis=-1, keepdims=True)
    inverse = lax.rsqrt(variance + LN_EPS)
    return centred * inverse, inverse


def norm_back(scaled, normed, inverse):
    return inverse * (
        scaled
        - jnp.mean(scaled, axis=-1, keepdims=True)
        - normed * jnp.mean(scaled * normed, axis=-1, keepdims=True)
    )


def fold_rows(values):
    return jnp.sum(values.reshape(values.shape[0] // 8, 8, values.shape[1]), axis=0)


def head_halves(pair):
    lane = lax.broadcasted_iota(jnp.int32, pair.shape, 1)
    zero = jnp.zeros_like(pair)
    return jnp.concatenate(
        [jnp.where(lane < HEAD_DIM, pair, zero), jnp.where(lane < HEAD_DIM, zero, pair)], axis=0
    )


def stack_heads(wide):
    return jnp.concatenate([wide[:, :SEG_LEN], wide[:, SEG_LEN:]], axis=0)


def row_spec(rows, columns):
    return pl.BlockSpec((rows, columns), lambda step, *_: (step, 0))


def held_spec(rows, columns, place=0):
    return pl.BlockSpec(
        (rows, columns), lambda step, *_: (0, place), pipeline_mode=pl.Buffered(1)
    )


def params():
    return pltpu.CompilerParams(vmem_limit_bytes=VMEM_LIMIT)


def attention_forward_body(
    counts, inputs, w_qkv, w_out, small, joined_out, probs_out, mixed_out, normed_out, inverse_out
):
    rows, width = inputs.shape
    at = small_places(width, small.shape[1] - 8 * width)
    values = inputs[...]
    for part, bias in ((0, "bq"), (1, None), (2, "bv")):
        columns = slice(part * width, (part + 1) * width)
        product = dot_nn(values, w_qkv[:, columns])
        if bias is not None:
            product = product + small[:, slice(*at[bias])]
        joined_out[:, columns] = product.astype(BF16)
    for segment in range(rows // SEG_LEN):
        place = slice(segment * SEG_LEN, (segment + 1) * SEG_LEN)
        count = counts[pl.program_id(0) * (rows // SEG_LEN) + segment]
        visible = lax.broadcasted_iota(jnp.int32, (SEG_LEN, 2 * SEG_LEN), 0) < count
        for pair in range(width // LANES):
            low, high = pair * LANES, (pair + 1) * LANES
            query = joined_out[place, low:high] * jnp.asarray(SCALE_QK, BF16)
            keyed = joined_out[place, width + low : width + high]
            valued = joined_out[place, 2 * width + low : 2 * width + high]
            scores = jnp.where(visible, dot_nt(keyed, head_halves(query)), NEG_FILL)
            raised = jnp.exp(scores - jnp.max(scores, axis=0, keepdims=True))
            probs = raised * (1.0 / jnp.sum(raised, axis=0, keepdims=True))
            probs_out[place, 2 * low : 2 * high] = probs
            mixed = dot_tn(stack_heads(probs.astype(BF16)), head_halves(valued))
            mixed_out[place, low:high] = mixed.astype(BF16)
    attended = dot_nt(mixed_out[...], w_out[...]) + small[:, slice(*at["bo"])]
    normed, inverse = normalize(values.astype(F32) + attended)
    normed_out[...] = normed
    inverse_out[...] = jnp.broadcast_to(inverse, inverse_out.shape)


def attention_forward(inputs, counts, packed, small, block=256):
    rows, width = inputs.shape
    return pl.pallas_call(
        attention_forward_body,
        grid_spec=pltpu.PrefetchScalarGridSpec(
            num_scalar_prefetch=1,
            grid=(rows // block,),
            in_specs=[
                row_spec(block, width),
                held_spec(width, 3 * width),
                held_spec(width, width, 3),
                held_spec(1, small.shape[1]),
            ],
            out_specs=[
                row_spec(block, 3 * width),
                row_spec(block, 2 * width),
                row_spec(block, width),
                row_spec(block, width),
                row_spec(block, LANES),
            ],
        ),
        out_shape=[
            jax.ShapeDtypeStruct((rows, 3 * width), BF16),
            jax.ShapeDtypeStruct((rows, 2 * width), F32),
            jax.ShapeDtypeStruct((rows, width), BF16),
            jax.ShapeDtypeStruct((rows, width), F32),
            jax.ShapeDtypeStruct((rows, LANES), F32),
        ],
        compiler_params=params(),
        name="attention_forward",
    )(counts, inputs, packed, packed, small)


def mlp_forward_body(
    counts,
    normed_one,
    cotangent,
    w_up,
    w_down,
    small,
    result_out,
    active_out,
    slope_out,
    second_out,
    sums_out,
):
    rows, width = normed_one.shape
    step = pl.program_id(0)
    at = small_places(width, small.shape[1] - 8 * width)
    hidden = normed_one[...] * small[:, slice(*at["g1"])] + small[:, slice(*at["s1"])]
    pre_act = dot_nn(hidden.astype(BF16), w_up[...]) + small[:, slice(*at["b1"])]
    spread = 0.5 * (1.0 + lax.erf(pre_act * math.sqrt(0.5)))
    density = jnp.exp(-0.5 * pre_act * pre_act) * (1.0 / math.sqrt(2.0 * math.pi))
    active = (pre_act * spread).astype(BF16)
    active_out[...] = active
    slope_out[...] = spread + pre_act * density
    second = hidden + dot_nt(active, w_down[...]) + small[:, slice(*at["b2"])]
    normed, inverse = normalize(second)
    gain = small[:, slice(*at["g2"])]
    index = lax.broadcasted_iota(jnp.int32, (SEG_LEN, 1), 0)
    live = jnp.concatenate(
        [
            (index < counts[step * (rows // SEG_LEN) + segment]).astype(F32)
            for segment in range(rows // SEG_LEN)
        ],
        axis=0,
    )
    result_out[...] = ((normed * gain + small[:, slice(*at["s2"])]) * live).astype(BF16)
    incoming = cotangent[...].astype(F32) * live
    grad_second = norm_back(incoming * gain, normed, inverse)
    second_out[...] = grad_second

    @pl.when(step == 0)
    def _():
        sums_out[...] = jnp.zeros_like(sums_out)

    sums_out[0] += fold_rows(incoming * normed)
    sums_out[1] += fold_rows(incoming)
    sums_out[2] += fold_rows(grad_second)


def mlp_forward(normed_one, counts, cotangent, packed, small, block=256):
    rows, width = normed_one.shape
    hidden = packed.shape[1] // 2
    return pl.pallas_call(
        mlp_forward_body,
        grid_spec=pltpu.PrefetchScalarGridSpec(
            num_scalar_prefetch=1,
            grid=(rows // block,),
            in_specs=[
                row_spec(block, width),
                row_spec(block, width),
                held_spec(width, hidden),
                held_spec(width, hidden, 1),
                held_spec(1, small.shape[1]),
            ],
            out_specs=[
                row_spec(block, width),
                row_spec(block, hidden),
                row_spec(block, hidden),
                row_spec(block, width),
                pl.BlockSpec((3, 8, width), lambda step, *_: (0, 0, 0)),
            ],
        ),
        out_shape=[
            jax.ShapeDtypeStruct((rows, width), BF16),
            jax.ShapeDtypeStruct((rows, hidden), BF16),
            jax.ShapeDtypeStruct((rows, hidden), F32),
            jax.ShapeDtypeStruct((rows, width), F32),
            jax.ShapeDtypeStruct((3, 8, width), F32),
        ],
        compiler_params=params(),
        name="mlp_forward",
    )(counts, normed_one, cotangent, packed, packed, small)


def mlp_backward_body(
    grad_second, slope, normed_one, inverse_one, w_up, w_down, small, pre_out, first_out, sums_out, wide_out
):
    rows, width = normed_one.shape
    hidden = slope.shape[1]
    chunk = width
    at = small_places(width, hidden)

    @pl.when(pl.program_id(0) == 0)
    def _():
        sums_out[...] = jnp.zeros_like(sums_out)
        wide_out[...] = jnp.zeros_like(wide_out)

    incoming = grad_second[...]
    incoming_low = incoming.astype(BF16)
    grad_hidden = incoming
    for piece in range(hidden // chunk):
        columns = slice(piece * chunk, (piece + 1) * chunk)
        grad_pre = dot_nn(incoming_low, w_down[:, columns]) * slope[:, columns]
        wide_out[:, columns] += fold_rows(grad_pre)
        grad_low = grad_pre.astype(BF16)
        pre_out[:, columns] = grad_low
        grad_hidden = grad_hidden + dot_nt(grad_low, w_up[:, columns])
    normed = normed_one[...]
    sums_out[0] += fold_rows(grad_hidden * normed)
    sums_out[1] += fold_rows(grad_hidden)
    grad_first = norm_back(
        grad_hidden * small[:, slice(*at["g1"])], normed, inverse_one[:, :1]
    )
    first_out[...] = grad_first
    sums_out[2] += fold_rows(grad_first)


def mlp_backward(grad_second, slope, normed_one, inverse_one, packed, small, block=256):
    rows, width = normed_one.shape
    hidden = slope.shape[1]
    return pl.pallas_call(
        mlp_backward_body,
        grid=(rows // block,),
        in_specs=[
            row_spec(block, width),
            row_spec(block, hidden),
            row_spec(block, width),
            row_spec(block, LANES),
            held_spec(width, hidden),
            held_spec(width, hidden, 1),
            held_spec(1, small.shape[1]),
        ],
        out_specs=[
            row_spec(block, hidden),
            row_spec(block, width),
            pl.BlockSpec((3, 8, width), lambda step: (0, 0, 0)),
            pl.BlockSpec((8, hidden), lambda step: (0, 0)),
        ],
        out_shape=[
            jax.ShapeDtypeStruct((rows, hidden), BF16),
            jax.ShapeDtypeStruct((rows, width), F32),
            jax.ShapeDtypeStruct((3, 8, width), F32),
            jax.ShapeDtypeStruct((8, hidden), F32),
        ],
        compiler_params=params(),
        name="mlp_backward",
    )(grad_second, slope, normed_one, inverse_one, packed, packed, small)


def attention_backward_body(
    grad_first, joined, probs, w_out, joined_grad_out, sums_out, grad_mixed
):
    rows, width = grad_first.shape

    @pl.when(pl.program_id(0) == 0)
    def _():
        sums_out[...] = jnp.zeros_like(sums_out)

    grad_mixed[...] = dot_nn(grad_first[...].astype(BF16), w_out[...]).astype(BF16)
    for segment in range(rows // SEG_LEN):
        place = slice(segment * SEG_LEN, (segment + 1) * SEG_LEN)
        for pair in range(width // LANES):
            low, high = pair * LANES, (pair + 1) * LANES
            query = joined[place, low:high]
            keyed = joined[place, width + low : width + high]
            valued = joined[place, 2 * width + low : 2 * width + high]
            grad_halves = head_halves(grad_mixed[place, low:high])
            weights = probs[place, 2 * low : 2 * high]
            grad_probs = dot_nt(valued, grad_halves)
            grad_valued = dot_nn(weights.astype(BF16), grad_halves)
            inner = jnp.sum(weights * grad_probs, axis=0, keepdims=True)
            scores_low = (weights * (grad_probs - inner) * SCALE_QK).astype(BF16)
            grad_keyed = dot_nn(scores_low, head_halves(query))
            grad_query = dot_tn(stack_heads(scores_low), head_halves(keyed))
            joined_grad_out[place, low:high] = grad_query.astype(BF16)
            joined_grad_out[place, width + low : width + high] = grad_keyed.astype(BF16)
            joined_grad_out[place, 2 * width + low : 2 * width + high] = grad_valued.astype(BF16)
            sums_out[0, :, low:high] += fold_rows(grad_query)
            sums_out[1, :, low:high] += fold_rows(grad_valued)


def attention_backward(grad_first, joined, probs, packed, block=256):
    rows, width = grad_first.shape
    return pl.pallas_call(
        attention_backward_body,
        grid=(rows // block,),
        in_specs=[
            row_spec(block, width),
            row_spec(block, 3 * width),
            row_spec(block, 2 * width),
            held_spec(width, width, 3),
        ],
        out_specs=[
            row_spec(block, 3 * width),
            pl.BlockSpec((2, 8, width), lambda step: (0, 0, 0)),
        ],
        out_shape=[
            jax.ShapeDtypeStruct((rows, 3 * width), BF16),
            jax.ShapeDtypeStruct((2, 8, width), F32),
        ],
        scratch_shapes=[pltpu.VMEM((block, width), BF16)],
        compiler_params=params(),
        name="attention_backward",
    )(grad_first, joined, probs, packed)


def grad_tokens_body(joined_grad, grad_first, w_qkv, grad_out):
    grad_out[...] = (dot_nt(joined_grad[...], w_qkv[...]) + grad_first[...]).astype(BF16)


def grad_tokens(joined_grad, grad_first, packed, block=512):
    rows, width = grad_first.shape
    return pl.pallas_call(
        grad_tokens_body,
        grid=(rows // block,),
        in_specs=[
            row_spec(block, 3 * width),
            row_spec(block, width),
            held_spec(width, 3 * width),
        ],
        out_specs=row_spec(block, width),
        out_shape=jax.ShapeDtypeStruct((rows, width), BF16),
        compiler_params=params(),
        name="grad_tokens",
    )(joined_grad, grad_first, packed)


def weight_grad_body(core, left, right, keep_out, send_out, total):
    total[...] = dot_tn(left[...], right[...])
    groups, rows = keep_out.shape[0], keep_out.shape[1]
    for group in range(groups):
        mine = pl.multiple_of((2 * group + core[0]) * rows, rows)
        other = pl.multiple_of((2 * group + 1 - core[0]) * rows, rows)
        keep_out[group] = total[pl.ds(mine, rows), :]
        send_out[group] = total[pl.ds(other, rows), :].astype(BF16)


def weight_grad(core, left, right, groups, block=768):
    tokens, height = left.shape
    width = right.shape[1]
    rows = height // (2 * groups)
    out_spec = pl.BlockSpec((groups, rows, block), lambda step, *_: (0, 0, step))
    return pl.pallas_call(
        weight_grad_body,
        grid_spec=pltpu.PrefetchScalarGridSpec(
            num_scalar_prefetch=1,
            grid=(width // block,),
            in_specs=[
                pl.BlockSpec((tokens, height), lambda step, *_: (0, 0)),
                pl.BlockSpec((tokens, block), lambda step, *_: (0, step)),
            ],
            out_specs=[out_spec, out_spec],
            scratch_shapes=[pltpu.VMEM((height, block), F32)],
        ),
        out_shape=[
            jax.ShapeDtypeStruct((groups, rows, width), F32),
            jax.ShapeDtypeStruct((groups, rows, width), BF16),
        ],
        compiler_params=params(),
        name="weight_grad",
    )(core, left, right)


def scatter_sum(keep, send, swap, peers):
    groups, rows, width = keep.shape
    received = lax.ppermute(send, ALL, swap)
    both = (keep + received.astype(F32)).astype(BF16)
    pieces = lax.all_to_all(both.reshape(groups * rows, width), PEERS, 0, 0, tiled=True)
    return jnp.sum(pieces.reshape(peers, groups * rows // peers, width).astype(F32), axis=0)


def adam_update(weight, first_moment, second_moment, grad_clip, rate, decay):
    fresh_one = BETA_ONE * first_moment + (1.0 - BETA_ONE) * grad_clip
    fresh_two = BETA_TWO * second_moment + (1.0 - BETA_TWO) * grad_clip * grad_clip
    correct_one = 1.0 - BETA_ONE**STEP
    correct_two = 1.0 - BETA_TWO**STEP
    stepped = fresh_one / correct_one / (jnp.sqrt(fresh_two / correct_two) + ADAM_EPS)
    updated = weight - rate * (stepped + decay * weight)
    return (updated, fresh_one, fresh_two, updated.astype(BF16))


def body(
    high_count,
    inner_count,
    tokens,
    cotangent,
    seg_counts,
    w_qkv,
    w_out,
    w_up,
    w_down,
    small_params,
    first_qkv,
    second_qkv,
    first_out,
    second_out,
    first_up,
    second_up,
    first_down,
    second_down,
    first_small,
    second_small,
):
    device_count = 2 * high_count * inner_count
    peers = high_count * inner_count
    masters = (w_qkv, w_out, w_up, w_down, small_params)
    own_rows, width = w_out.shape
    hidden = w_up.shape[1]
    core = lax.axis_index("core").astype(jnp.int32).reshape(1)
    swap = [
        ((high * 2 + half) * inner_count + inner, (high * 2 + 1 - half) * inner_count + inner)
        for high in range(high_count)
        for half in range(2)
        for inner in range(inner_count)
    ]

    own_small = small_params.shape[0]
    small_wide = -(-own_small // LANES) * LANES
    small_block = jnp.pad(
        small_params.astype(BF16).reshape(1, own_small),
        ((0, own_rows - 1), (0, small_wide - own_small)),
    )
    front = jnp.concatenate([w_qkv.astype(BF16), w_out.astype(BF16), small_block], axis=1)
    back = jnp.concatenate([w_up.astype(BF16), w_down.astype(BF16)], axis=1)
    packed_front = lax.all_gather(front, ALL, axis=0, tiled=True)
    packed_back = lax.all_gather(back, ALL, axis=0, tiled=True)
    small = (
        packed_front.reshape(device_count, own_rows, front.shape[1])[
            :, 0, 4 * width : 4 * width + own_small
        ]
        .reshape(1, device_count * own_small)
        .astype(F32)
    )

    joined, probs, mixed, normed_one, inverse_one = attention_forward(
        tokens, seg_counts, packed_front, small
    )
    result, active, slope, grad_second, sums_two = mlp_forward(
        normed_one, seg_counts, cotangent, packed_back, small
    )
    second_low = grad_second.astype(BF16)
    sum_down = scatter_sum(*weight_grad(core, second_low, active, high_count), swap, peers)
    at = small_places(width, hidden)
    hidden_low = (normed_one * small[:, slice(*at["g1"])] + small[:, slice(*at["s1"])]).astype(BF16)
    grad_pre, grad_first, sums_one, sums_wide = mlp_backward(
        grad_second, slope, normed_one, inverse_one, packed_back, small
    )
    sum_up = scatter_sum(*weight_grad(core, hidden_low, grad_pre, high_count), swap, peers)
    first_low = grad_first.astype(BF16)
    sum_out = scatter_sum(*weight_grad(core, first_low, mixed, high_count), swap, peers)
    joined_grad, sums_qv = attention_backward(grad_first, joined, probs, packed_front)
    sum_qkv = scatter_sum(*weight_grad(core, tokens, joined_grad, high_count), swap, peers)
    grad_inputs = grad_tokens(joined_grad, grad_first, packed_front)

    grad_small = jnp.concatenate(
        [
            jnp.sum(sums_qv, axis=1).reshape(-1),
            jnp.sum(sums_one[2], axis=0),
            jnp.sum(sums_wide, axis=0),
            jnp.sum(sums_two[2], axis=0),
            jnp.sum(sums_one[:2], axis=1).reshape(-1),
            jnp.sum(sums_two[:2], axis=1).reshape(-1),
        ]
    )
    small_pieces = lax.all_to_all(
        grad_small.reshape(device_count, own_small), ALL, 0, 0, tiled=True
    )
    sum_small = jnp.sum(small_pieces, axis=0)

    summed = (sum_qkv, sum_out, sum_up, sum_down, sum_small)
    squares = jnp.float32(0.0)
    for piece in summed:
        squares = squares + jnp.sum(piece * piece)
    spread = jnp.broadcast_to(squares, (device_count, LANES))
    total = jnp.sum(lax.all_to_all(spread, ALL, 0, 0, tiled=True)[:, 0])
    grad_norm = jnp.sqrt(total)
    factor = CLIP_LIMIT / jnp.maximum(grad_norm, CLIP_LIMIT)
    firsts = (first_qkv, first_out, first_up, first_down, first_small)
    seconds = (second_qkv, second_out, second_up, second_down, second_small)
    results = []
    for place in range(5):
        rate = RATE_SMALL if place == 4 else RATE_MATRIX
        decay = 0.0 if place == 4 else DECAY
        results.extend(
            adam_update(
                masters[place], firsts[place], seconds[place], summed[place] * factor, rate, decay
            )
        )
    return (result, grad_inputs, grad_norm, *results)


def solution(mesh):
    outer, inner = mesh.devices.shape
    finer = Mesh(mesh.devices.reshape(outer // 2, 2, inner), ALL)
    rows, flat = P(ALL, None), P(ALL)
    return jax.shard_map(
        functools.partial(body, outer // 2, inner),
        mesh=finer,
        in_specs=(rows, rows, flat) + (rows,) * 4 + (flat,) + (rows,) * 8 + (flat,) * 2,
        out_specs=(rows, rows, P()) + (rows,) * 16 + (flat,) * 4,
        check_vma=False,
    )
```

time: 1040 us -> 531 us (0.51)
  matrix products: 330 us -> 0 us
  waiting for transfers between devices: 430 us -> 227 us
  Pallas kernels: 0 us -> 187 us
  blocking collectives: 122 us -> 0 us
  local copies, waits for them, and re-layouts: 79.1 us -> 15.6 us
  starting transfers between devices: 0.33 us -> 26.5 us
    reduce_scatter x4 -> x0, waiting for transfers between devices: 348 us -> none  [the longest x1 140 us: body(): lax.psum_scatter(summed[3], ('dp', 'fsdp'), scatter_dimension=0, tiled=True)]
    dot_general x36 -> x0, matrix products: 330 us -> none  [the longest x8 128 us: plain_dot(): return jnp.dot(left, right, preferred_element_type=jnp.float32)]
    pallas_call x0 -> x9, Pallas kernels: none -> 187 us  [the longest x4 49.9 us: weight_grad(): pl.pallas_call(weight_grad_body, grid_spec=pltpu.PrefetchScalarGridSpec(n...]
    all_to_all x0 -> x6, waiting for transfers between devices: none -> 96.7 us  [the longest x4 92 us: scatter_sum(): lax.all_to_all(both.reshape(groups * rows, width), PEERS, 0, 0, tiled=True)]
    unnamed x2 -> x0, blocking collectives: 82.4 us -> none
    psum x1 -> x0, blocking collectives: 39.8 us -> none  [body(): total = lax.psum(squares, ('dp', 'fsdp'))]
    all_gather x4 -> x2, waiting for transfers between devices: 81.2 us -> 120 us  [the longest x1 66.6 us: body(): packed_front = lax.all_gather(front, ALL, axis=0, tiled=True)]
    all_to_all x0 -> x6, starting transfers between devices: none -> 25.9 us  [the longest x4 17.9 us: scatter_sum(): lax.all_to_all(both.reshape(groups * rows, width), PEERS, 0, 0, tiled=True)]
  transfers between devices with their start and end apart: 8 -> 12, of which waited for: 6 -> 9; matrix products, arithmetic and copies ran while one was open for 24% -> 10% of each run, Pallas kernels for 0% -> 15%
where the time goes in v1:
time: 531 us; the launch traced here: 529 us
  waiting for transfers between devices  227 us (43%)
  Pallas kernels  187 us (35%)
  other arithmetic  53.5 us (10%)
  starting transfers between devices  26.5 us (5%)
  between operations  19.5 us (4%)
  local copies, waits for them, and re-layouts  15.6 us (3%)
    all_to_all x4, waiting for transfers between devices, scatter_sum(): lax.all_to_all(both.reshape(groups * rows, width), PEERS, 0, 0, tiled=True)  92 us
    all_gather x1, waiting for transfers between devices, body(): packed_front = lax.all_gather(front, ALL, axis=0, tiled=True)  66.6 us
    all_gather x1, waiting for transfers between devices, body(): packed_back = lax.all_gather(back, ALL, axis=0, tiled=True)  53.8 us
    pallas_call x4, Pallas kernels, weight_grad(): pl.pallas_call(weight_grad_body, grid_spec=pltpu.PrefetchScalarGridSpec(n...  49.9 us
    pallas_call x1, Pallas kernels, mlp_forward(): pl.pallas_call(mlp_forward_body, grid_spec=pltpu.PrefetchScalarGridSpec(n...  37.6 us
    pallas_call x1, Pallas kernels, mlp_backward(): pl.pallas_call(mlp_backward_body, grid=(rows // block,), in_specs=[row_sp...  30.8 us
    pallas_call x1, Pallas kernels, attention_forward(): pl.pallas_call(attention_forward_body, grid_spec=pltpu.PrefetchScalarGrid...  28.8 us
    pallas_call x1, Pallas kernels, attention_backward(): pl.pallas_call(attention_backward_body, grid=(rows // block,), in_specs=[...  27.4 us
  transfers between devices with their start and end apart: 12, of which 9 were waited for; matrix products, arithmetic and copies ran while one was open for 10% of the time, Pallas kernels for 15%

profile of v1, /device:TPU:0, one launch (start us, length us, event | category | flops | bytes accessed | tf_op | source)
XLA Modules:
  0.0 529.1 jit_solution(18285261776297644763)
XLA Ops:
  13.3 66.6 %all-gather.3.cloned.1.call-done.w_qkv.w_out = bf16[768,3456]{1,0:T(8,128)(2,1)} async-done(((bf16[24,3456]{1,0:T(8,128)(2,1)}), bf16[768,3456]{1,0:T(8,128)(2,1)}) %all-gather.3.cloned.1.call-update) | async-done | bytes 5308432 | tf_op jit(solution)/shard_map/all_gather | solution.py:496
  79.9 1.1 fusion.6
  81.6 28.8 %attention_forward.1 = (bf16[2048,2304]{1,0:T(8,128)(2,1)}, f32[2048,1536]{1,0:T(8,128)}, bf16[2048,768]{1,0:T(8,128)(2,1)}, f32[2048,768]{1,0:T(8,128)}, f32[2048,128]{1,0:T(8,128)}) custom-call(s32[16]{0:T(128)} %counts.3, bf16[2048,768]{1,0:T(8,128)(2,1)} %left.1, bf16[768,3456]{1,0:T(8,128)(2,1)} %all-gather.3.cloned.1.call-done.w_qkv.w_out, ...), custom_call_target="tpu_custom_call" | custom-call | tf_op jit(solution)/shard_map/attention_forward/pallas_call | solution.py:142
  110.4 53.8 %all-gather.5.cloned.1.call-done.w_up.w_down = bf16[768,6144]{1,0:T(8,128)(2,1)} async-done(((bf16[24,6144]{1,0:T(8,128)(2,1)}), bf16[768,6144]{1,0:T(8,128)(2,1)}) %all-gather.5.cloned.1.call-update) | async-done | bytes 9437200 | tf_op jit(solution)/shard_map/all_gather | solution.py:497
  164.3 37.6 %mlp_forward.1 = (bf16[2048,768]{1,0:T(8,128)(2,1)}, bf16[2048,3072]{1,0:T(8,128)(2,1)}, f32[2048,3072]{1,0:T(8,128)}, f32[2048,768]{1,0:T(8,128)}, f32[3,8,768]{2,1,0:T(8,128)}) custom-call(s32[16]{0:T(128)} %counts.3, f32[2048,768]{1,0:T(8,128)} %get-tuple-element.47.normed_one, bf16[2048,768]{1,0:T(8,128)(2,1)} %cotangent.1, ...), custom_call_target="tpu_custom_call" | custom-call | tf_op jit(solution)/shard_map/mlp_forward/pallas_call | solution.py:224
  201.9 30.8 %mlp_backward.1 = (bf16[2048,3072]{1,0:T(8,128)(2,1)}, f32[2048,768]{1,0:T(8,128)}, f32[3,8,768]{2,1,0:T(8,128)}, f32[8,3072]{1,0:T(8,128)}) custom-call(f32[2048,768]{1,0:T(8,128)} %get-tuple-element.49.grad_second, f32[2048,3072]{1,0:T(8,128)} %get-tuple-element.50.slope, f32[2048,768]{1,0:T(8,128)} %get-tuple-element.47.normed_one, ...), custom_call_target="tpu_custom_call" | custom-call | tf_op jit(solution)/shard_map/mlp_backward/pallas_call | solution.py:292
  232.7 27.4 %attention_backward.1 = (bf16[2048,2304]{1,0:T(8,128)(2,1)}, f32[2,8,768]{2,1,0:T(8,128)}) custom-call(f32[2048,768]{1,0:T(8,128)} %get-tuple-element.52.grad_first, bf16[2048,2304]{1,0:T(8,128)(2,1)} %get-tuple-element.53.joined, f32[2048,1536]{1,0:T(8,128)} %get-tuple-element.54.probs, bf16[768,3456]{1,0:T(8,128)(2,1)} %all-gather.3.cloned.1.call-done.w_qkv.w_out), custom_call_target="tpu_custom_call" | custom-call | tf_op jit(solution)/shard_map/attention_backward/pallas_call | solution.py:355
  260.1 12.6 %weight_grad.4 = (f32[2,192,2304]{2,1,0:T(8,128)}, bf16[2,192,2304]{2,1,0:T(8,128)(2,1)}) custom-call(s32[1]{0:T(128)} %bitcast.1.core, bf16[2048,768]{1,0:T(8,128)(2,1)} %left.1, bf16[2048,2304]{1,0:T(8,128)(2,1)} %get-tuple-element.55.joined_grad.right), custom_call_target="tpu_custom_call" | custom-call | tf_op jit(solution)/shard_map/weight_grad/pallas_call | solution.py:414
  272.9 4.7 convert_element_type.92.left
  277.7 6.8 %weight_grad.5 = (f32[2,192,768]{2,1,0:T(8,128)}, bf16[2,192,768]{2,1,0:T(8,128)(2,1)}) custom-call(s32[1]{0:T(128)} %bitcast.1.core, bf16[2048,768]{1,0:T(8,128)(2,1)} %convert_element_type.92.left, bf16[2048,768]{1,0:T(8,128)(2,1)} %get-tuple-element.58.right), custom_call_target="tpu_custom_call" | custom-call | tf_op jit(solution)/shard_map/weight_grad/pallas_call | solution.py:414
  284.8 1.5 constant_dynamic-update-slice_fusion.5
  287.5 1.3 constant_dynamic-update-slice_fusion.4
  289.7 1.3 reshape.112
  291.0 1.3 reshape.113
  292.3 1.3 constant_dynamic-update-slice_fusion.3
  294.4 1.3 constant_dynamic-update-slice_fusion.2
  295.7 1.3 constant_dynamic-update-slice_fusion.1
  297.0 1.3 constant_dynamic-update-slice_fusion
  298.3 1.5 all_to_all.44
  299.8 3.4 all-to-all-start.4
  303.2 2.3 add_convert_fusion.4
  305.5 4.7 all-to-all-done.4
  310.3 4.3 all-to-all-start.1
  315.3 3.1 add_convert_fusion.3
  318.4 13.1 %all-to-all-done.1 = bf16[16,24,768]{2,1,0:T(8,128)(2,1)} async-done(((bf16[16,24,768]{2,1,0:T(8,128)(2,1)}), bf16[16,24,768]{2,1,0:T(8,128)(2,1)}, u32[]{:S(2)}, u32[]{:S(2)}) %all-to-all-start.1) | async-done | bytes 589856 | tf_op jit(solution)/shard_map/all_to_all | solution.py:439
  331.5 3.7 all-to-all-start
  335.2 5.0 add_convert_fusion.left
  340.2 15.2 %weight_grad.6 = (f32[2,192,3072]{2,1,0:T(8,128)}, bf16[2,192,3072]{2,1,0:T(8,128)(2,1)}) custom-call(s32[1]{0:T(128)} %bitcast.1.core, bf16[2048,768]{1,0:T(8,128)(2,1)} %add_convert_fusion.left, bf16[2048,3072]{1,0:T(8,128)(2,1)} %get-tuple-element.61.right), custom_call_target="tpu_custom_call" | custom-call | tf_op jit(solution)/shard_map/weight_grad/pallas_call | solution.py:414
  355.5 4.7 collective-permute-done.2
  360.2 4.6 add_convert_fusion.2
  364.8 10.9 %all-to-all-done = bf16[16,24,2304]{2,1,0:T(8,128)(2,1)S(1)} async-done(((bf16[16,24,2304]{2,1,0:T(8,128)(2,1)}), bf16[16,24,2304]{2,1,0:T(8,128)(2,1)S(1)}, u32[]{:S(2)}, u32[]{:S(2)}) %all-to-all-start) | async-done | bytes 1769504 | tf_op jit(solution)/shard_map/all_to_all | solution.py:439
  375.6 1.2 copy-done
  376.9 4.2 all-to-all-start.2
  381.1 4.8 convert_element_type.100.left
  385.8 15.3 %weight_grad.7 = (f32[2,192,3072]{2,1,0:T(8,128)}, bf16[2,192,3072]{2,1,0:T(8,128)(2,1)}) custom-call(s32[1]{0:T(128)} %bitcast.1.core, bf16[2048,768]{1,0:T(8,128)(2,1)} %convert_element_type.100.left, bf16[2048,3072]{1,0:T(8,128)(2,1)} %get-tuple-element.64.right), custom_call_target="tpu_custom_call" | custom-call | tf_op jit(solution)/shard_map/weight_grad/pallas_call | solution.py:414
  401.1 4.7 collective-permute-done.3
  405.8 4.6 add_convert_fusion.1
  410.4 23.3 %all-to-all-done.2 = bf16[16,24,3072]{2,1,0:T(8,128)(2,1)S(1)} async-done(((bf16[16,24,3072]{2,1,0:T(8,128)(2,1)}), bf16[16,24,3072]{2,1,0:T(8,128)(2,1)S(1)}, u32[]{:S(2)}, u32[]{:S(2)}) %all-to-all-start.2) | async-done | bytes 2359328 | tf_op jit(solution)/shard_map/all_to_all | solution.py:439
  433.7 5.8 %all-to-all-start.3 = ((bf16[16,24,3072]{2,1,0:T(8,128)(2,1)}), bf16[16,24,3072]{2,1,0:T(8,128)(2,1)}, u32[]{:S(2)}, u32[]{:S(2)}) async-start(bf16[16,24,3072]{2,1,0:T(8,128)(2,1)} %bitcast.9), calls=%async_computation.3 | async-start | bytes 4718592 | tf_op jit(solution)/shard_map/all_to_all | solution.py:439
  440.9 1.2 convert_reduce_fusion.3
  442.7 1.7 convert_reduce_fusion.2
  447.5 44.7 %all-to-all-done.3 = bf16[16,24,3072]{2,1,0:T(8,128)(2,1)} async-done(((bf16[16,24,3072]{2,1,0:T(8,128)(2,1)}), bf16[16,24,3072]{2,1,0:T(8,128)(2,1)}, u32[]{:S(2)}, u32[]{:S(2)}) %all-to-all-start.3) | async-done | bytes 2359328 | tf_op jit(solution)/shard_map/all_to_all | solution.py:439
  492.2 2.1 convert_reduce_fusion
  497.5 4.7 all-to-all-start.5
  502.4 12.9 %grad_tokens.1 = bf16[2048,768]{1,0:T(8,128)(2,1)} custom-call(bf16[2048,2304]{1,0:T(8,128)(2,1)} %get-tuple-element.55.joined_grad.right, f32[2048,768]{1,0:T(8,128)} %get-tuple-element.52.grad_first, bf16[768,3456]{1,0:T(8,128)(2,1)} %all-gather.3.cloned.1.call-done.w_qkv.w_out), custom_call_target="tpu_custom_call" | custom-call | tf_op jit(solution)/shard_map/grad_tokens/pallas_call | solution.py:384
  516.6 1.3 fusion.8
  518.7 1.0 fusion.16
  519.7 1.5 fusion.10
  (74 shorter events, 17.4 us)
Async XLA Ops:
  7.2 72.7 %all-gather.3.cloned.1.call-start = ((), (), s32[]{:S(2)}) async-start(), calls=%async_computation.6 | async-start | bytes 5474304 | tf_op jit(solution)/shard_map/all_gather | solution.py:496
  10.5 153.8 %all-gather.5.cloned.1.call-start = ((), (), s32[]{:S(2)}) async-start(), calls=%async_computation.7 | async-start | bytes 9732096 | tf_op jit(solution)/shard_map/all_gather | solution.py:497
  272.7 42.6 %collective-permute-start = (bf16[2,192,2304]{2,1,0:T(8,128)(2,1)}, bf16[2,192,2304]{2,1,0:T(8,128)(2,1)}, u32[]{:S(2)}, u32[]{:S(2)}) collective-permute-start(bf16[2,192,2304]{2,1,0:T(8,128)(2,1)} %get-tuple-element.57), channel_id=1, source_target_pairs={{0,8},{1,9},{2,10},{3,11},{4,12},{5,13},{6,14},{7,15},{8,0},{9,1},... | collective-permute-start | bytes 5308424 | tf_op jit(solution)/shard_map/ppermute | solution.py:437
  272.9 4.7 copy-start.16
  277.7 8.5 %copy-start.15 = (f32[3,8,768]{2,1,0:T(8,128)S(1)}, f32[3,8,768]{2,1,0:T(8,128)}, u32[]{:S(2)}) copy-start(f32[3,8,768]{2,1,0:T(8,128)} %get-tuple-element.68) | copy-start | bytes 221188
  277.7 9.2 %copy-start.14 = (f32[3,8,768]{2,1,0:T(8,128)S(1)}, f32[3,8,768]{2,1,0:T(8,128)}, u32[]{:S(2)}) copy-start(f32[3,8,768]{2,1,0:T(8,128)} %get-tuple-element.70) | copy-start | bytes 221188
  284.5 30.8 %copy-start.1 = (f32[2,192,2304]{2,1,0:T(8,128)S(1)}, f32[2,192,2304]{2,1,0:T(8,128)}, u32[]{:S(2)}) copy-start(f32[2,192,2304]{2,1,0:T(8,128)} %get-tuple-element.56) | copy-start | bytes 10616836
  284.5 18.7 %collective-permute-start.1 = (bf16[2,192,768]{2,1,0:T(8,128)(2,1)}, bf16[2,192,768]{2,1,0:T(8,128)(2,1)}, u32[]{:S(2)}, u32[]{:S(2)}) collective-permute-start(bf16[2,192,768]{2,1,0:T(8,128)(2,1)} %get-tuple-element.60), channel_id=1, source_target_pairs={{0,8},{1,9},{2,10},{3,11},{4,12},{5,13},{6,14},{7,15},{8,0},{9,1},... | collective-permute-start | bytes 1769480 | tf_op jit(solution)/shard_map/ppermute | solution.py:437
  299.8 10.4 %all-to-all-start.4 = ((f32[32,1,288]{2,1,0:T(1,128)}), f32[32,1,288]{2,1,0:T(1,128)}, u32[]{:S(2)}, u32[]{:S(2)}) async-start(f32[32,1,288]{2,1,0:T(1,128)} %all_to_all.44), calls=%async_computation.4 | async-start | bytes 98304 | tf_op jit(solution)/shard_map/all_to_all | solution.py:536
  310.3 21.2 %all-to-all-start.1 = ((bf16[16,24,768]{2,1,0:T(8,128)(2,1)}), bf16[16,24,768]{2,1,0:T(8,128)(2,1)}, u32[]{:S(2)}, u32[]{:S(2)}) async-start(bf16[16,24,768]{2,1,0:T(8,128)(2,1)} %bitcast.10), calls=%async_computation.1 | async-start | bytes 1179648 | tf_op jit(solution)/shard_map/all_to_all | solution.py:439
  331.5 44.2 %all-to-all-start = ((bf16[16,24,2304]{2,1,0:T(8,128)(2,1)}), bf16[16,24,2304]{2,1,0:T(8,128)(2,1)S(1)}, u32[]{:S(2)}, u32[]{:S(2)}) async-start(bf16[16,24,2304]{2,1,0:T(8,128)(2,1)} %bitcast.2), calls=%async_computation | async-start | bytes 3538944 | tf_op jit(solution)/shard_map/all_to_all | solution.py:439
  355.4 4.7 collective-permute-start.2
  375.6 1.3 copy-start
  376.9 56.8 %all-to-all-start.2 = ((bf16[16,24,3072]{2,1,0:T(8,128)(2,1)}), bf16[16,24,3072]{2,1,0:T(8,128)(2,1)S(1)}, u32[]{:S(2)}, u32[]{:S(2)}) async-start(bf16[16,24,3072]{2,1,0:T(8,128)(2,1)} %bitcast.8), calls=%async_computation.2 | async-start | bytes 4718592 | tf_op jit(solution)/shard_map/all_to_all | solution.py:439
  401.1 4.7 collective-permute-start.3
  433.7 58.5 %all-to-all-start.3 = ((bf16[16,24,3072]{2,1,0:T(8,128)(2,1)}), bf16[16,24,3072]{2,1,0:T(8,128)(2,1)}, u32[]{:S(2)}, u32[]{:S(2)}) async-start(bf16[16,24,3072]{2,1,0:T(8,128)(2,1)} %bitcast.9), calls=%async_computation.3 | async-start | bytes 4718592 | tf_op jit(solution)/shard_map/all_to_all | solution.py:439
  440.3 4.8 copy-start.17
  497.5 17.7 %all-to-all-start.5 = ((f32[32,1,128]{2,1,0:T(1,128)}), f32[32,1,128]{2,1,0:T(1,128)S(1)}, u32[]{:S(2)}, u32[]{:S(2)}) async-start(f32[32,1,128]{2,1,0:T(1,128)} %broadcast_in_dim.3), calls=%async_computation.5 | async-start | bytes 32768 | tf_op jit(solution)/shard_map/all_to_all | solution.py:546
  502.2 15.7 %copy-start.9 = (f32[24,768]{1,0:T(8,128)S(1)}, f32[24,768]{1,0:T(8,128)}, u32[]{:S(2)}) copy-start(f32[24,768]{1,0:T(8,128)} %param.22) | copy-start | bytes 221188
  502.2 15.7 %copy-start.12 = (f32[24,768]{1,0:T(8,128)S(1)}, f32[24,768]{1,0:T(8,128)}, u32[]{:S(2)}) copy-start(f32[24,768]{1,0:T(8,128)} %param.28) | copy-start | bytes 221188
  502.2 15.7 %copy-start.13 = (f32[24,768]{1,0:T(8,128)S(1)}, f32[24,768]{1,0:T(8,128)}, u32[]{:S(2)}) copy-start(f32[24,768]{1,0:T(8,128)} %param.29) | copy-start | bytes 221188
  502.3 16.4 %copy-start.4 = (f32[24,2304]{1,0:T(8,128)S(1)}, f32[24,2304]{1,0:T(8,128)}, u32[]{:S(2)}) copy-start(f32[24,2304]{1,0:T(8,128)} %param.21) | copy-start | bytes 663556
  502.3 16.4 %copy-start.10 = (f32[24,2304]{1,0:T(8,128)S(1)}, f32[24,2304]{1,0:T(8,128)}, u32[]{:S(2)}) copy-start(f32[24,2304]{1,0:T(8,128)} %param.26) | copy-start | bytes 663556
  502.3 16.4 %copy-start.11 = (f32[24,2304]{1,0:T(8,128)S(1)}, f32[24,2304]{1,0:T(8,128)}, u32[]{:S(2)}) copy-start(f32[24,2304]{1,0:T(8,128)} %param.27) | copy-start | bytes 663556
  502.3 17.4 %copy-start.2 = (f32[24,3072]{1,0:T(8,128)S(1)}, f32[24,3072]{1,0:T(8,128)}, u32[]{:S(2)}) copy-start(f32[24,3072]{1,0:T(8,128)} %param.24) | copy-start | bytes 884740
  502.3 17.4 %copy-start.3 = (f32[24,3072]{1,0:T(8,128)S(1)}, f32[24,3072]{1,0:T(8,128)}, u32[]{:S(2)}) copy-start(f32[24,3072]{1,0:T(8,128)} %param.23) | copy-start | bytes 884740
  502.3 17.3 %copy-start.5 = (f32[24,3072]{1,0:T(8,128)S(1)}, f32[24,3072]{1,0:T(8,128)}, u32[]{:S(2)}) copy-start(f32[24,3072]{1,0:T(8,128)} %param.32) | copy-start | bytes 884740
  502.3 17.3 %copy-start.6 = (f32[24,3072]{1,0:T(8,128)S(1)}, f32[24,3072]{1,0:T(8,128)}, u32[]{:S(2)}) copy-start(f32[24,3072]{1,0:T(8,128)} %param.33) | copy-start | bytes 884740
  502.3 17.3 %copy-start.7 = (f32[24,3072]{1,0:T(8,128)S(1)}, f32[24,3072]{1,0:T(8,128)}, u32[]{:S(2)}) copy-start(f32[24,3072]{1,0:T(8,128)} %param.31) | copy-start | bytes 884740
  502.4 17.3 %copy-start.8 = (f32[24,3072]{1,0:T(8,128)S(1)}, f32[24,3072]{1,0:T(8,128)}, u32[]{:S(2)}) copy-start(f32[24,3072]{1,0:T(8,128)} %param.30) | copy-start | bytes 884740
Sparse Core Ops, SparseCore 0:
  11.5 68.3 all-gather.2
  83.3 80.8 all-gather.4

commit v2 on v1

v2 whole, which is shorter than its diff:
```python
import functools
import math

import jax
import jax.numpy as jnp
from jax import lax
from jax.experimental import pallas as pl
from jax.experimental.pallas import tpu as pltpu
from jax.sharding import Mesh
from jax.sharding import PartitionSpec as P

HEAD_DIM = 64
SEG_LEN = 128
STEP = 10
NEG_FILL = -1e30
SCALE_QK = 0.125
LN_EPS = 1e-05
BETA_ONE = 0.9
BETA_TWO = 0.999
ADAM_EPS = 1e-08
RATE_MATRIX = 0.03
RATE_SMALL = 0.3
DECAY = 0.01
CLIP_LIMIT = 1.0

LANES = 128
VMEM_LIMIT = 60 * 1024 * 1024
SMALL_VMEM = 28 * 1024 * 1024
F32 = jnp.float32
BF16 = jnp.bfloat16
ALL = ("hi", "core", "zed", "low")
PEERS = ("hi", "zed", "low")
PLANE = ("hi", "low")


def dot_nn(left, right):
    return jnp.dot(left, right, preferred_element_type=F32)


def dot_nt(left, right):
    return lax.dot_general(left, right, (((1,), (1,)), ((), ())), preferred_element_type=F32)


def dot_tn(left, right):
    return lax.dot_general(left, right, (((0,), (0,)), ((), ())), preferred_element_type=F32)


def small_places(width, hidden):
    front = 3 * width + hidden
    return {
        "bq": (0, width),
        "bv": (width, 2 * width),
        "bo": (2 * width, 3 * width),
        "b1": (3 * width, front),
        "b2": (front, front + width),
        "g1": (front + width, front + 2 * width),
        "s1": (front + 2 * width, front + 3 * width),
        "g2": (front + 3 * width, front + 4 * width),
        "s2": (front + 4 * width, front + 5 * width),
    }


def normalize(values):
    row_mean = jnp.mean(values, axis=-1, keepdims=True)
    centred = values - row_mean
    variance = jnp.mean(centred * centred, axis=-1, keepdims=True)
    inverse = lax.rsqrt(variance + LN_EPS)
    return centred * inverse, inverse


def norm_back(scaled, normed, inverse):
    return inverse * (
        scaled
        - jnp.mean(scaled, axis=-1, keepdims=True)
        - normed * jnp.mean(scaled * normed, axis=-1, keepdims=True)
    )


def fold_rows(values):
    return jnp.sum(values.reshape(values.shape[0] // 8, 8, values.shape[1]), axis=0)


def head_halves(pair):
    lane = lax.broadcasted_iota(jnp.int32, pair.shape, 1)
    zero = jnp.zeros_like(pair)
    return jnp.concatenate(
        [jnp.where(lane < HEAD_DIM, pair, zero), jnp.where(lane < HEAD_DIM, zero, pair)], axis=0
    )


def stack_heads(wide):
    return jnp.concatenate([wide[:, :SEG_LEN], wide[:, SEG_LEN:]], axis=0)


def row_spec(rows, columns):
    return pl.BlockSpec((rows, columns), lambda step, *_: (step, 0))


def held_spec(rows, columns, place=0):
    return pl.BlockSpec(
        (rows, columns), lambda step, *_: (0, place), pipeline_mode=pl.Buffered(1)
    )


def whole_spec(shape):
    return pl.BlockSpec(shape, lambda *_: (0,) * len(shape))


def call_kernel(
    body, name, grid, inputs, in_specs, outs, out_specs, scalars=(), scratch=(), after=(), aliases=None, flops=0,
    vmem=VMEM_LIMIT,
):
    lead, kept = len(scalars), len(scalars) + len(inputs)

    def wrapped(*refs):
        body(*refs[:kept], *refs[kept + len(after) :])

    listed = outs if isinstance(outs, list) else [outs]
    moved = sum(math.prod(x.shape) * x.dtype.itemsize for x in (*inputs, *listed))
    return pl.pallas_call(
        wrapped,
        grid_spec=pltpu.PrefetchScalarGridSpec(
            num_scalar_prefetch=lead,
            grid=grid,
            in_specs=[*in_specs, *[pl.BlockSpec(memory_space=pl.ANY)] * len(after)],
            out_specs=out_specs,
            scratch_shapes=list(scratch),
        ),
        out_shape=outs,
        input_output_aliases=aliases or {},
        cost_estimate=pl.CostEstimate(
            flops=int(flops), bytes_accessed=moved, transcendentals=0
        ),
        compiler_params=pltpu.CompilerParams(vmem_limit_bytes=vmem),
        name=name,
    )(*scalars, *inputs, *after)


def shaped(shape, kind):
    return jax.ShapeDtypeStruct(shape, kind)


def attention_forward_body(
    core, counts, inputs, mine_a, theirs_a, mine_b, theirs_b, small, joined_out, probs_out, mixed_out, w_qkv, sems
):
    rows, width = inputs.shape
    at = small_places(width, small.shape[1] - 8 * width)

    @pl.when(pl.program_id(0) == 0)
    def _():
        copies = []
        groups, span, half = mine_a.shape
        for column, (mine, theirs) in enumerate(((mine_a, theirs_a), (mine_b, theirs_b))):
            for group in range(groups):
                for flip, source in enumerate((mine, theirs)):
                    owner = 2 * group + (core[0] if flip == 0 else 1 - core[0])
                    target = w_qkv.at[
                        pl.ds(pl.multiple_of(owner * span, span), span),
                        column * half : (column + 1) * half,
                    ]
                    copies.append(
                        pltpu.make_async_copy(
                            source.at[group, :, :half], target, sems.at[len(copies)]
                        )
                    )
        for copy in copies:
            copy.start()
        for copy in copies:
            copy.wait()

    values = inputs[...]
    for part, bias in ((0, "bq"), (1, None), (2, "bv")):
        columns = slice(part * width, (part + 1) * width)
        product = dot_nn(values, w_qkv[:, columns])
        if bias is not None:
            product = product + small[:, slice(*at[bias])]
        joined_out[:, columns] = product.astype(BF16)
    for segment in range(rows // SEG_LEN):
        place = slice(segment * SEG_LEN, (segment + 1) * SEG_LEN)
        count = counts[pl.program_id(0) * (rows // SEG_LEN) + segment]
        visible = lax.broadcasted_iota(jnp.int32, (SEG_LEN, 2 * SEG_LEN), 0) < count
        for pair in range(width // LANES):
            low, high = pair * LANES, (pair + 1) * LANES
            query = joined_out[place, low:high] * jnp.asarray(SCALE_QK, BF16)
            keyed = joined_out[place, width + low : width + high]
            valued = joined_out[place, 2 * width + low : 2 * width + high]
            scores = jnp.where(visible, dot_nt(keyed, head_halves(query)), NEG_FILL)
            raised = jnp.exp(scores - jnp.max(scores, axis=0, keepdims=True))
            probs = raised * (1.0 / jnp.sum(raised, axis=0, keepdims=True))
            probs_out[place, 2 * low : 2 * high] = probs
            mixed = dot_tn(stack_heads(probs.astype(BF16)), head_halves(valued))
            mixed_out[place, low:high] = mixed.astype(BF16)


def attention_forward(core, counts, inputs, quarters, small, block=256):
    rows, width = inputs.shape
    hbm = pl.BlockSpec(memory_space=pl.ANY)
    return call_kernel(
        attention_forward_body,
        "attention_forward",
        (rows // block,),
        [inputs, *quarters, small],
        [row_spec(block, width), hbm, hbm, hbm, hbm, held_spec(1, small.shape[1])],
        [
            shaped((rows, 3 * width), BF16),
            shaped((rows, 2 * width), F32),
            shaped((rows, width), BF16),
            shaped((width, 3 * width), BF16),
        ],
        [
            row_spec(block, 3 * width),
            row_spec(block, 2 * width),
            row_spec(block, width),
            pl.BlockSpec((width, 3 * width), lambda *_: (0, 0), pipeline_mode=pl.Buffered(1)),
        ],
        scalars=[core, counts],
        scratch=[pltpu.SemaphoreType.DMA((4 * quarters[0].shape[0],))],
        flops=12 * rows * width * width,
    )


def mlp_forward_body(
    counts,
    inputs,
    mixed,
    cotangent,
    w_up,
    w_down,
    w_out,
    small,
    result_out,
    normed_out,
    inverse_out,
    hidden_out,
    active_out,
    slope_out,
    second_out,
    second_low_out,
    sums_out,
):
    rows, width = inputs.shape
    step = pl.program_id(0)
    at = small_places(width, small.shape[1] - 8 * width)
    attended = dot_nt(mixed[...], w_out[...]) + small[:, slice(*at["bo"])]
    normed_one, inverse_one = normalize(inputs[...].astype(F32) + attended)
    normed_out[...] = normed_one
    inverse_out[...] = jnp.broadcast_to(inverse_one, inverse_out.shape)
    hidden = normed_one * small[:, slice(*at["g1"])] + small[:, slice(*at["s1"])]
    hidden_low = hidden.astype(BF16)
    hidden_out[...] = hidden_low
    pre_act = dot_nn(hidden_low, w_up[...]) + small[:, slice(*at["b1"])]
    spread = 0.5 * (1.0 + lax.erf(pre_act * math.sqrt(0.5)))
    density = jnp.exp(-0.5 * pre_act * pre_act) * (1.0 / math.sqrt(2.0 * math.pi))
    active = (pre_act * spread).astype(BF16)
    active_out[...] = active
    slope_out[...] = spread + pre_act * density
    second = hidden + dot_nt(active, w_down[...]) + small[:, slice(*at["b2"])]
    normed, inverse = normalize(second)
    gain = small[:, slice(*at["g2"])]
    index = lax.broadcasted_iota(jnp.int32, (SEG_LEN, 1), 0)
    live = jnp.concatenate(
        [
            (index < counts[step * (rows // SEG_LEN) + segment]).astype(F32)
            for segment in range(rows // SEG_LEN)
        ],
        axis=0,
    )
    result_out[...] = ((normed * gain + small[:, slice(*at["s2"])]) * live).astype(BF16)
    incoming = cotangent[...].astype(F32) * live
    grad_second = norm_back(incoming * gain, normed, inverse)
    second_out[...] = grad_second
    second_low_out[...] = grad_second.astype(BF16)

    @pl.when(step == 0)
    def _():
        sums_out[...] = jnp.zeros_like(sums_out)

    sums_out[0] += fold_rows(incoming * normed)
    sums_out[1] += fold_rows(incoming)
    sums_out[2] += fold_rows(grad_second)


def mlp_forward(counts, inputs, mixed, cotangent, packed, small, block=256):
    rows, width = inputs.shape
    hidden = (packed.shape[1] - width) // 2
    return call_kernel(
        mlp_forward_body,
        "mlp_forward",
        (rows // block,),
        [inputs, mixed, cotangent, packed, packed, packed, small],
        [
            row_spec(block, width),
            row_spec(block, width),
            row_spec(block, width),
            held_spec(width, hidden),
            held_spec(width, hidden, 1),
            held_spec(width, width, 2 * hidden // width),
            held_spec(1, small.shape[1]),
        ],
        [
            shaped((rows, width), BF16),
            shaped((rows, width), F32),
            shaped((rows, LANES), F32),
            shaped((rows, width), BF16),
            shaped((rows, hidden), BF16),
            shaped((rows, hidden), F32),
            shaped((rows, width), F32),
            shaped((rows, width), BF16),
            shaped((3, 8, width), F32),
        ],
        [
            row_spec(block, width),
            row_spec(block, width),
            row_spec(block, LANES),
            row_spec(block, width),
            row_spec(block, hidden),
            row_spec(block, hidden),
            row_spec(block, width),
            row_spec(block, width),
            whole_spec((3, 8, width)),
        ],
        scalars=[counts],
        flops=2 * rows * width * (width + 2 * hidden),
    )


def mlp_backward_body(fresh, *refs):
    grad_second, slope, normed_one, inverse_one, w_up, w_down, small = refs[:7]
    pre_out, first_out, first_low_out, sums_out, wide_out = refs[-5:]
    rows, width = normed_one.shape
    hidden = slope.shape[1]
    chunk = width
    at = small_places(width, hidden)

    @pl.when(pl.program_id(0) == 0)
    def _():
        if fresh:
            sums_out[...] = jnp.zeros_like(sums_out)
            wide_out[...] = jnp.zeros_like(wide_out)
        else:
            sums_out[...] = refs[7][...]
            wide_out[...] = refs[8][...]

    incoming = grad_second[...]
    incoming_low = incoming.astype(BF16)
    grad_hidden = incoming
    for piece in range(hidden // chunk):
        columns = slice(piece * chunk, (piece + 1) * chunk)
        grad_pre = dot_nn(incoming_low, w_down[:, columns]) * slope[:, columns]
        wide_out[:, columns] += fold_rows(grad_pre)
        grad_low = grad_pre.astype(BF16)
        pre_out[:, columns] = grad_low
        grad_hidden = grad_hidden + dot_nt(grad_low, w_up[:, columns])
    normed = normed_one[...]
    sums_out[0] += fold_rows(grad_hidden * normed)
    sums_out[1] += fold_rows(grad_hidden)
    grad_first = norm_back(
        grad_hidden * small[:, slice(*at["g1"])], normed, inverse_one[:, :1]
    )
    first_out[...] = grad_first
    first_low_out[...] = grad_first.astype(BF16)
    sums_out[2] += fold_rows(grad_first)


def mlp_backward(
    grad_second, slope, normed_one, inverse_one, packed, small, span, earlier=None, after=(), block=256
):
    rows, width = normed_one.shape
    hidden = slope.shape[1]

    def placed(columns):
        return pl.BlockSpec((block, columns), lambda step, *_: (span[0] + step, 0))

    hbm = pl.BlockSpec(memory_space=pl.ANY)
    sums_spec, wide_spec = whole_spec((3, 8, width)), whole_spec((8, hidden))
    inputs = [grad_second, slope, normed_one, inverse_one, packed, packed, small]
    in_specs = [
        placed(width),
        placed(hidden),
        placed(width),
        placed(LANES),
        held_spec(width, hidden),
        held_spec(width, hidden, 1),
        held_spec(1, small.shape[1]),
    ]
    aliases = None
    if earlier is not None:
        inputs += [earlier[3], earlier[4], *earlier[:3]]
        in_specs += [sums_spec, wide_spec, hbm, hbm, hbm]
        aliases = {9: 0, 10: 1, 11: 2}
    return call_kernel(
        functools.partial(mlp_backward_body, earlier is None),
        "mlp_backward",
        (span[1] - span[0],),
        inputs,
        in_specs,
        [
            shaped((rows, hidden), BF16),
            shaped((rows, width), F32),
            shaped((rows, width), BF16),
            shaped((3, 8, width), F32),
            shaped((8, hidden), F32),
        ],
        [placed(hidden), placed(width), placed(width), sums_spec, wide_spec],
        after=after,
        aliases=aliases,
        flops=4 * (span[1] - span[0]) * block * width * hidden,
    )


def attention_backward_body(fresh, *refs):
    first_low, joined, probs, w_out = refs[:4]
    joined_grad_out, sums_out, grad_mixed = refs[-3:]
    rows, width = first_low.shape

    @pl.when(pl.program_id(0) == 0)
    def _():
        sums_out[...] = jnp.zeros_like(sums_out) if fresh else refs[4][...]

    grad_mixed[...] = dot_nn(first_low[...], w_out[...]).astype(BF16)
    for segment in range(rows // SEG_LEN):
        place = slice(segment * SEG_LEN, (segment + 1) * SEG_LEN)
        for pair in range(width // LANES):
            low, high = pair * LANES, (pair + 1) * LANES
            query = joined[place, low:high]
            keyed = joined[place, width + low : width + high]
            valued = joined[place, 2 * width + low : 2 * width + high]
            grad_halves = head_halves(grad_mixed[place, low:high])
            weights = probs[place, 2 * low : 2 * high]
            grad_probs = dot_nt(valued, grad_halves)
            grad_valued = dot_nn(weights.astype(BF16), grad_halves)
            inner = jnp.sum(weights * grad_probs, axis=0, keepdims=True)
            scores_low = (weights * (grad_probs - inner) * SCALE_QK).astype(BF16)
            grad_keyed = dot_nn(scores_low, head_halves(query))
            grad_query = dot_tn(stack_heads(scores_low), head_halves(keyed))
            joined_grad_out[place, low:high] = grad_query.astype(BF16)
            joined_grad_out[place, width + low : width + high] = grad_keyed.astype(BF16)
            joined_grad_out[place, 2 * width + low : 2 * width + high] = grad_valued.astype(BF16)
            sums_out[0, :, low:high] += fold_rows(grad_query)
            sums_out[1, :, low:high] += fold_rows(grad_valued)


def attention_backward(first_low, joined, probs, packed, span, earlier=None, after=(), block=256):
    rows, width = first_low.shape

    def placed(columns):
        return pl.BlockSpec((block, columns), lambda step, *_: (span[0] + step, 0))

    inputs = [first_low, joined, probs, packed]
    in_specs = [
        placed(width),
        placed(3 * width),
        placed(2 * width),
        held_spec(width, width, (packed.shape[1] - width) // width),
    ]
    aliases = None
    if earlier is not None:
        inputs += [earlier[1], earlier[0]]
        in_specs += [whole_spec((2, 8, width)), pl.BlockSpec(memory_space=pl.ANY)]
        aliases = {5: 0}
    return call_kernel(
        functools.partial(attention_backward_body, earlier is None),
        "attention_backward",
        (span[1] - span[0],),
        inputs,
        in_specs,
        [shaped((rows, 3 * width), BF16), shaped((2, 8, width), F32)],
        [placed(3 * width), whole_spec((2, 8, width))],
        scratch=[pltpu.VMEM((block, width), BF16)],
        after=after,
        aliases=aliases,
        flops=16 * (span[1] - span[0]) * block * width * width,
    )


def grad_tokens_body(joined_grad, grad_first, w_qkv, grad_out):
    grad_out[...] = (dot_nt(joined_grad[...], w_qkv[...]) + grad_first[...]).astype(BF16)


def grad_tokens(joined_grad, grad_first, w_qkv, after=(), block=512):
    rows, width = grad_first.shape
    return call_kernel(
        grad_tokens_body,
        "grad_tokens",
        (rows // block,),
        [joined_grad, grad_first, w_qkv],
        [row_spec(block, 3 * width), row_spec(block, width), held_spec(width, 3 * width)],
        shaped((rows, width), BF16),
        row_spec(block, width),
        after=after,
        flops=6 * rows * width * width,
    )


def weight_grad_body(has_extra, core, left, right, *refs):
    keep_out, send_out, total = refs[-3:]
    block = right.shape[1]
    total[...] = dot_tn(left[...], right[...])
    groups, rows = keep_out.shape[0], keep_out.shape[1]
    step = pl.program_id(0)
    columns = pl.ds(pl.multiple_of(step * block, block), block) if has_extra else slice(None)
    for group in range(groups):
        for flip, target in enumerate((keep_out, send_out)):
            half = core[0] if flip == 0 else 1 - core[0]
            start = pl.multiple_of((2 * group + half) * rows, rows)
            target[group, :, columns] = total[pl.ds(start, rows), :].astype(BF16)
    if has_extra:
        extra = refs[0]

        @pl.when(step == 0)
        def _():
            for group in range(groups):
                for flip, target in enumerate((keep_out, send_out)):
                    half = core[0] if flip == 0 else 1 - core[0]
                    target[group, :, target.shape[2] - LANES :] = extra[group, half].astype(BF16)


def weight_grad(core, left, right, groups, extra=None, after=(), block=768):
    tokens, height = left.shape
    width = right.shape[1]
    rows = height // (2 * groups)
    inputs = [left, right]
    in_specs = [
        whole_spec((tokens, height)),
        pl.BlockSpec((tokens, block), lambda step, *_: (0, step)),
    ]
    if extra is None:
        shape = (groups, rows, width)
        out_spec = pl.BlockSpec((groups, rows, block), lambda step, *_: (0, 0, step))
    else:
        inputs.append(extra)
        in_specs.append(whole_spec(extra.shape))
        shape = (groups, rows, width + LANES)
        out_spec = whole_spec(shape)
    return call_kernel(
        functools.partial(weight_grad_body, extra is not None),
        "weight_grad",
        (width // block,),
        inputs,
        in_specs,
        [shaped(shape, BF16)] * 2,
        [out_spec, out_spec],
        scalars=[core],
        scratch=[pltpu.VMEM((height, block), F32)],
        after=after,
        flops=2 * tokens * height * width,
    )


def add_body(*refs):
    both_out, column = refs[-1], 0
    for keep, received in zip(refs[:-1:2], refs[1:-1:2]):
        width = keep.shape[-1]
        both_out[..., column : column + width] = (
            keep[...].astype(F32) + received[...].astype(F32)
        ).astype(BF16)
        column += width


def add_pairs(pairs, after=()):
    groups, rows = pairs[0][0].shape[:2]
    arrays = [array for pair in pairs for array in pair]
    shape = (groups, rows, sum(pair[0].shape[-1] for pair in pairs))
    return call_kernel(
        add_body,
        "add_pairs",
        (1,),
        arrays,
        [whole_spec(array.shape) for array in arrays],
        shaped(shape, BF16),
        whole_spec(shape),
        after=after,
        vmem=SMALL_VMEM,
    )


def fold_body(pieces, total_out):
    total_out[...] = jnp.sum(pieces[...].astype(F32), axis=0)


def fold_pieces(pieces, after=()):
    count, rows, width = pieces.shape
    return call_kernel(
        fold_body,
        "fold_pieces",
        (1,),
        [pieces],
        [whole_spec(pieces.shape)],
        shaped((rows, width), F32),
        whole_spec((rows, width)),
        after=after,
        vmem=SMALL_VMEM,
    )


def squares_body(pieces, *refs):
    total_out, spread_out = refs[-2:]
    total = jnp.sum(pieces[...].astype(F32), axis=0)
    total_out[...] = total
    squares = jnp.sum(total * total)
    for other in refs[:-2]:
        squares = squares + jnp.sum(other[...] * other[...])
    spread_out[...] = jnp.zeros(spread_out.shape, F32) + squares


def fold_with_squares(pieces, others, copies, after=()):
    count, rows, width = pieces.shape
    inputs = [pieces, *others]
    outs = [shaped((rows, width), F32), shaped((copies, LANES), F32)]
    return call_kernel(
        squares_body,
        "fold_with_squares",
        (1,),
        inputs,
        [whole_spec(array.shape) for array in inputs],
        outs,
        [whole_spec(array.shape) for array in outs],
        after=after,
        vmem=SMALL_VMEM,
    )


def update_body(places, squares, *refs):
    count = len(places)
    norm_out, results = refs[-1], refs[-1 - 4 * count : -1]
    states = refs[-1 - 7 * count : -1 - 4 * count]
    totals = refs[: -1 - 7 * count]
    grad_norm = jnp.sqrt(jnp.sum(squares[:, :1], axis=0, keepdims=True))
    factor = CLIP_LIMIT / jnp.maximum(grad_norm, CLIP_LIMIT)
    norm_out[...] = jnp.broadcast_to(grad_norm, norm_out.shape)
    for index, (source, low, high) in enumerate(places):
        weight, first, second = (ref[...] for ref in states[3 * index : 3 * index + 3])
        fresh = adam_update(
            weight, first, second, totals[source][:, low:high] * factor, RATE_MATRIX, DECAY
        )
        for target, value in zip(results[4 * index : 4 * index + 4], fresh):
            target[...] = value


def update_weights(squares, totals, places, states):
    inputs = [squares, *totals, *states]
    outs = []
    for index in range(len(places)):
        shape = states[3 * index].shape
        outs += [shaped(shape, F32)] * 3 + [shaped(shape, BF16)]
    outs.append(shaped((1, LANES), F32))
    return call_kernel(
        functools.partial(update_body, places),
        "update_weights",
        (1,),
        inputs,
        [whole_spec(array.shape) for array in inputs],
        outs,
        [whole_spec(array.shape) for array in outs],
        vmem=SMALL_VMEM,
    )


def gather_axis(value, axis, size):
    pieces = [value] + [
        lax.ppermute(value, axis, [(place, place ^ step) for place in range(size)])
        for step in range(1, size)
    ]
    stacked = jnp.stack(pieces)
    place, bit = lax.axis_index(axis), 1
    while bit < size:
        paired = stacked.reshape(size // (2 * bit), 2, bit, *value.shape)
        stacked = jnp.where((place & bit) != 0, paired[:, ::-1], paired).reshape(stacked.shape)
        bit *= 2
    return stacked


def adam_update(weight, first_moment, second_moment, grad_clip, rate, decay):
    fresh_one = BETA_ONE * first_moment + (1.0 - BETA_ONE) * grad_clip
    fresh_two = BETA_TWO * second_moment + (1.0 - BETA_TWO) * grad_clip * grad_clip
    correct_one = 1.0 - BETA_ONE**STEP
    correct_two = 1.0 - BETA_TWO**STEP
    stepped = fresh_one / correct_one / (jnp.sqrt(fresh_two / correct_two) + ADAM_EPS)
    updated = weight - rate * (stepped + decay * weight)
    return (updated, fresh_one, fresh_two, updated.astype(BF16))


def body(
    high_count,
    zed_count,
    low_count,
    tokens,
    cotangent,
    seg_counts,
    w_qkv,
    w_out,
    w_up,
    w_down,
    small_params,
    first_qkv,
    second_qkv,
    first_out,
    second_out,
    first_up,
    second_up,
    first_down,
    second_down,
    first_small,
    second_small,
):
    inner_count = zed_count * low_count
    device_count = 2 * high_count * inner_count
    own_rows, width = w_out.shape
    hidden = w_up.shape[1]
    own_small = small_params.shape[0]
    core = lax.axis_index("core").astype(jnp.int32).reshape(1)
    swap = [(0, 1), (1, 0)]

    back = jnp.concatenate([w_up.astype(BF16), w_down.astype(BF16), w_out.astype(BF16)], axis=1)
    packed = lax.all_gather(back, ALL, axis=0, tiled=True)
    low_qkv = w_qkv.astype(BF16)
    per_row = own_small // own_rows
    small_block = jnp.pad(
        small_params.astype(BF16).reshape(own_rows, per_row), ((0, 0), (0, LANES - per_row))
    )
    along = gather_axis(jnp.concatenate([low_qkv, small_block], axis=1), "zed", zed_count)
    split = low_qkv.shape[1] // 2
    quarters = []
    for piece, order in ((along[..., :split], (0, 1)), (along[..., split:], (1, 0))):
        for stage in order:
            if stage == 0:
                piece = jnp.moveaxis(gather_axis(piece, "low", low_count), 0, -3)
            else:
                piece = gather_axis(piece, "hi", high_count)
        quarters.append(piece.reshape(high_count, inner_count * own_rows, piece.shape[-1]))
    quarters = [
        half
        for quarter in quarters
        for half in (quarter, lax.ppermute(quarter, "core", swap))
    ]
    mine, theirs = (half[..., split : split + per_row] for half in quarters[2:])
    small = (
        jnp.where(core[0] == 0, jnp.stack([mine, theirs], 1), jnp.stack([theirs, mine], 1))
        .reshape(1, device_count * own_small)
        .astype(F32)
    )

    joined, probs, mixed, whole_qkv = attention_forward(core, seg_counts, tokens, quarters, small)
    (
        result,
        normed_one,
        inverse_one,
        hidden_low,
        active,
        slope,
        grad_second,
        second_low,
        sums_two,
    ) = mlp_forward(seg_counts, tokens, mixed, cotangent, packed, small)


    def swap_cores(parts):
        keep, send = parts
        return keep, lax.ppermute(send, "core", swap)

    def peer_sum(both):
        columns = both.shape[-1]
        pieces = lax.all_to_all(both.reshape(-1, columns), PEERS, 0, 0, tiled=True)
        return pieces.reshape(high_count * inner_count, own_rows, columns)

    blocks = tokens.shape[0] // 256
    early_blocks, half_blocks = max(blocks // 4, 1), max(blocks // 2, 1)
    saved = (grad_second, slope, normed_one, inverse_one, packed, small)
    down = weight_grad(core, second_low, active, high_count)
    early = mlp_backward(*saved, (0, early_blocks), after=[down[0]])
    down = add_pairs([swap_cores(down)], after=[early[3]])
    grad_pre, grad_first, first_low, sums_one, sums_wide = mlp_backward(
        *saved, (early_blocks, blocks), earlier=early, after=[down]
    )
    down = peer_sum(down)
    up = weight_grad(core, hidden_low, grad_pre, high_count)
    out = weight_grad(core, first_low, mixed, high_count, after=[up[0]])
    upout = add_pairs([swap_cores(up), swap_cores(out)])
    saved = (first_low, joined, probs, packed)
    early = attention_backward(*saved, (0, half_blocks), after=[upout])
    sum_down = fold_pieces(down, after=[early[1]])
    upout = peer_sum(upout)
    joined_grad, sums_qv = attention_backward(
        *saved, (half_blocks, blocks), earlier=early, after=[sum_down]
    )
    grad_small = jnp.concatenate(
        [
            jnp.sum(sums_qv, axis=1).reshape(-1),
            jnp.sum(sums_one[2], axis=0),
            jnp.sum(sums_wide, axis=0),
            jnp.sum(sums_two[2], axis=0),
            jnp.sum(sums_one[:2], axis=1).reshape(-1),
            jnp.sum(sums_two[:2], axis=1).reshape(-1),
        ]
    )
    by_owner = jnp.pad(
        grad_small.reshape(high_count, 2, inner_count * own_rows, per_row),
        ((0, 0),) * 3 + ((0, LANES - per_row),),
    )
    qkv = weight_grad(core, tokens, joined_grad, high_count, extra=by_owner)
    qkv = add_pairs([swap_cores(qkv)])
    grad_inputs = grad_tokens(joined_grad, grad_first, whole_qkv, after=[qkv])
    sum_upout = fold_pieces(upout, after=[grad_inputs])
    sum_front, spread = fold_with_squares(peer_sum(qkv), [sum_upout, sum_down], device_count)
    squares = lax.all_to_all(spread, ALL, 0, 0, tiled=True)
    *updated, norm_row = update_weights(
        squares,
        [sum_front, sum_upout, sum_down],
        ((0, 0, 3 * width), (1, hidden, hidden + width), (1, 0, hidden), (2, 0, hidden)),
        [
            *(w_qkv, first_qkv, second_qkv),
            *(w_out, first_out, second_out),
            *(w_up, first_up, second_up),
            *(w_down, first_down, second_down),
        ],
    )
    grad_norm = norm_row[0, 0]
    factor = CLIP_LIMIT / jnp.maximum(grad_norm, CLIP_LIMIT)
    sum_small = sum_front[:, 3 * width : 3 * width + per_row].reshape(own_small)
    updated += adam_update(
        small_params, first_small, second_small, sum_small * factor, RATE_SMALL, 0.0
    )
    return (result, grad_inputs, grad_norm, *updated)


def solution(mesh):
    outer, inner = mesh.devices.shape
    finer = Mesh(mesh.devices.reshape(outer // 2, 2, inner // 2, 2), ALL)
    rows, flat = P(ALL, None), P(ALL)
    return jax.shard_map(
        functools.partial(body, outer // 2, inner // 2, 2),
        mesh=finer,
        in_specs=(rows, rows, flat) + (rows,) * 4 + (flat,) + (rows,) * 8 + (flat,) * 2,
        out_specs=(rows, rows, P()) + (rows,) * 16 + (flat,) * 4,
        check_vma=False,
    )
```

time: 531 us -> 407 us (0.77)
  waiting for transfers between devices: 227 us -> 97.4 us
  other arithmetic: 53.5 us -> 8.01 us
  Pallas kernels: 187 us -> 217 us
  local copies, waits for them, and re-layouts: 15.6 us -> 28.8 us
  blocking collectives: 0 us -> 10.4 us
    all_gather x2 -> x1, waiting for transfers between devices: 120 us -> 30.4 us  [body(): packed = lax.all_gather(back, ALL, axis=0, tiled=True)]
    all_to_all x6 -> x3, waiting for transfers between devices: 96.7 us -> 34.4 us  [peer_sum(): pieces = lax.all_to_all(both.reshape(-1, columns), PEERS, 0, 0, tiled=True)]
    convert_element_type x12 -> x5, other arithmetic: 33.7 us -> 3.72 us  [the longest x1 0.98 us: body(): w_down.astype(BF16)]
    pallas_call x9 -> x18, Pallas kernels: 187 us -> 217 us  [call_kernel(): pl.pallas_call(wrapped, grid_spec=pltpu.PrefetchScalarGridSpec(num_scalar...]
    ppermute x4 -> x13, waiting for transfers between devices: 9.49 us -> 32.7 us  [the longest x7 25.3 us: gather_axis(): lax.ppermute(value, axis, [(place, place ^ step) for place in range(size)])]
    unnamed x41 -> x77, local copies, waits for them, and re-layouts: 8.06 us -> 25.8 us
    ppermute x4 -> x13, starting transfers between devices: 0.51 us -> 11.9 us  [the longest x7 10.5 us: gather_axis(): lax.ppermute(value, axis, [(place, place ^ step) for place in range(size)])]
    all_to_all x0 -> x1, blocking collectives: none -> 10.4 us  [body(): squares = lax.all_to_all(spread, ALL, 0, 0, tiled=True)]
  transfers between devices with their start and end apart: 12 -> 17, of which waited for: 9 -> 12; matrix products, arithmetic and copies ran while one was open for 10% -> 2% of each run, Pallas kernels for 15% -> 36%
where the time goes in v2:
time: 407 us; the launch traced here: 406 us
  Pallas kernels  217 us (53%)
  waiting for transfers between devices  97.4 us (24%)
  starting transfers between devices  29.3 us (7%)
  local copies, waits for them, and re-layouts  28.8 us (7%)
  between operations  15.2 us (4%)
  blocking collectives  10.4 us (3%)
  other arithmetic  8.01 us (2%)
    pallas_call x18, Pallas kernels, call_kernel(): pl.pallas_call(wrapped, grid_spec=pltpu.PrefetchScalarGridSpec(num_scalar...  217 us
    all_to_all x3, waiting for transfers between devices, peer_sum(): pieces = lax.all_to_all(both.reshape(-1, columns), PEERS, 0, 0, tiled=True)  34.4 us
    all_gather x1, waiting for transfers between devices, body(): packed = lax.all_gather(back, ALL, axis=0, tiled=True)  30.4 us
    unnamed x77, local copies, waits for them, and re-layouts  25.8 us
    ppermute x7, waiting for transfers between devices, gather_axis(): lax.ppermute(value, axis, [(place, place ^ step) for place in range(size)])  25.3 us
    all_to_all x3, starting transfers between devices, peer_sum(): pieces = lax.all_to_all(both.reshape(-1, columns), PEERS, 0, 0, tiled=True)  17.3 us
    ppermute x7, starting transfers between devices, gather_axis(): lax.ppermute(value, axis, [(place, place ^ step) for place in range(size)])  10.5 us
    all_to_all x1, blocking collectives, body(): squares = lax.all_to_all(spread, ALL, 0, 0, tiled=True)  10.4 us
  transfers between devices with their start and end apart: 17, of which 12 were waited for; matrix products, arithmetic and copies ran while one was open for 2% of the time, Pallas kernels for 36%

profile of v2, /device:TPU:0, one launch (start us, length us, event | category | flops | bytes accessed | tf_op | source)
XLA Modules:
  0.0 405.9 jit_solution(2458978466347750200)
XLA Ops:
  8.1 1.0 convert_element_type.31
  9.1 1.0 convert_element_type.32
  12.6 4.1 %collective-permute-start.1 = (bf16[24,2432]{1,0:T(8,128)(2,1)S(1)}, bf16[24,2432]{1,0:T(8,128)(2,1)S(1)}, u32[]{:S(2)}, u32[]{:S(2)}) collective-permute-start(bf16[24,2432]{1,0:T(8,128)(2,1)S(1)} %get-tuple-element.142), channel_id=1, source_target_pairs={{0,4},{2,6},{4,0},{6,2},{1,5},{3,7},{5,1},{7,3},{8,12},{10,14},{12... | collective-permute-start | bytes 350216 | tf_op jit(solution)/shard_map/ppermute | solution.py:661
  16.7 1.6 collective-permute-start
  18.3 5.8 %collective-permute-done.1 = bf16[24,2432]{1,0:T(8,128)(2,1)S(1)} collective-permute-done((bf16[24,2432]{1,0:T(8,128)(2,1)S(1)}, bf16[24,2432]{1,0:T(8,128)(2,1)S(1)}, u32[]{:S(2)}, u32[]{:S(2)}) %collective-permute-start.1) | collective-permute-done | bytes 116768 | tf_op jit(solution)/shard_map/ppermute | solution.py:661
  24.1 2.3 collective-permute-done.2
  26.7 1.4 collective-permute-start.3
  28.1 1.6 collective-permute-start.6
  29.7 3.1 collective-permute-done.3
  32.9 1.6 collective-permute-start.4
  34.5 1.3 collective-permute-done.6
  36.3 8.4 %collective-permute-done.4 = bf16[4,2,24,1152]{3,2,0,1:T(8,128)(2,1)S(1)} collective-permute-done((bf16[4,2,24,1152]{3,2,0,1:T(8,128)(2,1)S(1)}, bf16[4,2,24,1152]{3,2,0,1:T(8,128)(2,1)S(1)}, u32[]{:S(2)}, u32[]{:S(2)}) %collective-permute-start.4) | collective-permute-done | bytes 442400 | tf_op jit(solution)/shard_map/ppermute | solution.py:661
  44.7 4.4 %collective-permute-done.7 = bf16[2,4,24,1280]{3,2,1,0:T(8,128)(2,1)S(1)} collective-permute-done((bf16[2,4,24,1280]{3,2,1,0:T(8,128)(2,1)S(1)}, bf16[2,4,24,1280]{3,2,1,0:T(8,128)(2,1)S(1)}, u32[]{:S(2)}, u32[]{:S(2)}) %collective-permute-start.7) | collective-permute-done | bytes 491552 | tf_op jit(solution)/shard_map/ppermute | solution.py:661
  50.5 1.6 collective-permute-done.8.refs_6_
  53.5 25.1 %attention_forward.1 = (bf16[2048,2304]{1,0:T(8,128)(2,1)}, f32[2048,1536]{1,0:T(8,128)}, bf16[2048,768]{1,0:T(8,128)(2,1)}, bf16[768,2304]{1,0:T(8,128)(2,1)}) custom-call(s32[1]{0:T(128)} %bitcast.refs_0_, s32[16]{0:T(128)} %refs_0_.1, bf16[2048,768]{1,0:T(8,128)(2,1)} %refs_1_.5, bf16[2,192,1152]{2,1,0:T(8,128)(2,1)} %bitcast.56, ...), custom_call_target="tpu_custom_call" | custom-call | flops 14495514624 | bytes 35622912 | tf_op jit(solution)/shard_map/attention_forward/pallas_call | solution.py:120
  78.6 30.4 %all-gather.2.cloned.1.call-done.refs_4_.refs_5_.refs_6_.refs_3_ = bf16[768,6912]{1,0:T(8,128)(2,1)} async-done(((bf16[24,6912]{1,0:T(8,128)(2,1)}), bf16[768,6912]{1,0:T(8,128)(2,1)}) %all-gather.2.cloned.1.call-update) | async-done | bytes 10616848 | tf_op jit(solution)/shard_map/all_gather | solution.py:715
  109.0 46.1 %mlp_forward.1 = (bf16[2048,768]{1,0:T(8,128)(2,1)}, f32[2048,768]{1,0:T(8,128)}, f32[2048,128]{1,0:T(8,128)}, bf16[2048,768]{1,0:T(8,128)(2,1)}, bf16[2048,3072...) custom-call(s32[16]{0:T(128)} %refs_0_.1, ...), custom_call_target="tpu_custom_call" | custom-call | flops 21743271936 | bytes 102215680 | tf_op jit(solution)/shard_map/mlp_forward/pallas_call | solution.py:120
  155.1 15.1 %weight_grad.4 = (bf16[2,192,3072]{2,1,0:T(8,128)(2,1)}, bf16[2,192,3072]{2,1,0:T(8,128)(2,1)}) custom-call(s32[1]{0:T(128)} %bitcast.refs_0_, bf16[2048,768]{1,0:T(8,128)(2,1)} %get-tuple-element.83.refs_1_, bf16[2048,3072]{1,0:T(8,128)(2,1)} %get-tuple-element.84.refs_2_), custom_call_target="tpu_custom_call" | custom-call | flops 9663676416 | bytes 20447232 | tf_op jit(solution)/shard_map/weight_grad/pallas_call | solution.py:120
  170.4 13.2 %mlp_backward.2 = (bf16[2048,3072]{1,0:T(8,128)(2,1)}, f32[2048,768]{1,0:T(8,128)}, bf16[2048,768]{1,0:T(8,128)(2,1)}, f32[3,8,768]{2,1,0:T(8,128)}, f32[8,3072]{1,0:T(8,128)}) custom-call(f32[2048,768]{1,0:T(8,128)} %get-tuple-element.79.refs_0_, f32[2048,3072]{1,0:T(8,128)} %get-tuple-element.80.refs_1_, f32[2048,768]{1,0:T(8,128)} %get-tuple-element.81.refs_2_, ...), custom_call_target="tpu_custom_call" | custom-call | flops 4831838208 | bytes 82259968 | tf_op jit(solution)/shard_map/mlp_backward/pallas_call | solution.py:120
  184.6 3.6 add_pairs.3.refs_12_
  188.1 4.1 %all-to-all-start = ((bf16[16,24,3072]{2,1,0:T(8,128)(2,1)}), bf16[16,24,3072]{2,1,0:T(8,128)(2,1)S(1)}, u32[]{:S(2)}, u32[]{:S(2)}) async-start(bf16[16,24,3072]{2,1,0:T(8,128)(2,1)} %bitcast.24), calls=%async_computation | async-start | bytes 4718592 | tf_op jit(solution)/shard_map/all_to_all | solution.py:763
  192.2 25.7 %mlp_backward.3 = (bf16[2048,3072]{1,0:T(8,128)(2,1)}, f32[2048,768]{1,0:T(8,128)}, bf16[2048,768]{1,0:T(8,128)(2,1)}, f32[3,8,768]{2,1,0:T(8,128)}, f32[8,3072]{1,0:T(8,128)}) custom-call(f32[2048,768]{1,0:T(8,128)} %get-tuple-element.79.refs_0_, ...), custom_call_target="tpu_custom_call", output_to_operand_aliasing={{0}: (9, {}), {1}: (10, {}), {2}: (11, {})} | custom-call | flops 14495514624 | bytes 104452096 | tf_op jit(solution)/shard_map/mlp_backward/pallas_call | solution.py:120
  217.9 15.0 %weight_grad.5 = (bf16[2,192,3072]{2,1,0:T(8,128)(2,1)}, bf16[2,192,3072]{2,1,0:T(8,128)(2,1)}) custom-call(s32[1]{0:T(128)} %bitcast.refs_0_, bf16[2048,768]{1,0:T(8,128)(2,1)} %get-tuple-element.95.refs_1_, bf16[2048,3072]{1,0:T(8,128)(2,1)} %get-tuple-element.96.refs_2_), custom_call_target="tpu_custom_call" | custom-call | flops 9663676416 | bytes 20447232 | tf_op jit(solution)/shard_map/weight_grad/pallas_call | solution.py:120
  233.0 6.6 %weight_grad.6 = (bf16[2,192,768]{2,1,0:T(8,128)(2,1)}, bf16[2,192,768]{2,1,0:T(8,128)(2,1)}) custom-call(s32[1]{0:T(128)} %bitcast.refs_0_, bf16[2048,768]{1,0:T(8,128)(2,1)} %get-tuple-element.92.refs_1_.refs_0_, bf16[2048,768]{1,0:T(8,128)(2,1)} %get-tuple-element.77.refs_2_, bf16[2,192,3072]{2,1,0:T(8,128)(2,1)} %get-tuple-element.97.refs_3_.refs_0_), custom_call_target="tpu_custom_call" | custom-call | flops 2415919104 | bytes 7471104 | tf_op jit(solution)/shard_map/weight_grad/pallas_call | solution.py:120
  240.0 1.8 collective-permute-done.11.refs_3_
  241.9 1.7 copy-done.10
  243.5 1.1 copy-done.15
  244.6 3.9 add_pairs.4.refs_4_
  248.5 1.4 copy-done.1
  249.9 6.9 %all-to-all-start.2 = ((bf16[16,24,3840]{2,1,0:T(8,128)(2,1)}), bf16[16,24,3840]{2,1,0:T(8,128)(2,1)S(1)}, u32[]{:S(2)}, u32[]{:S(2)}) async-start(bf16[16,24,3840]{2,1,0:T(8,128)(2,1)} %bitcast.26), calls=%async_computation.2 | async-start | bytes 5898240 | tf_op jit(solution)/shard_map/all_to_all | solution.py:763
  257.0 15.4 %attention_backward.2 = (bf16[2048,2304]{1,0:T(8,128)(2,1)}, f32[2,8,768]{2,1,0:T(8,128)}) custom-call(bf16[2048,768]{1,0:T(8,128)(2,1)} %get-tuple-element.92.refs_1_.refs_0_, bf16[2048,2304]{1,0:T(8,128)(2,1)} %get-tuple-element.93.refs_1_, f32[2048,1536]{1,0:T(8,128)} %get-tuple-element.94.refs_2_, ...), custom_call_target="tpu_custom_call" | custom-call | flops 9663676416 | bytes 45268992 | tf_op jit(solution)/shard_map/attention_backward/pallas_call | solution.py:120
  272.4 1.7 copy-done.2
  275.9 15.4 %attention_backward.3 = (bf16[2048,2304]{1,0:T(8,128)(2,1)}, f32[2,8,768]{2,1,0:T(8,128)}) custom-call(bf16[2048,768]{1,0:T(8,128)(2,1)} %get-tuple-element.92.refs_1_.refs_0_, bf16[2048,2304]{1,0:T(8,128)(2,1)} %get-tuple-element.93.refs_1_, f32[2048,1536]{1,0:T(8,128)} %get-tuple-element.94.refs_2_, ...), custom_call_target="tpu_custom_call", output_to_operand_aliasing={{0}: (5, {})} | custom-call | flops 9663676416 | bytes 54755328 | tf_op jit(solution)/shard_map/attention_backward/pallas_call | solution.py:120
  293.4 13.0 %weight_grad.7 = (bf16[2,192,2432]{2,1,0:T(8,128)(2,1)}, bf16[2,192,2432]{2,1,0:T(8,128)(2,1)}) custom-call(s32[1]{0:T(128)} %bitcast.refs_0_, bf16[2048,768]{1,0:T(8,128)(2,1)} %refs_1_.5, bf16[2048,2304]{1,0:T(8,128)(2,1)} %get-tuple-element.103.refs_2_.refs_0_, f32[2,2,192,128]{3,2,1,0:T(8,128)} %pad.9.refs_3_), custom_call_target="tpu_custom_call" | custom-call | flops 7247757312 | bytes 16711680 | tf_op jit(solution)/shard_map/weight_grad/pallas_call | solution.py:120
  306.5 4.0 collective-permute-done.12.refs_1_
  310.5 1.5 copy-done.11
  312.4 1.2 copy-done.3
  313.7 7.9 %all-to-all-done.2.refs_0_ = bf16[16,24,3840]{2,1,0:T(8,128)(2,1)S(1)} async-done(((bf16[16,24,3840]{2,1,0:T(8,128)(2,1)}), bf16[16,24,3840]{2,1,0:T(8,128)(2,1)S(1)}, u32[]{:S(2)}, u32[]{:S(2)}) %all-to-all-start.2) | async-done | bytes 2949152 | tf_op jit(solution)/shard_map/all_to_all | solution.py:763
  321.6 6.3 %all-to-all-start.1 = ((bf16[16,24,2432]{2,1,0:T(8,128)(2,1)}), bf16[16,24,2432]{2,1,0:T(8,128)(2,1)}, u32[]{:S(2)}, u32[]{:S(2)}) async-start(bf16[16,24,2432]{2,1,0:T(8,128)(2,1)} %bitcast.46), calls=%async_computation.1 | async-start | bytes 3735552 | tf_op jit(solution)/shard_map/all_to_all | solution.py:763
  327.9 13.4 %grad_tokens.1.refs_1_ = bf16[2048,768]{1,0:T(8,128)(2,1)} custom-call(bf16[2048,2304]{1,0:T(8,128)(2,1)} %get-tuple-element.103.refs_2_.refs_0_, f32[2048,768]{1,0:T(8,128)} %get-tuple-element.104.refs_1_, bf16[768,2304]{1,0:T(8,128)(2,1)} %get-tuple-element.105.refs_2_, bf16[2,192,2432]{2,1,0:T(8,128)(2,1)} %copy-done.3), custom_call_target="tpu_custom_call" | custom-call | flops 7247757312 | bytes 22413312 | tf_op jit(solution)/shard_map/grad_tokens/pallas_call | solution.py:120
  341.3 1.9 copy-done.9
  344.3 26.4 %all-to-all-done.1.refs_0_ = bf16[16,24,2432]{2,1,0:T(8,128)(2,1)} async-done(((bf16[16,24,2432]{2,1,0:T(8,128)(2,1)}), bf16[16,24,2432]{2,1,0:T(8,128)(2,1)}, u32[]{:S(2)}, u32[]{:S(2)}) %all-to-all-start.1) | async-done | bytes 1867808 | tf_op jit(solution)/shard_map/all_to_all | solution.py:763
  370.7 1.0 copy-done.7
  371.7 2.1 fold_with_squares.1
  373.9 10.4 %all_to_all.38 = f32[32,1,128]{2,1,0:T(1,128)S(1)} all-to-all(f32[32,1,128]{2,1,0:T(1,128)S(1)} %bitcast.48), channel_id=1, replica_groups=mesh['hi'=2,'core'=2,'zed'=4,'low'=2] {'hi','core','zed','low'}, dimensions={0} | all-to-all | bytes 32768 | tf_op jit(solution)/shard_map/all_to_all | solution.py:805
  384.3 1.0 copy-done.8
  387.1 1.0 copy-done.17
  395.5 2.2 update_weights.1
  (129 shorter events, 24.5 us)
Async XLA Ops:
  7.2 101.8 %all-gather.2.cloned.1.call-start = ((), (), s32[]{:S(2)}) async-start(), calls=%async_computation.4 | async-start | bytes 10948608 | tf_op jit(solution)/shard_map/all_gather | solution.py:715
  12.6 11.4 %collective-permute-start.1 = (bf16[24,2432]{1,0:T(8,128)(2,1)S(1)}, bf16[24,2432]{1,0:T(8,128)(2,1)S(1)}, u32[]{:S(2)}, u32[]{:S(2)}) collective-permute-start(bf16[24,2432]{1,0:T(8,128)(2,1)S(1)} %get-tuple-element.142), channel_id=1, source_target_pairs={{0,4},{2,6},{4,0},{6,2},{1,5},{3,7},{5,1},{7,3},{8,12},{10,14},{12... | collective-permute-start | bytes 350216 | tf_op jit(solution)/shard_map/ppermute | solution.py:661
  16.7 7.3 %collective-permute-start = (bf16[24,2432]{1,0:T(8,128)(2,1)S(1)}, bf16[24,2432]{1,0:T(8,128)(2,1)S(1)}, u32[]{:S(2)}, u32[]{:S(2)}) collective-permute-start(bf16[24,2432]{1,0:T(8,128)(2,1)S(1)} %get-tuple-element.142), channel_id=1, source_target_pairs={{0,2},{2,0},{4,6},{6,4},{1,3},{3,1},{5,7},{7,5},{8,10},{10,8},{12,... | collective-permute-start | bytes 350216 | tf_op jit(solution)/shard_map/ppermute | solution.py:661
  18.3 8.1 %collective-permute-start.2 = (bf16[24,2432]{1,0:T(8,128)(2,1)S(1)}, bf16[24,2432]{1,0:T(8,128)(2,1)S(1)}, u32[]{:S(2)}, u32[]{:S(2)}) collective-permute-start(bf16[24,2432]{1,0:T(8,128)(2,1)S(1)} %get-tuple-element.142), channel_id=1, source_target_pairs={{0,6},{2,4},{4,2},{6,0},{1,7},{3,5},{5,3},{7,1},{8,14},{10,12},{12... | collective-permute-start | bytes 350216 | tf_op jit(solution)/shard_map/ppermute | solution.py:661
  26.7 6.1 %collective-permute-start.3 = (bf16[4,24,1152]{2,1,0:T(8,128)(2,1)S(1)}, bf16[4,24,1152]{2,1,0:T(8,128)(2,1)S(1)}, u32[]{:S(2)}, u32[]{:S(2)}) collective-permute-start(bf16[4,24,1152]{2,1,0:T(8,128)(2,1)S(1)} %get-tuple-element.138), channel_id=1, source_target_pairs={{0,1},{1,0},{2,3},{3,2},{4,5},{5,4},{6,7},{7,6},{8,9},{9,8},{10,11... | collective-permute-start | bytes 663560 | tf_op jit(solution)/shard_map/ppermute | solution.py:661
  28.1 7.7 %collective-permute-start.6 = (bf16[4,24,1280]{2,1,0:T(8,128)(2,1)S(1)}, bf16[4,24,1280]{2,1,0:T(8,128)(2,1)S(1)}, u32[]{:S(2)}, u32[]{:S(2)}) collective-permute-start(bf16[4,24,1280]{2,1,0:T(8,128)(2,1)S(1)} %get-tuple-element.136), channel_id=1, source_target_pairs={{0,16},{16,0},{1,17},{17,1},{2,18},{18,2},{3,19},{19,3},{4,20},{20... | collective-permute-start | bytes 737288 | tf_op jit(solution)/shard_map/ppermute | solution.py:661
  32.9 11.7 %collective-permute-start.4 = (bf16[4,2,24,1152]{3,2,0,1:T(8,128)(2,1)S(1)}, bf16[4,2,24,1152]{3,2,0,1:T(8,128)(2,1)S(1)}, u32[]{:S(2)}, u32[]{:S(2)}) collective-permute-start(bf16[4,2,24,1152]{3,2,0,1:T(8,128)(2,1)S(1)} %get-tuple-element.140), channel_id=1, source_target_pairs={{0,16},{16,0},{1,17},{17,1},{2,18},{18,2},{3,19},{19,3},{4,20},{20... | collective-permute-start | bytes 1327112 | tf_op jit(solution)/shard_map/ppermute | solution.py:661
  35.9 13.3 %collective-permute-start.7 = (bf16[2,4,24,1280]{3,2,1,0:T(8,128)(2,1)S(1)}, bf16[2,4,24,1280]{3,2,1,0:T(8,128)(2,1)S(1)}, u32[]{:S(2)}, u32[]{:S(2)}) collective-permute-start(bf16[2,4,24,1280]{3,2,1,0:T(8,128)(2,1)S(1)} %reverse_select_fusion.2), channel_id=1, source_target_pairs={{0,1},{1,0},{2,3},{3,2},{4,5},{5,4},{6,7},{7,6},{8,9},{9,8},{10,11... | collective-permute-start | bytes 1474568 | tf_op jit(solution)/shard_map/ppermute | solution.py:661
  49.4 4.1 %copy-start.27 = (bf16[2,2,4,24,1280]{4,3,0,2,1:T(8,128)(2,1)}, bf16[2,2,4,24,1280]{4,3,0,2,1:T(8,128)(2,1)S(1)}, u32[]{:S(2)}) copy-start(bf16[2,2,4,24,1280]{4,3,0,2,1:T(8,128)(2,1)S(1)} %reverse_select_fusion) | copy-start | bytes 2949124
  49.5 2.6 collective-permute-start.8
  49.8 3.8 copy-start.28
  49.8 3.7 collective-permute-start.5
  52.1 1.4 copy-start.32
  170.2 13.5 %collective-permute-start.9 = (bf16[2,192,3072]{2,1,0:T(8,128)(2,1)}, bf16[2,192,3072]{2,1,0:T(8,128)(2,1)}, u32[]{:S(2)}, u32[]{:S(2)}) collective-permute-start(bf16[2,192,3072]{2,1,0:T(8,128)(2,1)} %get-tuple-element.91), channel_id=1, source_target_pairs={{0,8},{8,0},{1,9},{9,1},{2,10},{10,2},{3,11},{11,3},{4,12},{12,4},... | collective-permute-start | bytes 7077896 | tf_op jit(solution)/shard_map/ppermute | solution.py:759
  170.4 13.2 %copy-start = (bf16[2,192,3072]{2,1,0:T(8,128)(2,1)S(1)}, bf16[2,192,3072]{2,1,0:T(8,128)(2,1)}, u32[]{:S(2)}) copy-start(bf16[2,192,3072]{2,1,0:T(8,128)(2,1)} %get-tuple-element.85.refs_7_.refs_0_) | copy-start | bytes 7077892
  183.7 0.9 copy-start.16
  188.1 60.4 %all-to-all-start = ((bf16[16,24,3072]{2,1,0:T(8,128)(2,1)}), bf16[16,24,3072]{2,1,0:T(8,128)(2,1)S(1)}, u32[]{:S(2)}, u32[]{:S(2)}) async-start(bf16[16,24,3072]{2,1,0:T(8,128)(2,1)} %bitcast.24), calls=%async_computation | async-start | bytes 4718592 | tf_op jit(solution)/shard_map/all_to_all | solution.py:763
  232.9 8.9 %collective-permute-start.10 = (bf16[2,192,3072]{2,1,0:T(8,128)(2,1)}, bf16[2,192,3072]{2,1,0:T(8,128)(2,1)}, u32[]{:S(2)}, u32[]{:S(2)}) collective-permute-start(bf16[2,192,3072]{2,1,0:T(8,128)(2,1)} %get-tuple-element.98), channel_id=1, source_target_pairs={{0,8},{8,0},{1,9},{9,1},{2,10},{10,2},{3,11},{11,3},{4,12},{12,4},... | collective-permute-start | bytes 7077896 | tf_op jit(solution)/shard_map/ppermute | solution.py:759
  239.6 2.2 collective-permute-start.11
  241.9 1.7 copy-start.10
  243.5 1.1 copy-start.15
  248.5 8.3 %copy-start.30 = (f32[3,8,768]{2,1,0:T(8,128)S(1)}, f32[3,8,768]{2,1,0:T(8,128)}, u32[]{:S(2)}) copy-start(f32[3,8,768]{2,1,0:T(8,128)} %get-tuple-element.109) | copy-start | bytes 221188
  248.5 8.4 %copy-start.31 = (f32[3,8,768]{2,1,0:T(8,128)S(1)}, f32[3,8,768]{2,1,0:T(8,128)}, u32[]{:S(2)}) copy-start(f32[3,8,768]{2,1,0:T(8,128)} %get-tuple-element.107) | copy-start | bytes 221188
  248.5 8.4 %copy-start.29 = (f32[8,3072]{1,0:T(8,128)S(1)}, f32[8,3072]{1,0:T(8,128)}, u32[]{:S(2)}) copy-start(f32[8,3072]{1,0:T(8,128)} %get-tuple-element.108) | copy-start | bytes 294916
  248.5 1.4 copy-start.1
  249.9 71.7 %all-to-all-start.2 = ((bf16[16,24,3840]{2,1,0:T(8,128)(2,1)}), bf16[16,24,3840]{2,1,0:T(8,128)(2,1)S(1)}, u32[]{:S(2)}, u32[]{:S(2)}) async-start(bf16[16,24,3840]{2,1,0:T(8,128)(2,1)} %bitcast.26), calls=%async_computation.2 | async-start | bytes 5898240 | tf_op jit(solution)/shard_map/all_to_all | solution.py:763
  272.4 1.7 copy-start.2
  306.4 4.0 collective-permute-start.12
  310.5 1.5 copy-start.11
  312.4 1.2 copy-start.3
  321.6 49.2 %all-to-all-start.1 = ((bf16[16,24,2432]{2,1,0:T(8,128)(2,1)}), bf16[16,24,2432]{2,1,0:T(8,128)(2,1)}, u32[]{:S(2)}, u32[]{:S(2)}) async-start(bf16[16,24,2432]{2,1,0:T(8,128)(2,1)} %bitcast.46), calls=%async_computation.1 | async-start | bytes 3735552 | tf_op jit(solution)/shard_map/all_to_all | solution.py:763
  341.3 1.9 copy-start.9
  343.2 27.6 %copy-start.5 = (f32[24,3072]{1,0:T(8,128)S(1)}, f32[24,3072]{1,0:T(8,128)}, u32[]{:S(2)}) copy-start(f32[24,3072]{1,0:T(8,128)} %copy-done.4) | copy-start | bytes 884740
  343.2 41.1 %copy-start.12 = (f32[24,3072]{1,0:T(8,128)S(1)}, f32[24,3072]{1,0:T(8,128)}, u32[]{:S(2)}) copy-start(f32[24,3072]{1,0:T(8,128)} %refs_13_.1) | copy-start | bytes 884740
  370.7 1.0 copy-start.7
  371.7 26.7 %copy-start.33 = (f32[288]{0:T(512)S(1)}, f32[288]{0:T(512)}, u32[]{:S(2)}) copy-start(f32[288]{0:T(512)} %param.25) | copy-start | bytes 3460
  371.7 26.7 %copy-start.34 = (f32[288]{0:T(512)S(1)}, f32[288]{0:T(512)}, u32[]{:S(2)}) copy-start(f32[288]{0:T(512)} %param.34) | copy-start | bytes 3460
  371.7 26.8 %copy-start.35 = (f32[288]{0:T(512)S(1)}, f32[288]{0:T(512)}, u32[]{:S(2)}) copy-start(f32[288]{0:T(512)} %param.35) | copy-start | bytes 3460
  384.2 1.0 copy-start.8
  385.2 1.0 copy-start.13
  386.2 0.9 copy-start.14
  387.1 1.0 copy-start.17
  388.1 1.0 copy-start.18
  389.1 1.0 copy-start.19
  390.0 1.0 copy-start.20
  391.9 0.9 copy-start.22
  392.8 0.9 copy-start.23
  393.7 0.9 copy-start.25
  (5 other events, 4.0 us)
Sparse Core Ops, SparseCore 0:
  11.0 97.9 all-gather.1

commit v3 on v2

--- a/solution.py
+++ b/solution.py
@@ -25,7 +25,7 @@
 
 LANES = 128
 VMEM_LIMIT = 60 * 1024 * 1024
-SMALL_VMEM = 28 * 1024 * 1024
+SMALL_VMEM = 60 * 1024 * 1024
 F32 = jnp.float32
 BF16 = jnp.bfloat16
 ALL = ("hi", "core", "zed", "low")
@@ -141,7 +141,7 @@
 
 
 def attention_forward_body(
-    core, counts, inputs, mine_a, theirs_a, mine_b, theirs_b, small, joined_out, probs_out, mixed_out, w_qkv, sems
+    core, counts, inputs, mine_a, theirs_a, mine_b, theirs_b, small, joined_out, probs_out, mixed_out, normed_out, inverse_out, hidden_out, w_qkv, w_out, sems
 ):
     rows, width = inputs.shape
     at = small_places(width, small.shape[1] - 8 * width)
@@ -149,18 +149,23 @@
     @pl.when(pl.program_id(0) == 0)
     def _():
         copies = []
-        groups, span, half = mine_a.shape
-        for column, (mine, theirs) in enumerate(((mine_a, theirs_a), (mine_b, theirs_b))):
+        groups, span, cut = mine_a.shape
+        rest = 3 * width - cut
+        moves = (
+            (mine_a, theirs_a, w_qkv, 0, 0, cut),
+            (mine_b, theirs_b, w_qkv, 0, cut, rest),
+            (mine_b, theirs_b, w_out, rest + LANES, 0, width),
+        )
+        for mine, theirs, target, source, place, wide in moves:
             for group in range(groups):
-                for flip, source in enumerate((mine, theirs)):
+                for flip, half in enumerate((mine, theirs)):
                     owner = 2 * group + (core[0] if flip == 0 else 1 - core[0])
-                    target = w_qkv.at[
-                        pl.ds(pl.multiple_of(owner * span, span), span),
-                        column * half : (column + 1) * half,
+                    block = target.at[
+                        pl.ds(pl.multiple_of(owner * span, span), span), place : place + wide
                     ]
                     copies.append(
                         pltpu.make_async_copy(
-                            source.at[group, :, :half], target, sems.at[len(copies)]
+                            half.at[group, :, source : source + wide], block, sems.at[len(copies)]
                         )
                     )
         for copy in copies:
@@ -190,6 +195,12 @@
             probs_out[place, 2 * low : 2 * high] = probs
             mixed = dot_tn(stack_heads(probs.astype(BF16)), head_halves(valued))
             mixed_out[place, low:high] = mixed.astype(BF16)
+    attended = dot_nt(mixed_out[...], w_out[...]) + small[:, slice(*at["bo"])]
+    normed, inverse = normalize(values.astype(F32) + attended)
+    normed_out[...] = normed
+    inverse_out[...] = jnp.broadcast_to(inverse, inverse_out.shape)
+    hidden = normed * small[:, slice(*at["g1"])] + small[:, slice(*at["s1"])]
+    hidden_out[...] = hidden.astype(BF16)
 
 
 def attention_forward(core, counts, inputs, quarters, small, block=256):
@@ -205,49 +216,47 @@
             shaped((rows, 3 * width), BF16),
             shaped((rows, 2 * width), F32),
             shaped((rows, width), BF16),
+            shaped((rows, width), F32),
+            shaped((rows, LANES), F32),
+            shaped((rows, width), BF16),
             shaped((width, 3 * width), BF16),
+            shaped((width, width), BF16),
         ],
         [
             row_spec(block, 3 * width),
             row_spec(block, 2 * width),
             row_spec(block, width),
-            pl.BlockSpec((width, 3 * width), lambda *_: (0, 0), pipeline_mode=pl.Buffered(1)),
+            row_spec(block, width),
+            row_spec(block, LANES),
+            row_spec(block, width),
+            held_spec(width, 3 * width),
+            held_spec(width, width),
         ],
         scalars=[core, counts],
-        scratch=[pltpu.SemaphoreType.DMA((4 * quarters[0].shape[0],))],
+        scratch=[pltpu.SemaphoreType.DMA((6 * quarters[0].shape[0],))],
         flops=12 * rows * width * width,
     )
 
 
 def mlp_forward_body(
     counts,
-    inputs,
-    mixed,
+    normed_one,
     cotangent,
     w_up,
     w_down,
-    w_out,
     small,
     result_out,
-    normed_out,
-    inverse_out,
-    hidden_out,
     active_out,
     slope_out,
     second_out,
     second_low_out,
     sums_out,
 ):
-    rows, width = inputs.shape
+    rows, width = normed_one.shape
     step = pl.program_id(0)
     at = small_places(width, small.shape[1] - 8 * width)
-    attended = dot_nt(mixed[...], w_out[...]) + small[:, slice(*at["bo"])]
-    normed_one, inverse_one = normalize(inputs[...].astype(F32) + attended)
-    normed_out[...] = normed_one
-    inverse_out[...] = jnp.broadcast_to(inverse_one, inverse_out.shape)
-    hidden = normed_one * small[:, slice(*at["g1"])] + small[:, slice(*at["s1"])]
+    hidden = normed_one[...] * small[:, slice(*at["g1"])] + small[:, slice(*at["s1"])]
     hidden_low = hidden.astype(BF16)
-    hidden_out[...] = hidden_low
     pre_act = dot_nn(hidden_low, w_up[...]) + small[:, slice(*at["b1"])]
     spread = 0.5 * (1.0 + lax.erf(pre_act * math.sqrt(0.5)))
     density = jnp.exp(-0.5 * pre_act * pre_act) * (1.0 / math.sqrt(2.0 * math.pi))
@@ -280,27 +289,22 @@
     sums_out[2] += fold_rows(grad_second)
 
 
-def mlp_forward(counts, inputs, mixed, cotangent, packed, small, block=256):
-    rows, width = inputs.shape
-    hidden = (packed.shape[1] - width) // 2
+def mlp_forward(counts, normed_one, cotangent, packed, small, block=256):
+    rows, width = normed_one.shape
+    hidden = packed.shape[1] // 2
     return call_kernel(
         mlp_forward_body,
         "mlp_forward",
         (rows // block,),
-        [inputs, mixed, cotangent, packed, packed, packed, small],
-        [
-            row_spec(block, width),
+        [normed_one, cotangent, packed, packed, small],
+        [
             row_spec(block, width),
             row_spec(block, width),
             held_spec(width, hidden),
             held_spec(width, hidden, 1),
-            held_spec(width, width, 2 * hidden // width),
             held_spec(1, small.shape[1]),
         ],
         [
-            shaped((rows, width), BF16),
-            shaped((rows, width), F32),
-            shaped((rows, LANES), F32),
             shaped((rows, width), BF16),
             shaped((rows, hidden), BF16),
             shaped((rows, hidden), F32),
@@ -309,9 +313,6 @@
             shaped((3, 8, width), F32),
         ],
         [
-            row_spec(block, width),
-            row_spec(block, width),
-            row_spec(block, LANES),
             row_spec(block, width),
             row_spec(block, hidden),
             row_spec(block, hidden),
@@ -320,7 +321,7 @@
             whole_spec((3, 8, width)),
         ],
         scalars=[counts],
-        flops=2 * rows * width * (width + 2 * hidden),
+        flops=4 * rows * width * hidden,
     )
 
 
@@ -440,18 +441,18 @@
             sums_out[1, :, low:high] += fold_rows(grad_valued)
 
 
-def attention_backward(first_low, joined, probs, packed, span, earlier=None, after=(), block=256):
+def attention_backward(first_low, joined, probs, w_out, span, earlier=None, after=(), block=256):
     rows, width = first_low.shape
 
     def placed(columns):
         return pl.BlockSpec((block, columns), lambda step, *_: (span[0] + step, 0))
 
-    inputs = [first_low, joined, probs, packed]
+    inputs = [first_low, joined, probs, w_out]
     in_specs = [
         placed(width),
         placed(3 * width),
         placed(2 * width),
-        held_spec(width, width, (packed.shape[1] - width) // width),
+        held_spec(width, width),
     ]
     aliases = None
     if earlier is not None:
@@ -489,6 +490,26 @@
         row_spec(block, width),
         after=after,
         flops=6 * rows * width * width,
+    )
+
+
+def pack_body(*refs):
+    packed_out, column = refs[-1], 0
+    for ref in refs[:-1]:
+        packed_out[:, column : column + ref.shape[1]] = ref[...].astype(BF16)
+        column += ref.shape[1]
+
+
+def pack_rows(arrays):
+    shape = (arrays[0].shape[0], sum(array.shape[1] for array in arrays))
+    return call_kernel(
+        pack_body,
+        "pack_rows",
+        (1,),
+        arrays,
+        [whole_spec(array.shape) for array in arrays],
+        shaped(shape, BF16),
+        whole_spec(shape),
     )
 
 
@@ -711,15 +732,17 @@
     core = lax.axis_index("core").astype(jnp.int32).reshape(1)
     swap = [(0, 1), (1, 0)]
 
-    back = jnp.concatenate([w_up.astype(BF16), w_down.astype(BF16), w_out.astype(BF16)], axis=1)
+    back = pack_rows([w_up, w_down])
     packed = lax.all_gather(back, ALL, axis=0, tiled=True)
     low_qkv = w_qkv.astype(BF16)
     per_row = own_small // own_rows
     small_block = jnp.pad(
         small_params.astype(BF16).reshape(own_rows, per_row), ((0, 0), (0, LANES - per_row))
     )
-    along = gather_axis(jnp.concatenate([low_qkv, small_block], axis=1), "zed", zed_count)
-    split = low_qkv.shape[1] // 2
+    front = jnp.concatenate([low_qkv, small_block, w_out.astype(BF16)], axis=1)
+    along = gather_axis(front, "zed", zed_count)
+    split = 2 * width
+    at_small = low_qkv.shape[1] - split
     quarters = []
     for piece, order in ((along[..., :split], (0, 1)), (along[..., split:], (1, 0))):
         for stage in order:
@@ -733,26 +756,26 @@
         for quarter in quarters
         for half in (quarter, lax.ppermute(quarter, "core", swap))
     ]
-    mine, theirs = (half[..., split : split + per_row] for half in quarters[2:])
+    mine, theirs = (half[..., at_small : at_small + per_row] for half in quarters[2:])
     small = (
         jnp.where(core[0] == 0, jnp.stack([mine, theirs], 1), jnp.stack([theirs, mine], 1))
         .reshape(1, device_count * own_small)
         .astype(F32)
     )
 
-    joined, probs, mixed, whole_qkv = attention_forward(core, seg_counts, tokens, quarters, small)
     (
-        result,
+        joined,
+        probs,
+        mixed,
         normed_one,
         inverse_one,
         hidden_low,
-        active,
-        slope,
-        grad_second,
-        second_low,
-        sums_two,
-    ) = mlp_forward(seg_counts, tokens, mixed, cotangent, packed, small)
-
+        whole_qkv,
+        whole_out,
+    ) = attention_forward(core, seg_counts, tokens, quarters, small)
+    result, active, slope, grad_second, second_low, sums_two = mlp_forward(
+        seg_counts, normed_one, cotangent, packed, small
+    )
 
     def swap_cores(parts):
         keep, send = parts
@@ -764,25 +787,23 @@
         return pieces.reshape(high_count * inner_count, own_rows, columns)
 
     blocks = tokens.shape[0] // 256
-    early_blocks, half_blocks = max(blocks // 4, 1), max(blocks // 2, 1)
     saved = (grad_second, slope, normed_one, inverse_one, packed, small)
-    down = weight_grad(core, second_low, active, high_count)
-    early = mlp_backward(*saved, (0, early_blocks), after=[down[0]])
-    down = add_pairs([swap_cores(down)], after=[early[3]])
+    down = weight_grad(core, second_low, active, high_count, block=512)
+    down = add_pairs([swap_cores(down)])
     grad_pre, grad_first, first_low, sums_one, sums_wide = mlp_backward(
-        *saved, (early_blocks, blocks), earlier=early, after=[down]
+        *saved, (0, blocks), after=[down]
     )
     down = peer_sum(down)
-    up = weight_grad(core, hidden_low, grad_pre, high_count)
-    out = weight_grad(core, first_low, mixed, high_count, after=[up[0]])
-    upout = add_pairs([swap_cores(up), swap_cores(out)])
-    saved = (first_low, joined, probs, packed)
-    early = attention_backward(*saved, (0, half_blocks), after=[upout])
-    sum_down = fold_pieces(down, after=[early[1]])
-    upout = peer_sum(upout)
+    up = weight_grad(core, hidden_low, grad_pre, high_count, block=512)
+    out = weight_grad(core, first_low, mixed, high_count, after=[up[0]], block=256)
+    up = add_pairs([swap_cores(up)], after=[out[0]])
+    sum_down = fold_pieces(down, after=[up])
+    out = swap_cores(out)
     joined_grad, sums_qv = attention_backward(
-        *saved, (half_blocks, blocks), earlier=early, after=[sum_down]
-    )
+        first_low, joined, probs, whole_out, (0, blocks), after=[sum_down]
+    )
+    up = peer_sum(up)
+
     grad_small = jnp.concatenate(
         [
             jnp.sum(sums_qv, axis=1).reshape(-1),
@@ -798,15 +819,26 @@
         ((0, 0),) * 3 + ((0, LANES - per_row),),
     )
     qkv = weight_grad(core, tokens, joined_grad, high_count, extra=by_owner)
-    qkv = add_pairs([swap_cores(qkv)])
-    grad_inputs = grad_tokens(joined_grad, grad_first, whole_qkv, after=[qkv])
-    sum_upout = fold_pieces(upout, after=[grad_inputs])
-    sum_front, spread = fold_with_squares(peer_sum(qkv), [sum_upout, sum_down], device_count)
+    front = jnp.concatenate(
+        [
+            (keep.astype(F32) + received.astype(F32)).astype(BF16)
+            for keep, received in (swap_cores(qkv), out)
+        ],
+        axis=-1,
+    )
+    grad_inputs = grad_tokens(joined_grad, grad_first, whole_qkv, after=[front])
+    sum_up = fold_pieces(up, after=[grad_inputs])
+    sum_front, spread = fold_with_squares(peer_sum(front), [sum_up, sum_down], device_count)
     squares = lax.all_to_all(spread, ALL, 0, 0, tiled=True)
     *updated, norm_row = update_weights(
         squares,
-        [sum_front, sum_upout, sum_down],
-        ((0, 0, 3 * width), (1, hidden, hidden + width), (1, 0, hidden), (2, 0, hidden)),
+        [sum_front, sum_up, sum_down],
+        (
+            (0, 0, 3 * width),
+            (0, 3 * width + LANES, 4 * width + LANES),
+            (1, 0, hidden),
+            (2, 0, hidden),
+        ),
         [
             *(w_qkv, first_qkv, second_qkv),
             *(w_out, first_out, second_out),

time: 407 us -> 386 us (0.948)
  local copies, waits for them, and re-layouts: 28.8 us -> 8.35 us
    unnamed x77 -> x31, local copies, waits for them, and re-layouts: 25.8 us -> 4.42 us
    all_gather x1, waiting for transfers between devices: 30.4 us -> 11.2 us  [body(): packed = lax.all_gather(back, ALL, axis=0, tiled=True)]
    ppermute x7, waiting for transfers between devices: 25.3 us -> 34 us  [gather_axis(): lax.ppermute(value, axis, [(place, place ^ step) for place in range(size)])]
    all_to_all x3, waiting for transfers between devices: 34.4 us -> 38.7 us  [peer_sum(): pieces = lax.all_to_all(both.reshape(-1, columns), PEERS, 0, 0, tiled=True)]
    pallas_call x18 -> x16, Pallas kernels: 217 us -> 214 us  [call_kernel(): pl.pallas_call(wrapped, grid_spec=pltpu.PrefetchScalarGridSpec(num_scalar...]
  transfers between devices with their start and end apart: 17 -> 17, of which waited for: 12 -> 10; matrix products, arithmetic and copies ran while one was open for 2% -> 3% of each run, Pallas kernels for 36% -> 38%
where the time goes in v3:
time: 386 us; the launch traced here: 385 us
  Pallas kernels  214 us (55%)
  waiting for transfers between devices  94.5 us (24%)
  starting transfers between devices  30.6 us (8%)
  between operations  15.1 us (4%)
  blocking collectives  12 us (3%)
  other arithmetic  10.1 us (3%)
  local copies, waits for them, and re-layouts  8.35 us (2%)
    pallas_call x16, Pallas kernels, call_kernel(): pl.pallas_call(wrapped, grid_spec=pltpu.PrefetchScalarGridSpec(num_scalar...  214 us
    all_to_all x3, waiting for transfers between devices, peer_sum(): pieces = lax.all_to_all(both.reshape(-1, columns), PEERS, 0, 0, tiled=True)  38.7 us
    ppermute x7, waiting for transfers between devices, gather_axis(): lax.ppermute(value, axis, [(place, place ^ step) for place in range(size)])  34 us
    all_to_all x3, starting transfers between devices, peer_sum(): pieces = lax.all_to_all(both.reshape(-1, columns), PEERS, 0, 0, tiled=True)  18.5 us
    all_to_all x1, blocking collectives, body(): squares = lax.all_to_all(spread, ALL, 0, 0, tiled=True)  12 us
    all_gather x1, waiting for transfers between devices, body(): packed = lax.all_gather(back, ALL, axis=0, tiled=True)  11.2 us
    ppermute x7, starting transfers between devices, gather_axis(): lax.ppermute(value, axis, [(place, place ^ step) for place in range(size)])  10.7 us
    ppermute x4, waiting for transfers between devices, swap_cores(): return (keep, lax.ppermute(send, 'core', swap))  8.66 us
  transfers between devices with their start and end apart: 17, of which 10 were waited for; matrix products, arithmetic and copies ran while one was open for 3% of the time, Pallas kernels for 38%

profile of v3, /device:TPU:0, one launch (start us, length us, event | category | flops | bytes accessed | tf_op | source)
XLA Modules:
  0.0 384.9 jit_solution(4880082602975824053)
XLA Ops:
  7.2 1.8 pack_rows.1
  9.1 0.7 convert_element_type.40
  9.8 0.9 convert_element_type.41
  10.7 0.9 convert_element_type.39
  11.7 4.1 %collective-permute-start.1 = (bf16[24,3200]{1,0:T(8,128)(2,1)S(1)}, bf16[24,3200]{1,0:T(8,128)(2,1)S(1)}, u32[]{:S(2)}, u32[]{:S(2)}) collective-permute-start(bf16[24,3200]{1,0:T(8,128)(2,1)S(1)} %fusion.6), channel_id=1, source_target_pairs={{0,4},{2,6},{4,0},{6,2},{1,5},{3,7},{5,1},{7,3},{8,12},{10,14},{12... | collective-permute-start | bytes 460808 | tf_op jit(solution)/shard_map/ppermute | solution.py:682
  15.8 1.6 collective-permute-start
  17.4 7.3 %collective-permute-done.1 = bf16[24,3200]{1,0:T(8,128)(2,1)S(1)} collective-permute-done((bf16[24,3200]{1,0:T(8,128)(2,1)S(1)}, bf16[24,3200]{1,0:T(8,128)(2,1)S(1)}, u32[]{:S(2)}, u32[]{:S(2)}) %collective-permute-start.1) | collective-permute-done | bytes 153632 | tf_op jit(solution)/shard_map/ppermute | solution.py:682
  24.7 3.0 collective-permute-done.2
  28.2 1.6 collective-permute-start.3
  29.8 1.6 collective-permute-start.6
  31.4 4.5 %collective-permute-done.3 = bf16[4,24,1536]{2,1,0:T(8,128)(2,1)S(1)} collective-permute-done((bf16[4,24,1536]{2,1,0:T(8,128)(2,1)S(1)}, bf16[4,24,1536]{2,1,0:T(8,128)(2,1)S(1)}, u32[]{:S(2)}, u32[]{:S(2)}) %collective-permute-start.3) | collective-permute-done | bytes 294944 | tf_op jit(solution)/shard_map/ppermute | solution.py:682
  36.1 1.6 collective-permute-start.4
  37.6 1.3 collective-permute-done.6
  39.5 17.7 %collective-permute-done.4 = bf16[4,2,24,1536]{3,2,0,1:T(8,128)(2,1)S(1)} collective-permute-done((bf16[4,2,24,1536]{3,2,0,1:T(8,128)(2,1)S(1)}, bf16[4,2,24,1536]{3,2,0,1:T(8,128)(2,1)S(1)}, u32[]{:S(2)}, u32[]{:S(2)}) %collective-permute-start.4) | collective-permute-done | bytes 589856 | tf_op jit(solution)/shard_map/ppermute | solution.py:682
  59.0 2.0 collective-permute-done.8.refs_6_
  61.0 0.9 slice_bitcast_fusion
  62.3 0.9 reshape.154.refs_7_.refs_5_.refs_6_
  63.3 31.9 %attention_forward.1 = (bf16[2048,2304]{1,0:T(8,128)(2,1)}, f32[2048,1536]{1,0:T(8,128)}, bf16[2048,768]{1,0:T(8,128)(2,1)}, f32[2048,768]{1,0:T(8,128)}, f32[20...) custom-call(s32[1]{0:T(128)} %bitcast.refs_0_, s32[16]{0:T(128)} %refs_0_.3, ...), custom_call_target="tpu_custom_call" | custom-call | flops 14495514624 | bytes 48467968 | tf_op jit(solution)/shard_map/attention_forward/pallas_call | solution.py:120
  95.2 11.2 %all-gather.2.cloned.1.call-done.refs_3_.refs_4_.refs_5_ = bf16[768,6144]{1,0:T(8,128)(2,1)} async-done(((bf16[24,6144]{1,0:T(8,128)(2,1)}), bf16[768,6144]{1,0:T(8,128)(2,1)}) %all-gather.2.cloned.1.call-update) | async-done | bytes 9437200 | tf_op jit(solution)/shard_map/all_gather | solution.py:736
  106.4 38.0 %mlp_forward.1 = (bf16[2048,768]{1,0:T(8,128)(2,1)}, bf16[2048,3072]{1,0:T(8,128)(2,1)}, f32[2048,3072]{1,0:T(8,128)}, f32[2048,768]{1,0:T(8,128)}, bf16[2048,768]{1,0:T(8,128)(2,1)}, /*index=5*/f32[3,8,768]{2,1,0:T(8,128)}) custom-call(s32[16]{0:T(128)} %refs_0_.3, f32[2048,768]{1,0:T(8,128)} %get-tuple-element.71.refs_1_.refs_2_, ...), custom_call_target="tpu_custom_call" | custom-call | flops 19327352832 | bytes 78753792 | tf_op jit(solution)/shard_map/mlp_forward/pallas_call | solution.py:120
  144.4 14.9 %weight_grad.4 = (bf16[2,192,3072]{2,1,0:T(8,128)(2,1)}, bf16[2,192,3072]{2,1,0:T(8,128)(2,1)}) custom-call(s32[1]{0:T(128)} %bitcast.refs_0_, bf16[2048,768]{1,0:T(8,128)(2,1)} %get-tuple-element.76.refs_1_, bf16[2048,3072]{1,0:T(8,128)(2,1)} %get-tuple-element.77.refs_2_), custom_call_target="tpu_custom_call" | custom-call | flops 9663676416 | bytes 20447232 | tf_op jit(solution)/shard_map/weight_grad/pallas_call | solution.py:120
  159.6 4.5 %collective-permute-done.9.refs_1_ = bf16[2,192,3072]{2,1,0:T(8,128)(2,1)S(1)} collective-permute-done((bf16[2,192,3072]{2,1,0:T(8,128)(2,1)}, bf16[2,192,3072]{2,1,0:T(8,128)(2,1)S(1)}, u32[]{:S(2)}, u32[]{:S(2)}) %collective-permute-start.9) | collective-permute-done | bytes 2359328 | tf_op jit(solution)/shard_map/ppermute | solution.py:782
  164.1 1.4 copy-done.2
  165.6 4.3 %add_pairs.2.refs_7_ = bf16[2,192,3072]{2,1,0:T(8,128)(2,1)} custom-call(bf16[2,192,3072]{2,1,0:T(8,128)(2,1)} %get-tuple-element.78.refs_0_, bf16[2,192,3072]{2,1,0:T(8,128)(2,1)} %copy-done.2), custom_call_target="tpu_custom_call" | custom-call | bytes 7077888 | tf_op jit(solution)/shard_map/add_pairs/pallas_call | solution.py:120
  169.8 4.6 %all-to-all-start = ((bf16[16,24,3072]{2,1,0:T(8,128)(2,1)}), bf16[16,24,3072]{2,1,0:T(8,128)(2,1)S(1)}, u32[]{:S(2)}, u32[]{:S(2)}) async-start(bf16[16,24,3072]{2,1,0:T(8,128)(2,1)} %bitcast.47), calls=%async_computation | async-start | bytes 4718592 | tf_op jit(solution)/shard_map/all_to_all | solution.py:786
  174.5 31.0 %mlp_backward.1 = (bf16[2048,3072]{1,0:T(8,128)(2,1)}, f32[2048,768]{1,0:T(8,128)}, bf16[2048,768]{1,0:T(8,128)(2,1)}, f32[3,8,768]{2,1,0:T(8,128)}, f32[8,3072]{1,0:T(8,128)}) custom-call(f32[2048,768]{1,0:T(8,128)} %get-tuple-element.73.refs_0_, f32[2048,3072]{1,0:T(8,128)} %get-tuple-element.74.refs_1_, f32[2048,768]{1,0:T(8,128)} %get-tuple-element.71.refs_1_.refs_2_, ...), custom_call_target="tpu_custom_call" | custom-call | flops 19327352832 | bytes 79900672 | tf_op jit(solution)/shard_map/mlp_backward/pallas_call | solution.py:120
  205.6 15.0 %weight_grad.5 = (bf16[2,192,3072]{2,1,0:T(8,128)(2,1)}, bf16[2,192,3072]{2,1,0:T(8,128)(2,1)}) custom-call(s32[1]{0:T(128)} %bitcast.refs_0_, bf16[2048,768]{1,0:T(8,128)(2,1)} %get-tuple-element.84.refs_1_, bf16[2048,3072]{1,0:T(8,128)(2,1)} %get-tuple-element.85.refs_2_), custom_call_target="tpu_custom_call" | custom-call | flops 9663676416 | bytes 20447232 | tf_op jit(solution)/shard_map/weight_grad/pallas_call | solution.py:120
  220.7 6.5 %weight_grad.6 = (bf16[2,192,768]{2,1,0:T(8,128)(2,1)}, bf16[2,192,768]{2,1,0:T(8,128)(2,1)}) custom-call(s32[1]{0:T(128)} %bitcast.refs_0_, bf16[2048,768]{1,0:T(8,128)(2,1)} %get-tuple-element.80.refs_1_.refs_0_, bf16[2048,768]{1,0:T(8,128)(2,1)} %get-tuple-element.88.refs_2_, bf16[2,192,3072]{2,1,0:T(8,128)(2,1)} %get-tuple-element.86.refs_3_.refs_0_), custom_call_target="tpu_custom_call" | custom-call | flops 2415919104 | bytes 7471104 | tf_op jit(solution)/shard_map/weight_grad/pallas_call | solution.py:120
  227.3 4.3 %add_pairs.3.refs_1_ = bf16[2,192,3072]{2,1,0:T(8,128)(2,1)} custom-call(bf16[2,192,3072]{2,1,0:T(8,128)(2,1)} %get-tuple-element.86.refs_3_.refs_0_, bf16[2,192,3072]{2,1,0:T(8,128)(2,1)} %collective-permute-done.10.refs_1_, bf16[2,192,768]{2,1,0:T(8,128)(2,1)} %get-tuple-element.89.refs_2_), custom_call_target="tpu_custom_call" | custom-call | bytes 7077888 | tf_op jit(solution)/shard_map/add_pairs/pallas_call | solution.py:120
  231.6 1.4 copy-done.1
  233.0 7.0 %all-to-all-start.2 = ((bf16[16,24,3072]{2,1,0:T(8,128)(2,1)}), bf16[16,24,3072]{2,1,0:T(8,128)(2,1)}, u32[]{:S(2)}, u32[]{:S(2)}) async-start(bf16[16,24,3072]{2,1,0:T(8,128)(2,1)} %bitcast.46), calls=%async_computation.2 | async-start | bytes 4718592 | tf_op jit(solution)/shard_map/all_to_all | solution.py:786
  240.0 2.7 fold_pieces.2.refs_4_.refs_2_.refs_3_
  242.7 27.2 %attention_backward.1 = (bf16[2048,2304]{1,0:T(8,128)(2,1)}, f32[2,8,768]{2,1,0:T(8,128)}) custom-call(bf16[2048,768]{1,0:T(8,128)(2,1)} %get-tuple-element.80.refs_1_.refs_0_, bf16[2048,2304]{1,0:T(8,128)(2,1)} %get-tuple-element.81.refs_1_, f32[2048,1536]{1,0:T(8,128)} %get-tuple-element.82.refs_2_, bf16[768,768]{1,0:T(8,128)(2,1)} %get-tuple-element.83.refs_3_, ...), custom_call_target="tpu_custom_call" | custom-call | flops 19327352832 | bytes 35831808 | tf_op jit(solution)/shard_map/attention_backward/pallas_call | solution.py:120
  269.8 0.8 reduce_sum.54
  271.2 0.8 pad.9.refs_3_
  272.0 13.2 %weight_grad.7 = (bf16[2,192,2432]{2,1,0:T(8,128)(2,1)}, bf16[2,192,2432]{2,1,0:T(8,128)(2,1)}) custom-call(s32[1]{0:T(128)} %bitcast.refs_0_, bf16[2048,768]{1,0:T(8,128)(2,1)} %refs_1_.5, bf16[2048,2304]{1,0:T(8,128)(2,1)} %get-tuple-element.90.refs_2_.refs_0_, f32[2,2,192,128]{3,2,1,0:T(8,128)} %pad.9.refs_3_), custom_call_target="tpu_custom_call" | custom-call | flops 7247757312 | bytes 16711680 | tf_op jit(solution)/shard_map/weight_grad/pallas_call | solution.py:120
  285.6 4.2 %collective-permute-done.12 = bf16[2,192,768]{2,1,0:T(8,128)(2,1)S(1)} collective-permute-done((bf16[2,192,768]{2,1,0:T(8,128)(2,1)S(1)}, bf16[2,192,768]{2,1,0:T(8,128)(2,1)S(1)}, u32[]{:S(2)}, u32[]{:S(2)}) %collective-permute-start.12) | collective-permute-done | bytes 589856 | tf_op jit(solution)/shard_map/ppermute | solution.py:782
  290.0 2.0 add_convert_fusion
  291.9 1.6 pad_maximum_fusion.refs_3_
  293.5 6.9 %all-to-all-start.1 = ((bf16[16,24,3200]{2,1,0:T(8,128)(2,1)}), bf16[16,24,3200]{2,1,0:T(8,128)(2,1)S(1)}, u32[]{:S(2)}, u32[]{:S(2)}) async-start(bf16[16,24,3200]{2,1,0:T(8,128)(2,1)} %bitcast.25), calls=%async_computation.1 | async-start | bytes 4915200 | tf_op jit(solution)/shard_map/all_to_all | solution.py:786
  300.4 13.4 %grad_tokens.1.refs_1_ = bf16[2048,768]{1,0:T(8,128)(2,1)} custom-call(bf16[2048,2304]{1,0:T(8,128)(2,1)} %get-tuple-element.90.refs_2_.refs_0_, f32[2048,768]{1,0:T(8,128)} %get-tuple-element.91.refs_1_, bf16[768,2304]{1,0:T(8,128)(2,1)} %get-tuple-element.92.refs_2_, bf16[2,192,3200]{2,1,0:T(8,128)(2,1)} %pad_maximum_fusion.refs_3_), custom_call_target="tpu_custom_call" | custom-call | flops 7247757312 | bytes 22413312 | tf_op jit(solution)/shard_map/grad_tokens/pallas_call | solution.py:120
  313.8 2.7 fold_pieces.3.refs_1_.refs_2_
  316.5 38.7 %all-to-all-done.1.refs_0_ = bf16[16,24,3200]{2,1,0:T(8,128)(2,1)S(1)} async-done(((bf16[16,24,3200]{2,1,0:T(8,128)(2,1)}), bf16[16,24,3200]{2,1,0:T(8,128)(2,1)S(1)}, u32[]{:S(2)}, u32[]{:S(2)}) %all-to-all-start.1) | async-done | bytes 2457632 | tf_op jit(solution)/shard_map/all_to_all | solution.py:786
  355.2 1.4 copy-done
  356.6 3.1 fold_with_squares.1
  359.7 12.0 %all_to_all.38 = f32[32,1,128]{2,1,0:T(1,128)} all-to-all(f32[32,1,128]{2,1,0:T(1,128)} %bitcast.64), channel_id=1, replica_groups=mesh['hi'=2,'core'=2,'zed'=4,'low'=2] {'hi','core','zed','low'}, dimensions={0} | all-to-all | bytes 32768 | tf_op jit(solution)/shard_map/all_to_all | solution.py:832
  371.7 4.2 %update_weights.1 = (f32[24,2304]{1,0:T(8,128)}, f32[24,2304]{1,0:T(8,128)}, f32[24,2304]{1,0:T(8,128)}, bf16[24,2304]{1,0:T(8,128)(2,1)}, f32[24,768]{1,0:T(8,1...) custom-call(f32[32,128]{1,0:T(8,128)} %bitcast.63, ...), custom_call_target="tpu_custom_call" | custom-call | bytes 6664704 | tf_op jit(solution)/shard_map/update_weights/pallas_call | solution.py:120
  376.6 0.7 slice_multiply_fusion
  (82 shorter events, 5.7 us)
Async XLA Ops:
  7.2 99.2 %all-gather.2.cloned.1.call-start = ((), (), s32[]{:S(2)}) async-start(), calls=%async_computation.4 | async-start | bytes 9732096 | tf_op jit(solution)/shard_map/all_gather | solution.py:736
  11.7 13.0 %collective-permute-start.1 = (bf16[24,3200]{1,0:T(8,128)(2,1)S(1)}, bf16[24,3200]{1,0:T(8,128)(2,1)S(1)}, u32[]{:S(2)}, u32[]{:S(2)}) collective-permute-start(bf16[24,3200]{1,0:T(8,128)(2,1)S(1)} %fusion.6), channel_id=1, source_target_pairs={{0,4},{2,6},{4,0},{6,2},{1,5},{3,7},{5,1},{7,3},{8,12},{10,14},{12... | collective-permute-start | bytes 460808 | tf_op jit(solution)/shard_map/ppermute | solution.py:682
  15.8 8.9 %collective-permute-start = (bf16[24,3200]{1,0:T(8,128)(2,1)S(1)}, bf16[24,3200]{1,0:T(8,128)(2,1)S(1)}, u32[]{:S(2)}, u32[]{:S(2)}) collective-permute-start(bf16[24,3200]{1,0:T(8,128)(2,1)S(1)} %fusion.6), channel_id=1, source_target_pairs={{0,2},{2,0},{4,6},{6,4},{1,3},{3,1},{5,7},{7,5},{8,10},{10,8},{12,... | collective-permute-start | bytes 460808 | tf_op jit(solution)/shard_map/ppermute | solution.py:682
  17.4 10.4 %collective-permute-start.2 = (bf16[24,3200]{1,0:T(8,128)(2,1)S(1)}, bf16[24,3200]{1,0:T(8,128)(2,1)S(1)}, u32[]{:S(2)}, u32[]{:S(2)}) collective-permute-start(bf16[24,3200]{1,0:T(8,128)(2,1)S(1)} %fusion.6), channel_id=1, source_target_pairs={{0,6},{2,4},{4,2},{6,0},{1,7},{3,5},{5,3},{7,1},{8,14},{10,12},{12... | collective-permute-start | bytes 460808 | tf_op jit(solution)/shard_map/ppermute | solution.py:682
  28.2 7.7 %collective-permute-start.3 = (bf16[4,24,1536]{2,1,0:T(8,128)(2,1)S(1)}, bf16[4,24,1536]{2,1,0:T(8,128)(2,1)S(1)}, u32[]{:S(2)}, u32[]{:S(2)}) collective-permute-start(bf16[4,24,1536]{2,1,0:T(8,128)(2,1)S(1)} %get-tuple-element.126), channel_id=1, source_target_pairs={{0,1},{1,0},{2,3},{3,2},{4,5},{5,4},{6,7},{7,6},{8,9},{9,8},{10,11... | collective-permute-start | bytes 884744 | tf_op jit(solution)/shard_map/ppermute | solution.py:682
  29.8 9.1 %collective-permute-start.6 = (bf16[4,24,1664]{2,1,0:T(8,128)(2,1)S(1)}, bf16[4,24,1664]{2,1,0:T(8,128)(2,1)S(1)}, u32[]{:S(2)}, u32[]{:S(2)}) collective-permute-start(bf16[4,24,1664]{2,1,0:T(8,128)(2,1)S(1)} %get-tuple-element.124), channel_id=1, source_target_pairs={{0,16},{16,0},{1,17},{17,1},{2,18},{18,2},{3,19},{19,3},{4,20},{20... | collective-permute-start | bytes 958472 | tf_op jit(solution)/shard_map/ppermute | solution.py:682
  36.1 21.2 %collective-permute-start.4 = (bf16[4,2,24,1536]{3,2,0,1:T(8,128)(2,1)S(1)}, bf16[4,2,24,1536]{3,2,0,1:T(8,128)(2,1)S(1)}, u32[]{:S(2)}, u32[]{:S(2)}) collective-permute-start(bf16[4,2,24,1536]{3,2,0,1:T(8,128)(2,1)S(1)} %get-tuple-element.128), channel_id=1, source_target_pairs={{0,16},{16,0},{1,17},{17,1},{2,18},{18,2},{3,19},{19,3},{4,20},{20... | collective-permute-start | bytes 1769480 | tf_op jit(solution)/shard_map/ppermute | solution.py:682
  39.1 18.2 %collective-permute-start.7 = (bf16[2,4,24,1664]{3,2,1,0:T(8,128)(2,1)S(1)}, bf16[2,4,24,1664]{3,2,1,0:T(8,128)(2,1)S(1)}, u32[]{:S(2)}, u32[]{:S(2)}) collective-permute-start(bf16[2,4,24,1664]{3,2,1,0:T(8,128)(2,1)S(1)} %reverse_select_fusion.2), channel_id=1, source_target_pairs={{0,1},{1,0},{2,3},{3,2},{4,5},{5,4},{6,7},{7,6},{8,9},{9,8},{10,11... | collective-permute-start | bytes 1916936 | tf_op jit(solution)/shard_map/ppermute | solution.py:682
  57.8 1.0 copy-start.4
  57.8 3.2 collective-permute-start.8
  58.2 5.1 %copy-start.5 = (bf16[2,4,2,24,1536]{4,3,2,1,0:T(8,128)(2,1)}, bf16[2,4,2,24,1536]{4,3,2,1,0:T(8,128)(2,1)S(1)}, u32[]{:S(2)}) copy-start(bf16[2,4,2,24,1536]{4,3,2,1,0:T(8,128)(2,1)S(1)} %copy.47) | copy-start | bytes 3538948
  58.2 5.1 %collective-permute-start.5 = (bf16[2,192,1536]{2,1,0:T(8,128)(2,1)S(1)}, bf16[2,192,1536]{2,1,0:T(8,128)(2,1)}, u32[]{:S(2)}, u32[]{:S(2)}) collective-permute-start(bf16[2,192,1536]{2,1,0:T(8,128)(2,1)S(1)} %bitcast.54), channel_id=1, source_target_pairs={{0,8},{8,0},{1,9},{9,1},{2,10},{10,2},{3,11},{11,3},{4,12},{12,4},... | collective-permute-start | bytes 3538952 | tf_op jit(solution)/shard_map/ppermute | solution.py:757
  159.4 4.7 %collective-permute-start.9 = (bf16[2,192,3072]{2,1,0:T(8,128)(2,1)}, bf16[2,192,3072]{2,1,0:T(8,128)(2,1)S(1)}, u32[]{:S(2)}, u32[]{:S(2)}) collective-permute-start(bf16[2,192,3072]{2,1,0:T(8,128)(2,1)} %get-tuple-element.79), channel_id=1, source_target_pairs={{0,8},{8,0},{1,9},{9,1},{2,10},{10,2},{3,11},{11,3},{4,12},{12,4},... | collective-permute-start | bytes 7077896 | tf_op jit(solution)/shard_map/ppermute | solution.py:782
  164.1 1.4 copy-start.2
  169.8 61.8 %all-to-all-start = ((bf16[16,24,3072]{2,1,0:T(8,128)(2,1)}), bf16[16,24,3072]{2,1,0:T(8,128)(2,1)S(1)}, u32[]{:S(2)}, u32[]{:S(2)}) async-start(bf16[16,24,3072]{2,1,0:T(8,128)(2,1)} %bitcast.47), calls=%async_computation | async-start | bytes 4718592 | tf_op jit(solution)/shard_map/all_to_all | solution.py:786
  205.5 15.0 %copy-start.7 = (f32[3,8,768]{2,1,0:T(8,128)S(1)}, f32[3,8,768]{2,1,0:T(8,128)}, u32[]{:S(2)}) copy-start(f32[3,8,768]{2,1,0:T(8,128)} %get-tuple-element.96) | copy-start | bytes 221188
  205.5 15.1 %copy-start.8 = (f32[3,8,768]{2,1,0:T(8,128)S(1)}, f32[3,8,768]{2,1,0:T(8,128)}, u32[]{:S(2)}) copy-start(f32[3,8,768]{2,1,0:T(8,128)} %get-tuple-element.94) | copy-start | bytes 221188
  205.5 15.1 %copy-start.6 = (f32[8,3072]{1,0:T(8,128)S(1)}, f32[8,3072]{1,0:T(8,128)}, u32[]{:S(2)}) copy-start(f32[8,3072]{1,0:T(8,128)} %get-tuple-element.95) | copy-start | bytes 294916
  220.5 6.7 %collective-permute-start.10 = (bf16[2,192,3072]{2,1,0:T(8,128)(2,1)}, bf16[2,192,3072]{2,1,0:T(8,128)(2,1)}, u32[]{:S(2)}, u32[]{:S(2)}) collective-permute-start(bf16[2,192,3072]{2,1,0:T(8,128)(2,1)} %get-tuple-element.87), channel_id=1, source_target_pairs={{0,8},{8,0},{1,9},{9,1},{2,10},{10,2},{3,11},{11,3},{4,12},{12,4},... | collective-permute-start | bytes 7077896 | tf_op jit(solution)/shard_map/ppermute | solution.py:782
  231.6 1.4 copy-start.1
  233.0 60.5 %all-to-all-start.2 = ((bf16[16,24,3072]{2,1,0:T(8,128)(2,1)}), bf16[16,24,3072]{2,1,0:T(8,128)(2,1)}, u32[]{:S(2)}, u32[]{:S(2)}) async-start(bf16[16,24,3072]{2,1,0:T(8,128)(2,1)} %bitcast.46), calls=%async_computation.2 | async-start | bytes 4718592 | tf_op jit(solution)/shard_map/all_to_all | solution.py:786
  271.9 13.4 %copy-start.12 = (bf16[2,192,768]{2,1,0:T(8,128)(2,1)S(1)}, bf16[2,192,768]{2,1,0:T(8,128)(2,1)}, u32[]{:S(2)}) copy-start(bf16[2,192,768]{2,1,0:T(8,128)(2,1)} %get-tuple-element.99) | copy-start | bytes 1769476
  272.0 17.9 %copy-start.3 = (bf16[2,192,768]{2,1,0:T(8,128)(2,1)S(1)}, bf16[2,192,768]{2,1,0:T(8,128)(2,1)}, u32[]{:S(2)}) copy-start(bf16[2,192,768]{2,1,0:T(8,128)(2,1)} %get-tuple-element.89.refs_2_) | copy-start | bytes 1769476
  285.1 4.8 %collective-permute-start.11 = (bf16[2,192,2432]{2,1,0:T(8,128)(2,1)}, bf16[2,192,2432]{2,1,0:T(8,128)(2,1)S(1)}, u32[]{:S(2)}, u32[]{:S(2)}) collective-permute-start(bf16[2,192,2432]{2,1,0:T(8,128)(2,1)} %get-tuple-element.98), channel_id=1, source_target_pairs={{0,8},{8,0},{1,9},{9,1},{2,10},{10,2},{3,11},{11,3},{4,12},{12,4},... | collective-permute-start | bytes 5603336 | tf_op jit(solution)/shard_map/ppermute | solution.py:782
  285.3 4.5 %collective-permute-start.12 = (bf16[2,192,768]{2,1,0:T(8,128)(2,1)S(1)}, bf16[2,192,768]{2,1,0:T(8,128)(2,1)S(1)}, u32[]{:S(2)}, u32[]{:S(2)}) collective-permute-start(bf16[2,192,768]{2,1,0:T(8,128)(2,1)S(1)} %copy-done.12), channel_id=1, source_target_pairs={{0,8},{8,0},{1,9},{9,1},{2,10},{10,2},{3,11},{11,3},{4,12},{12,4},... | collective-permute-start | bytes 1769480 | tf_op jit(solution)/shard_map/ppermute | solution.py:782
  293.5 61.6 %all-to-all-start.1 = ((bf16[16,24,3200]{2,1,0:T(8,128)(2,1)}), bf16[16,24,3200]{2,1,0:T(8,128)(2,1)S(1)}, u32[]{:S(2)}, u32[]{:S(2)}) async-start(bf16[16,24,3200]{2,1,0:T(8,128)(2,1)} %bitcast.25), calls=%async_computation.1 | async-start | bytes 4915200 | tf_op jit(solution)/shard_map/all_to_all | solution.py:786
  355.2 1.4 copy-start
  359.7 17.7 %copy-start.9 = (f32[288]{0:T(512)S(1)}, f32[288]{0:T(512)}, u32[]{:S(2)}) copy-start(f32[288]{0:T(512)} %param.25) | copy-start | bytes 3460
  359.7 17.7 %copy-start.10 = (f32[288]{0:T(512)S(1)}, f32[288]{0:T(512)}, u32[]{:S(2)}) copy-start(f32[288]{0:T(512)} %param.34) | copy-start | bytes 3460
  359.7 17.7 %copy-start.11 = (f32[288]{0:T(512)S(1)}, f32[288]{0:T(512)}, u32[]{:S(2)}) copy-start(f32[288]{0:T(512)} %param.35) | copy-start | bytes 3460
Sparse Core Ops, SparseCore 0:
  11.5 94.8 all-gather.1

commit v4 on v3

--- a/solution.py
+++ b/solution.py
@@ -238,7 +238,27 @@
     )
 
 
+def tile_spec(rows, columns, tiles):
+    return pl.BlockSpec((rows, columns), lambda step, *_: (jnp.minimum(step, tiles - 1), 0))
+
+
+def late_spec(shape, tiles):
+    return pl.BlockSpec(shape, lambda step, *_: (0, 0, jnp.maximum(step - tiles, 0)))
+
+
+def late_grad(tiles, core, left, right, keep_out, send_out, total):
+    step, block = pl.program_id(0), total.shape[1]
+
+    @pl.when(step >= tiles)
+    def _():
+        columns = pl.ds(pl.multiple_of((step - tiles) * block, block), block)
+        total[...] = dot_tn(left[...], right[:, columns])
+        split_rows(total, core, keep_out, send_out)
+
+
 def mlp_forward_body(
+    tiles,
+    core,
     counts,
     normed_one,
     cotangent,
@@ -246,178 +266,235 @@
     w_down,
     small,
     result_out,
-    active_out,
     slope_out,
     second_out,
-    second_low_out,
     sums_out,
+    keep_out,
+    send_out,
+    active_all,
+    second_all,
+    total,
+    sums,
 ):
-    rows, width = normed_one.shape
     step = pl.program_id(0)
-    at = small_places(width, small.shape[1] - 8 * width)
-    hidden = normed_one[...] * small[:, slice(*at["g1"])] + small[:, slice(*at["s1"])]
-    hidden_low = hidden.astype(BF16)
-    pre_act = dot_nn(hidden_low, w_up[...]) + small[:, slice(*at["b1"])]
-    spread = 0.5 * (1.0 + lax.erf(pre_act * math.sqrt(0.5)))
-    density = jnp.exp(-0.5 * pre_act * pre_act) * (1.0 / math.sqrt(2.0 * math.pi))
-    active = (pre_act * spread).astype(BF16)
-    active_out[...] = active
-    slope_out[...] = spread + pre_act * density
-    second = hidden + dot_nt(active, w_down[...]) + small[:, slice(*at["b2"])]
-    normed, inverse = normalize(second)
-    gain = small[:, slice(*at["g2"])]
-    index = lax.broadcasted_iota(jnp.int32, (SEG_LEN, 1), 0)
-    live = jnp.concatenate(
-        [
-            (index < counts[step * (rows // SEG_LEN) + segment]).astype(F32)
-            for segment in range(rows // SEG_LEN)
-        ],
-        axis=0,
-    )
-    result_out[...] = ((normed * gain + small[:, slice(*at["s2"])]) * live).astype(BF16)
-    incoming = cotangent[...].astype(F32) * live
-    grad_second = norm_back(incoming * gain, normed, inverse)
-    second_out[...] = grad_second
-    second_low_out[...] = grad_second.astype(BF16)
 
     @pl.when(step == 0)
     def _():
-        sums_out[...] = jnp.zeros_like(sums_out)
-
-    sums_out[0] += fold_rows(incoming * normed)
-    sums_out[1] += fold_rows(incoming)
-    sums_out[2] += fold_rows(grad_second)
-
-
-def mlp_forward(counts, normed_one, cotangent, packed, small, block=256):
+        sums[...] = jnp.zeros_like(sums)
+
+    @pl.when(step < tiles)
+    def _():
+        rows, width = normed_one.shape
+        at = small_places(width, small.shape[1] - 8 * width)
+        hidden = normed_one[...] * small[:, slice(*at["g1"])] + small[:, slice(*at["s1"])]
+        pre_act = dot_nn(hidden.astype(BF16), w_up[...]) + small[:, slice(*at["b1"])]
+        spread = 0.5 * (1.0 + lax.erf(pre_act * math.sqrt(0.5)))
+        density = jnp.exp(-0.5 * pre_act * pre_act) * (1.0 / math.sqrt(2.0 * math.pi))
+        active = (pre_act * spread).astype(BF16)
+        place = pl.ds(pl.multiple_of(step * rows, rows), rows)
+        active_all[place, :] = active
+        slope_out[...] = spread + pre_act * density
+        second = hidden + dot_nt(active, w_down[...]) + small[:, slice(*at["b2"])]
+        normed, inverse = normalize(second)
+        gain = small[:, slice(*at["g2"])]
+        index = lax.broadcasted_iota(jnp.int32, (SEG_LEN, 1), 0)
+        live = jnp.concatenate(
+            [
+                (index < counts[step * (rows // SEG_LEN) + segment]).astype(F32)
+                for segment in range(rows // SEG_LEN)
+            ],
+            axis=0,
+        )
+        result_out[...] = ((normed * gain + small[:, slice(*at["s2"])]) * live).astype(BF16)
+        incoming = cotangent[...].astype(F32) * live
+        grad_second = norm_back(incoming * gain, normed, inverse)
+        second_out[...] = grad_second
+        second_all[place, :] = grad_second.astype(BF16)
+        sums[0] += fold_rows(incoming * normed)
+        sums[1] += fold_rows(incoming)
+        sums[2] += fold_rows(grad_second)
+
+    @pl.when(step == tiles)
+    def _():
+        sums_out[...] = jnp.sum(sums[...], axis=1)
+
+    late_grad(tiles, core, second_all, active_all, keep_out, send_out, total)
+
+
+def mlp_forward(core, counts, normed_one, cotangent, packed, small, groups, block=256, wide=512):
     rows, width = normed_one.shape
     hidden = packed.shape[1] // 2
-    return call_kernel(
-        mlp_forward_body,
+    tiles = rows // block
+    shape = (groups, width // (2 * groups), hidden)
+    grad_spec = late_spec((*shape[:2], wide), tiles)
+    return call_kernel(
+        functools.partial(mlp_forward_body, tiles),
         "mlp_forward",
-        (rows // block,),
+        (tiles + hidden // wide,),
         [normed_one, cotangent, packed, packed, small],
         [
-            row_spec(block, width),
-            row_spec(block, width),
+            tile_spec(block, width, tiles),
+            tile_spec(block, width, tiles),
             held_spec(width, hidden),
             held_spec(width, hidden, 1),
             held_spec(1, small.shape[1]),
         ],
         [
             shaped((rows, width), BF16),
-            shaped((rows, hidden), BF16),
             shaped((rows, hidden), F32),
             shaped((rows, width), F32),
-            shaped((rows, width), BF16),
-            shaped((3, 8, width), F32),
-        ],
-        [
-            row_spec(block, width),
-            row_spec(block, hidden),
-            row_spec(block, hidden),
-            row_spec(block, width),
-            row_spec(block, width),
-            whole_spec((3, 8, width)),
-        ],
-        scalars=[counts],
-        flops=4 * rows * width * hidden,
-    )
-
-
-def mlp_backward_body(fresh, *refs):
-    grad_second, slope, normed_one, inverse_one, w_up, w_down, small = refs[:7]
-    pre_out, first_out, first_low_out, sums_out, wide_out = refs[-5:]
-    rows, width = normed_one.shape
-    hidden = slope.shape[1]
-    chunk = width
-    at = small_places(width, hidden)
-
-    @pl.when(pl.program_id(0) == 0)
-    def _():
-        if fresh:
-            sums_out[...] = jnp.zeros_like(sums_out)
-            wide_out[...] = jnp.zeros_like(wide_out)
-        else:
-            sums_out[...] = refs[7][...]
-            wide_out[...] = refs[8][...]
-
-    incoming = grad_second[...]
-    incoming_low = incoming.astype(BF16)
-    grad_hidden = incoming
-    for piece in range(hidden // chunk):
-        columns = slice(piece * chunk, (piece + 1) * chunk)
-        grad_pre = dot_nn(incoming_low, w_down[:, columns]) * slope[:, columns]
-        wide_out[:, columns] += fold_rows(grad_pre)
-        grad_low = grad_pre.astype(BF16)
-        pre_out[:, columns] = grad_low
-        grad_hidden = grad_hidden + dot_nt(grad_low, w_up[:, columns])
-    normed = normed_one[...]
-    sums_out[0] += fold_rows(grad_hidden * normed)
-    sums_out[1] += fold_rows(grad_hidden)
-    grad_first = norm_back(
-        grad_hidden * small[:, slice(*at["g1"])], normed, inverse_one[:, :1]
-    )
-    first_out[...] = grad_first
-    first_low_out[...] = grad_first.astype(BF16)
-    sums_out[2] += fold_rows(grad_first)
+            shaped((3, width), F32),
+            shaped(shape, BF16),
+            shaped(shape, BF16),
+        ],
+        [
+            tile_spec(block, width, tiles),
+            tile_spec(block, hidden, tiles),
+            tile_spec(block, width, tiles),
+            whole_spec((3, width)),
+            grad_spec,
+            grad_spec,
+        ],
+        scalars=[core, counts],
+        scratch=[
+            pltpu.VMEM((rows, hidden), BF16),
+            pltpu.VMEM((rows, width), BF16),
+            pltpu.VMEM((width, wide), F32),
+            pltpu.VMEM((3, 8, width), F32),
+        ],
+        flops=6 * rows * width * hidden,
+    )
+
+
+def mlp_backward_body(
+    tiles,
+    core,
+    grad_second,
+    slope,
+    normed_one,
+    inverse_one,
+    hidden_low,
+    w_up,
+    w_down,
+    small,
+    first_out,
+    first_low_out,
+    sums_out,
+    wide_out,
+    keep_out,
+    send_out,
+    pre_all,
+    hidden_all,
+    total,
+    sums,
+    wide_sums,
+):
+    step = pl.program_id(0)
+
+    @pl.when(step == 0)
+    def _():
+        sums[...] = jnp.zeros_like(sums)
+        wide_sums[...] = jnp.zeros_like(wide_sums)
+
+    @pl.when(step < tiles)
+    def _():
+        rows, width = normed_one.shape
+        hidden = slope.shape[1]
+        chunk = width
+        at = small_places(width, hidden)
+        place = pl.ds(pl.multiple_of(step * rows, rows), rows)
+        hidden_all[place, :] = hidden_low[...]
+        incoming = grad_second[...]
+        incoming_low = incoming.astype(BF16)
+        grad_hidden = incoming
+        for piece in range(hidden // chunk):
+            columns = slice(piece * chunk, (piece + 1) * chunk)
+            grad_pre = dot_nn(incoming_low, w_down[:, columns]) * slope[:, columns]
+            wide_sums[:, columns] += fold_rows(grad_pre)
+            grad_low = grad_pre.astype(BF16)
+            pre_all[place, columns] = grad_low
+            grad_hidden = grad_hidden + dot_nt(grad_low, w_up[:, columns])
+        normed = normed_one[...]
+        sums[0] += fold_rows(grad_hidden * normed)
+        sums[1] += fold_rows(grad_hidden)
+        grad_first = norm_back(
+            grad_hidden * small[:, slice(*at["g1"])], normed, inverse_one[:, :1]
+        )
+        first_out[...] = grad_first
+        first_low_out[...] = grad_first.astype(BF16)
+        sums[2] += fold_rows(grad_first)
+
+    @pl.when(step == tiles)
+    def _():
+        sums_out[...] = jnp.sum(sums[...], axis=1)
+        wide_out[...] = jnp.sum(wide_sums[...], axis=0, keepdims=True)
+
+    late_grad(tiles, core, hidden_all, pre_all, keep_out, send_out, total)
 
 
 def mlp_backward(
-    grad_second, slope, normed_one, inverse_one, packed, small, span, earlier=None, after=(), block=256
+    core, grad_second, slope, normed_one, inverse_one, hidden_low, packed, small, groups, after=(), block=256, wide=512
 ):
     rows, width = normed_one.shape
     hidden = slope.shape[1]
-
-    def placed(columns):
-        return pl.BlockSpec((block, columns), lambda step, *_: (span[0] + step, 0))
-
-    hbm = pl.BlockSpec(memory_space=pl.ANY)
-    sums_spec, wide_spec = whole_spec((3, 8, width)), whole_spec((8, hidden))
-    inputs = [grad_second, slope, normed_one, inverse_one, packed, packed, small]
-    in_specs = [
-        placed(width),
-        placed(hidden),
-        placed(width),
-        placed(LANES),
-        held_spec(width, hidden),
-        held_spec(width, hidden, 1),
-        held_spec(1, small.shape[1]),
-    ]
-    aliases = None
-    if earlier is not None:
-        inputs += [earlier[3], earlier[4], *earlier[:3]]
-        in_specs += [sums_spec, wide_spec, hbm, hbm, hbm]
-        aliases = {9: 0, 10: 1, 11: 2}
-    return call_kernel(
-        functools.partial(mlp_backward_body, earlier is None),
+    tiles = rows // block
+    shape = (groups, width // (2 * groups), hidden)
+    grad_spec = late_spec((*shape[:2], wide), tiles)
+    return call_kernel(
+        functools.partial(mlp_backward_body, tiles),
         "mlp_backward",
-        (span[1] - span[0],),
-        inputs,
-        in_specs,
-        [
-            shaped((rows, hidden), BF16),
+        (tiles + hidden // wide,),
+        [grad_second, slope, normed_one, inverse_one, hidden_low, packed, packed, small],
+        [
+            tile_spec(block, width, tiles),
+            tile_spec(block, hidden, tiles),
+            tile_spec(block, width, tiles),
+            tile_spec(block, LANES, tiles),
+            tile_spec(block, width, tiles),
+            held_spec(width, hidden),
+            held_spec(width, hidden, 1),
+            held_spec(1, small.shape[1]),
+        ],
+        [
             shaped((rows, width), F32),
             shaped((rows, width), BF16),
-            shaped((3, 8, width), F32),
-            shaped((8, hidden), F32),
-        ],
-        [placed(hidden), placed(width), placed(width), sums_spec, wide_spec],
+            shaped((3, width), F32),
+            shaped((1, hidden), F32),
+            shaped(shape, BF16),
+            shaped(shape, BF16),
+        ],
+        [
+            tile_spec(block, width, tiles),
+            tile_spec(block, width, tiles),
+            whole_spec((3, width)),
+            whole_spec((1, hidden)),
+            grad_spec,
+            grad_spec,
+        ],
+        scalars=[core],
+        scratch=[
+            pltpu.VMEM((rows, hidden), BF16),
+            pltpu.VMEM((rows, width), BF16),
+            pltpu.VMEM((width, wide), F32),
+            pltpu.VMEM((3, 8, width), F32),
+            pltpu.VMEM((8, hidden), F32),
+        ],
         after=after,
-        aliases=aliases,
-        flops=4 * (span[1] - span[0]) * block * width * hidden,
-    )
-
-
-def attention_backward_body(fresh, *refs):
-    first_low, joined, probs, w_out = refs[:4]
-    joined_grad_out, sums_out, grad_mixed = refs[-3:]
+        flops=6 * rows * width * hidden,
+    )
+
+
+def attention_backward_body(
+    first_low, joined, probs, w_out, pieces, joined_grad_out, sums_out, folded_out, grad_mixed, sums
+):
     rows, width = first_low.shape
-
-    @pl.when(pl.program_id(0) == 0)
-    def _():
-        sums_out[...] = jnp.zeros_like(sums_out) if fresh else refs[4][...]
-
+    step = pl.program_id(0)
+
+    @pl.when(step == 0)
+    def _():
+        sums[...] = jnp.zeros_like(sums)
+
+    folded_out[...] = jnp.sum(pieces[...].astype(F32), axis=0)
     grad_mixed[...] = dot_nn(first_low[...], w_out[...]).astype(BF16)
     for segment in range(rows // SEG_LEN):
         place = slice(segment * SEG_LEN, (segment + 1) * SEG_LEN)
@@ -437,40 +514,44 @@
             joined_grad_out[place, low:high] = grad_query.astype(BF16)
             joined_grad_out[place, width + low : width + high] = grad_keyed.astype(BF16)
             joined_grad_out[place, 2 * width + low : 2 * width + high] = grad_valued.astype(BF16)
-            sums_out[0, :, low:high] += fold_rows(grad_query)
-            sums_out[1, :, low:high] += fold_rows(grad_valued)
-
-
-def attention_backward(first_low, joined, probs, w_out, span, earlier=None, after=(), block=256):
+            sums[0, :, low:high] += fold_rows(grad_query)
+            sums[1, :, low:high] += fold_rows(grad_valued)
+
+    @pl.when(step == pl.num_programs(0) - 1)
+    def _():
+        sums_out[...] = jnp.sum(sums[...], axis=1)
+
+
+def attention_backward(first_low, joined, probs, w_out, pieces, after=(), block=256):
     rows, width = first_low.shape
-
-    def placed(columns):
-        return pl.BlockSpec((block, columns), lambda step, *_: (span[0] + step, 0))
-
-    inputs = [first_low, joined, probs, w_out]
-    in_specs = [
-        placed(width),
-        placed(3 * width),
-        placed(2 * width),
-        held_spec(width, width),
-    ]
-    aliases = None
-    if earlier is not None:
-        inputs += [earlier[1], earlier[0]]
-        in_specs += [whole_spec((2, 8, width)), pl.BlockSpec(memory_space=pl.ANY)]
-        aliases = {5: 0}
-    return call_kernel(
-        functools.partial(attention_backward_body, earlier is None),
+    steps = rows // block
+    count, own_rows, columns = pieces.shape
+    part = columns // steps
+    return call_kernel(
+        attention_backward_body,
         "attention_backward",
-        (span[1] - span[0],),
-        inputs,
-        in_specs,
-        [shaped((rows, 3 * width), BF16), shaped((2, 8, width), F32)],
-        [placed(3 * width), whole_spec((2, 8, width))],
-        scratch=[pltpu.VMEM((block, width), BF16)],
+        (steps,),
+        [first_low, joined, probs, w_out, pieces],
+        [
+            row_spec(block, width),
+            row_spec(block, 3 * width),
+            row_spec(block, 2 * width),
+            held_spec(width, width),
+            pl.BlockSpec((count, own_rows, part), lambda step, *_: (0, 0, step)),
+        ],
+        [
+            shaped((rows, 3 * width), BF16),
+            shaped((2, width), F32),
+            shaped((own_rows, columns), F32),
+        ],
+        [
+            row_spec(block, 3 * width),
+            whole_spec((2, width)),
+            pl.BlockSpec((own_rows, part), lambda step, *_: (0, step)),
+        ],
+        scratch=[pltpu.VMEM((block, width), BF16), pltpu.VMEM((2, 8, width), F32)],
         after=after,
-        aliases=aliases,
-        flops=16 * (span[1] - span[0]) * block * width * width,
+        flops=16 * rows * width * width,
     )
 
 
@@ -513,52 +594,40 @@
     )
 
 
-def weight_grad_body(has_extra, core, left, right, *refs):
-    keep_out, send_out, total = refs[-3:]
-    block = right.shape[1]
-    total[...] = dot_tn(left[...], right[...])
+def split_rows(total, core, keep_out, send_out, columns=slice(None), order=None):
     groups, rows = keep_out.shape[0], keep_out.shape[1]
-    step = pl.program_id(0)
-    columns = pl.ds(pl.multiple_of(step * block, block), block) if has_extra else slice(None)
     for group in range(groups):
         for flip, target in enumerate((keep_out, send_out)):
             half = core[0] if flip == 0 else 1 - core[0]
             start = pl.multiple_of((2 * group + half) * rows, rows)
-            target[group, :, columns] = total[pl.ds(start, rows), :].astype(BF16)
-    if has_extra:
-        extra = refs[0]
-
-        @pl.when(step == 0)
-        def _():
-            for group in range(groups):
-                for flip, target in enumerate((keep_out, send_out)):
-                    half = core[0] if flip == 0 else 1 - core[0]
-                    target[group, :, target.shape[2] - LANES :] = extra[group, half].astype(BF16)
-
-
-def weight_grad(core, left, right, groups, extra=None, after=(), block=768):
+            if order is None:
+                part = total[pl.ds(start, rows), :]
+            else:
+                size = rows // len(order)
+                places = [pl.multiple_of(start + place * size, 8) for place in order]
+                part = jnp.concatenate([total[pl.ds(place, size), :] for place in places], axis=0)
+            target[group, :, columns] = part.astype(BF16)
+
+
+def weight_grad_body(order, core, left, right, keep_out, send_out, total):
+    total[...] = dot_tn(left[...], right[...])
+    split_rows(total, core, keep_out, send_out, order=order)
+
+
+def weight_grad(core, left, right, groups, order=None, after=(), block=256):
     tokens, height = left.shape
     width = right.shape[1]
-    rows = height // (2 * groups)
-    inputs = [left, right]
-    in_specs = [
-        whole_spec((tokens, height)),
-        pl.BlockSpec((tokens, block), lambda step, *_: (0, step)),
-    ]
-    if extra is None:
-        shape = (groups, rows, width)
-        out_spec = pl.BlockSpec((groups, rows, block), lambda step, *_: (0, 0, step))
-    else:
-        inputs.append(extra)
-        in_specs.append(whole_spec(extra.shape))
-        shape = (groups, rows, width + LANES)
-        out_spec = whole_spec(shape)
-    return call_kernel(
-        functools.partial(weight_grad_body, extra is not None),
+    shape = (groups, height // (2 * groups), width)
+    out_spec = pl.BlockSpec((*shape[:2], block), lambda step, *_: (0, 0, step))
+    return call_kernel(
+        functools.partial(weight_grad_body, order),
         "weight_grad",
         (width // block,),
-        inputs,
-        in_specs,
+        [left, right],
+        [
+            whole_spec((tokens, height)),
+            pl.BlockSpec((tokens, block), lambda step, *_: (0, step)),
+        ],
         [shaped(shape, BF16)] * 2,
         [out_spec, out_spec],
         scalars=[core],
@@ -568,31 +637,117 @@
     )
 
 
-def add_body(*refs):
-    both_out, column = refs[-1], 0
-    for keep, received in zip(refs[:-1:2], refs[1:-1:2]):
+def qkv_grad_body(order, core, left, right, extra, keep_out, send_out, keep_last, send_last, total):
+    step, block = pl.program_id(0), right.shape[1]
+    total[...] = dot_tn(left[...], right[...])
+
+    @pl.when(step < 2)
+    def _():
+        columns = pl.ds(pl.multiple_of(step * block, block), block)
+        split_rows(total, core, keep_out, send_out, columns)
+
+    @pl.when(step == 2)
+    def _():
+        split_rows(total, core, keep_last, send_last, order=order)
+
+    @pl.when(step == 0)
+    def _():
+        for group in range(keep_out.shape[0]):
+            for flip, target in enumerate((keep_out, send_out)):
+                half = core[0] if flip == 0 else 1 - core[0]
+                target[group, :, target.shape[2] - LANES :] = extra[group, half].astype(BF16)
+
+
+def qkv_grad(core, left, right, groups, extra, order):
+    tokens, width = left.shape
+    lead = (groups, width // (2 * groups))
+    shapes = [(*lead, 2 * width + LANES)] * 2 + [(*lead, width)] * 2
+    return call_kernel(
+        functools.partial(qkv_grad_body, order),
+        "qkv_grad",
+        (3,),
+        [left, right, extra],
+        [
+            whole_spec((tokens, width)),
+            pl.BlockSpec((tokens, width), lambda step, *_: (0, step)),
+            whole_spec(extra.shape),
+        ],
+        [shaped(shape, BF16) for shape in shapes],
+        [whole_spec(shape) for shape in shapes],
+        scalars=[core],
+        scratch=[pltpu.VMEM((width, width), F32)],
+        flops=6 * tokens * width * width,
+    )
+
+
+def plane_split_body(count, place, keep_front, other_front, *refs):
+    arrays, front_out, outs = refs[: -count - 1], refs[-count - 1], refs[-count:]
+    column = 0
+    for keep, received in zip(arrays[::2], arrays[1::2]):
         width = keep.shape[-1]
-        both_out[..., column : column + width] = (
-            keep[...].astype(F32) + received[...].astype(F32)
-        ).astype(BF16)
+        for step, out in enumerate(outs):
+            chunk = place[0] ^ step
+            both = keep[chunk].astype(F32) + received[chunk].astype(F32)
+            out[:, column : column + width] = both.astype(out.dtype)
         column += width
-
-
-def add_pairs(pairs, after=()):
-    groups, rows = pairs[0][0].shape[:2]
-    arrays = [array for pair in pairs for array in pair]
-    shape = (groups, rows, sum(pair[0].shape[-1] for pair in pairs))
-    return call_kernel(
-        add_body,
-        "add_pairs",
+    front_out[...] = (keep_front[...].astype(F32) + other_front[...].astype(F32)).astype(BF16)
+
+
+def plane_split(front, pairs, place, count, after=()):
+    arrays = [part.reshape(count, -1, part.shape[-1]) for pair in pairs for part in pair]
+    shape = (arrays[0].shape[1], sum(array.shape[2] for array in arrays[::2]))
+    outs = [shaped(front[0].shape, BF16), shaped(shape, F32)] + [shaped(shape, BF16)] * (count - 1)
+    return call_kernel(
+        functools.partial(plane_split_body, count),
+        "plane_split",
         (1,),
-        arrays,
-        [whole_spec(array.shape) for array in arrays],
-        shaped(shape, BF16),
-        whole_spec(shape),
+        [*front, *arrays],
+        [whole_spec(array.shape) for array in (*front, *arrays)],
+        outs,
+        [whole_spec(out.shape) for out in outs],
+        scalars=[place],
         after=after,
-        vmem=SMALL_VMEM,
-    )
+    )
+
+
+def line_split_body(pieces, count, place, *refs):
+    outs, total = refs[-1 - count : -1], refs[-1]
+    total[...] = sum(ref[...].astype(F32) for ref in refs[:pieces])
+    rows = outs[0].shape[0]
+    for step, out in enumerate(outs):
+        start = pl.multiple_of((place[0] ^ step) * rows, rows)
+        out[...] = total[pl.ds(start, rows), :].astype(out.dtype)
+
+
+def line_split(pieces, place, count, after=()):
+    rows, width = pieces[0].shape
+    shape = (rows // count, width)
+    outs = [shaped(shape, F32)] + [shaped(shape, BF16)] * (count - 1)
+    return call_kernel(
+        functools.partial(line_split_body, len(pieces), count),
+        "line_split",
+        (1,),
+        pieces,
+        [whole_spec(piece.shape) for piece in pieces],
+        outs,
+        [whole_spec(shape)] * count,
+        scalars=[place],
+        scratch=[pltpu.VMEM((rows, width), F32)],
+        after=after,
+    )
+
+
+def trade(parts, axis):
+    count = len(parts)
+    return [parts[0]] + [
+        lax.ppermute(parts[step], axis, [(place, place ^ step) for place in range(count)])
+        for step in range(1, count)
+    ]
+
+
+def add_pairs(pairs):
+    sums = [(keep.astype(F32) + received.astype(F32)).astype(BF16) for keep, received in pairs]
+    return sums[0] if len(sums) == 1 else jnp.concatenate(sums, axis=-1)
 
 
 def fold_body(pieces, total_out):
@@ -614,22 +769,30 @@
     )
 
 
-def squares_body(pieces, *refs):
-    total_out, spread_out = refs[-2:]
+def squares_body(parts, pieces, *refs):
+    total_out, *totals, spread_out = refs[-3 if parts else -2 :]
+    others = refs[parts : len(refs) - (3 if parts else 2)]
     total = jnp.sum(pieces[...].astype(F32), axis=0)
     total_out[...] = total
     squares = jnp.sum(total * total)
-    for other in refs[:-2]:
+    if parts:
+        total = sum(ref[...].astype(F32) for ref in refs[:parts])
+        totals[0][...] = total
+        squares = squares + jnp.sum(total * total)
+    for other in others:
         squares = squares + jnp.sum(other[...] * other[...])
     spread_out[...] = jnp.zeros(spread_out.shape, F32) + squares
 
 
-def fold_with_squares(pieces, others, copies, after=()):
+def fold_with_squares(pieces, parts, others, copies, after=()):
     count, rows, width = pieces.shape
-    inputs = [pieces, *others]
-    outs = [shaped((rows, width), F32), shaped((copies, LANES), F32)]
-    return call_kernel(
-        squares_body,
+    inputs = [pieces, *parts, *others]
+    outs = [shaped((rows, width), F32)]
+    if parts:
+        outs.append(shaped(parts[0].shape, F32))
+    outs.append(shaped((copies, LANES), F32))
+    return call_kernel(
+        functools.partial(squares_body, len(parts)),
         "fold_with_squares",
         (1,),
         inputs,
@@ -773,8 +936,8 @@
         whole_qkv,
         whole_out,
     ) = attention_forward(core, seg_counts, tokens, quarters, small)
-    result, active, slope, grad_second, second_low, sums_two = mlp_forward(
-        seg_counts, normed_one, cotangent, packed, small
+    result, slope, grad_second, sums_two, *down = mlp_forward(
+        core, seg_counts, normed_one, cotangent, packed, small, high_count
     )
 
     def swap_cores(parts):
@@ -786,59 +949,74 @@
         pieces = lax.all_to_all(both.reshape(-1, columns), PEERS, 0, 0, tiled=True)
         return pieces.reshape(high_count * inner_count, own_rows, columns)
 
-    blocks = tokens.shape[0] // 256
-    saved = (grad_second, slope, normed_one, inverse_one, packed, small)
-    down = weight_grad(core, second_low, active, high_count, block=512)
     down = add_pairs([swap_cores(down)])
-    grad_pre, grad_first, first_low, sums_one, sums_wide = mlp_backward(
-        *saved, (0, blocks), after=[down]
+    grad_first, first_low, sums_one, sums_wide, *up = mlp_backward(
+        core,
+        grad_second,
+        slope,
+        normed_one,
+        inverse_one,
+        hidden_low,
+        packed,
+        small,
+        high_count,
+        after=[down],
     )
     down = peer_sum(down)
-    up = weight_grad(core, hidden_low, grad_pre, high_count, block=512)
-    out = weight_grad(core, first_low, mixed, high_count, after=[up[0]], block=256)
-    up = add_pairs([swap_cores(up)], after=[out[0]])
-    sum_down = fold_pieces(down, after=[up])
+    by_low = [zed * low_count + low for low in range(low_count) for zed in range(zed_count)]
+    order = by_low if own_rows % 8 == 0 else None
+    out = weight_grad(core, first_low, mixed, high_count, order, after=[up[0]])
+    keep, received = swap_cores(up)
+    keep, out_done = lax.optimization_barrier((keep, out[0]))
+    up = add_pairs([(keep, received)])
     out = swap_cores(out)
-    joined_grad, sums_qv = attention_backward(
-        first_low, joined, probs, whole_out, (0, blocks), after=[sum_down]
+    joined_grad, sums_qv, sum_down = attention_backward(
+        first_low, joined, probs, whole_out, down, after=[out_done, up]
     )
     up = peer_sum(up)
-
     grad_small = jnp.concatenate(
         [
-            jnp.sum(sums_qv, axis=1).reshape(-1),
-            jnp.sum(sums_one[2], axis=0),
-            jnp.sum(sums_wide, axis=0),
-            jnp.sum(sums_two[2], axis=0),
-            jnp.sum(sums_one[:2], axis=1).reshape(-1),
-            jnp.sum(sums_two[:2], axis=1).reshape(-1),
+            sums_qv.reshape(-1),
+            sums_one[2],
+            sums_wide[0],
+            sums_two[2],
+            sums_one[:2].reshape(-1),
+            sums_two[:2].reshape(-1),
         ]
     )
     by_owner = jnp.pad(
         grad_small.reshape(high_count, 2, inner_count * own_rows, per_row),
         ((0, 0),) * 3 + ((0, LANES - per_row),),
     )
-    qkv = weight_grad(core, tokens, joined_grad, high_count, extra=by_owner)
-    front = jnp.concatenate(
-        [
-            (keep.astype(F32) + received.astype(F32)).astype(BF16)
-            for keep, received in (swap_cores(qkv), out)
-        ],
-        axis=-1,
-    )
-    grad_inputs = grad_tokens(joined_grad, grad_first, whole_qkv, after=[front])
-    sum_up = fold_pieces(up, after=[grad_inputs])
-    sum_front, spread = fold_with_squares(peer_sum(front), [sum_up, sum_down], device_count)
+    *query, keep, send = qkv_grad(core, tokens, joined_grad, high_count, by_owner, order)
+    value = swap_cores((keep, send))
+    query = swap_cores(query)
+    if order is not None:
+        plane = high_count * low_count
+        high, low = lax.axis_index("hi"), lax.axis_index("low")
+        place = (high * low_count + low).astype(jnp.int32).reshape(1)
+        front, *last = plane_split(query, [value, out], place, plane)
+        last = trade(last, PLANE)
+        grad_inputs = grad_tokens(joined_grad, grad_first, whole_qkv, after=[front, last[0]])
+        place = lax.axis_index("zed").astype(jnp.int32).reshape(1)
+        last = trade(line_split(last, place, zed_count, after=[grad_inputs]), "zed")
+    else:
+        front = add_pairs([query, value, out])
+        grad_inputs = grad_tokens(joined_grad, grad_first, whole_qkv, after=[front])
+        last = []
+    sum_up = fold_pieces(up, after=[grad_inputs, *last[:1]])
+    sum_front, *sum_last, spread = fold_with_squares(
+        peer_sum(front), last, [sum_up, sum_down], device_count
+    )
+    cut = 2 * width + LANES
+    if order is None:
+        sum_last = [sum_front[:, cut:]]
+    sum_qkv = jnp.concatenate([sum_front[:, : 2 * width], sum_last[0][:, :width]], axis=1)
     squares = lax.all_to_all(spread, ALL, 0, 0, tiled=True)
     *updated, norm_row = update_weights(
         squares,
-        [sum_front, sum_up, sum_down],
-        (
-            (0, 0, 3 * width),
-            (0, 3 * width + LANES, 4 * width + LANES),
-            (1, 0, hidden),
-            (2, 0, hidden),
-        ),
+        [sum_qkv, sum_last[0], sum_up, sum_down],
+        ((0, 0, 3 * width), (1, width, 2 * width), (2, 0, hidden), (3, 0, hidden)),
         [
             *(w_qkv, first_qkv, second_qkv),
             *(w_out, first_out, second_out),
@@ -848,7 +1026,7 @@
     )
     grad_norm = norm_row[0, 0]
     factor = CLIP_LIMIT / jnp.maximum(grad_norm, CLIP_LIMIT)
-    sum_small = sum_front[:, 3 * width : 3 * width + per_row].reshape(own_small)
+    sum_small = sum_front[:, 2 * width : 2 * width + per_row].reshape(own_small)
     updated += adam_update(
         small_params, first_small, second_small, sum_small * factor, RATE_SMALL, 0.0
     )

time: 386 us -> 366 us (0.948)
  waiting for transfers between devices: 94.5 us -> 80.7 us
  blocking collectives: 12 us -> 0 us
  starting transfers between devices: 30.6 us -> 41.5 us
  Pallas kernels: 214 us -> 204 us
  other arithmetic: 10.1 us -> 14.1 us
    all_to_all x3, waiting for transfers between devices: 38.7 us -> 0.26 us  [peer_sum(): pieces = lax.all_to_all(both.reshape(-1, columns), PEERS, 0, 0, tiled=True)]
    ppermute x0 -> x6, waiting for transfers between devices: none -> 17.7 us  [trade(): lax.ppermute(parts[step], axis, [(place, place ^ step) for place in range...]
    all_to_all x1 -> x0, blocking collectives: 12 us -> none  [body(): squares = lax.all_to_all(spread, ALL, 0, 0, tiled=True)]
    pallas_call x16 -> x13, Pallas kernels: 214 us -> 204 us  [call_kernel(): pl.pallas_call(wrapped, grid_spec=pltpu.PrefetchScalarGridSpec(num_scalar...]
    ppermute x0 -> x6, starting transfers between devices: none -> 7.94 us  [trade(): lax.ppermute(parts[step], axis, [(place, place ^ step) for place in range...]
    all_to_all x0 -> x1, waiting for transfers between devices: none -> 6.35 us  [body(): squares = lax.all_to_all(spread, ALL, 0, 0, tiled=True)]
    convert_element_type x2, other arithmetic: 2.12 us -> 7.94 us  [add_pairs(): (keep.astype(F32) + received.astype(F32)).astype(BF16)]
    ppermute x4 -> x5, waiting for transfers between devices: 8.66 us -> 8.68 us  [swap_cores(): return (keep, lax.ppermute(send, 'core', swap))]
  transfers between devices with their start and end apart: 17 -> 25, of which waited for: 10 -> 17; matrix products, arithmetic and copies ran while one was open for 3% -> 4% of each run, Pallas kernels for 38% -> 40%
where the time goes in v4:
time: 366 us; the launch traced here: 365 us
  Pallas kernels  204 us (56%)
  waiting for transfers between devices  80.7 us (22%)
  starting transfers between devices  41.5 us (11%)
  between operations  15.2 us (4%)
  other arithmetic  14.1 us (4%)
  local copies, waits for them, and re-layouts  9.43 us (3%)
    pallas_call x13, Pallas kernels, call_kernel(): pl.pallas_call(wrapped, grid_spec=pltpu.PrefetchScalarGridSpec(num_scalar...  204 us
    ppermute x7, waiting for transfers between devices, gather_axis(): lax.ppermute(value, axis, [(place, place ^ step) for place in range(size)])  36.6 us
    all_to_all x3, starting transfers between devices, peer_sum(): pieces = lax.all_to_all(both.reshape(-1, columns), PEERS, 0, 0, tiled=True)  18 us
    ppermute x6, waiting for transfers between devices, trade(): lax.ppermute(parts[step], axis, [(place, place ^ step) for place in range...  17.7 us
    ppermute x7, starting transfers between devices, gather_axis(): lax.ppermute(value, axis, [(place, place ^ step) for place in range(size)])  11.1 us
    all_gather x1, waiting for transfers between devices, body(): packed = lax.all_gather(back, ALL, axis=0, tiled=True)  9.03 us
    ppermute x5, waiting for transfers between devices, swap_cores(): return (keep, lax.ppermute(send, 'core', swap))  8.68 us
    ppermute x6, starting transfers between devices, trade(): lax.ppermute(parts[step], axis, [(place, place ^ step) for place in range...  7.94 us
  transfers between devices with their start and end apart: 25, of which 17 were waited for; matrix products, arithmetic and copies ran while one was open for 4% of the time, Pallas kernels for 40%

profile of v4, /device:TPU:0, one launch (start us, length us, event | category | flops | bytes accessed | tf_op | source)
XLA Modules:
  0.0 365.0 jit_solution(6694360174986502020)
XLA Ops:
  7.2 1.8 pack_rows.1
  9.1 1.0 convert_element_type.39
  10.0 0.9 convert_element_type.41
  11.7 3.1 collective-permute-start
  14.8 2.6 collective-permute-start.1
  17.4 3.5 collective-permute-done
  21.0 11.1 %collective-permute-done.1 = bf16[24,3200]{1,0:T(8,128)(2,1)S(1)} collective-permute-done((bf16[24,3200]{1,0:T(8,128)(2,1)S(1)}, bf16[24,3200]{1,0:T(8,128)(2,1)S(1)}, u32[]{:S(2)}, u32[]{:S(2)}) %collective-permute-start.1) | collective-permute-done | bytes 153632 | tf_op jit(solution)/shard_map/ppermute | solution.py:845
  32.5 1.6 collective-permute-start.3
  34.1 1.6 collective-permute-start.6
  35.7 5.5 %collective-permute-done.3 = bf16[4,24,1536]{2,1,0:T(8,128)(2,1)S(1)} collective-permute-done((bf16[4,24,1536]{2,1,0:T(8,128)(2,1)S(1)}, bf16[4,24,1536]{2,1,0:T(8,128)(2,1)S(1)}, u32[]{:S(2)}, u32[]{:S(2)}) %collective-permute-start.3) | collective-permute-done | bytes 294944 | tf_op jit(solution)/shard_map/ppermute | solution.py:845
  41.4 1.5 collective-permute-start.4
  42.9 1.8 collective-permute-done.6
  45.7 14.6 %collective-permute-done.4 = bf16[4,2,24,1536]{3,2,0,1:T(8,128)(2,1)S(1)} collective-permute-done((bf16[4,2,24,1536]{3,2,0,1:T(8,128)(2,1)S(1)}, bf16[4,2,24,1536]{3,2,0,1:T(8,128)(2,1)S(1)}, u32[]{:S(2)}, u32[]{:S(2)}) %collective-permute-start.4) | collective-permute-done | bytes 589856 | tf_op jit(solution)/shard_map/ppermute | solution.py:845
  62.0 2.0 collective-permute-done.8.refs_6_
  64.0 0.9 slice_bitcast_fusion
  65.4 0.9 reshape.178.refs_7_.refs_6_.refs_8_
  66.3 31.9 %attention_forward.1 = (bf16[2048,2304]{1,0:T(8,128)(2,1)}, f32[2048,1536]{1,0:T(8,128)}, bf16[2048,768]{1,0:T(8,128)(2,1)}, f32[2048,768]{1,0:T(8,128)}, f32[20...) custom-call(s32[1]{0:T(128)} %bitcast.refs_0_, s32[16]{0:T(128)} %refs_1_.6, ...), custom_call_target="tpu_custom_call" | custom-call | flops 14495514624 | bytes 48467968 | tf_op jit(solution)/shard_map/attention_forward/pallas_call | solution.py:120
  98.2 9.0 %all-gather.2.cloned.1.call-done.refs_4_.refs_5_.refs_6_.refs_7_ = bf16[768,6144]{1,0:T(8,128)(2,1)} async-done(((bf16[24,6144]{1,0:T(8,128)(2,1)}), bf16[768,6144]{1,0:T(8,128)(2,1)}) %all-gather.2.cloned.1.call-update) | async-done | bytes 9437200 | tf_op jit(solution)/shard_map/all_gather | solution.py:899
  107.3 49.6 %mlp_forward.1 = (bf16[2048,768]{1,0:T(8,128)(2,1)}, f32[2048,3072]{1,0:T(8,128)}, f32[2048,768]{1,0:T(8,128)}, f32[3,768]{1,0:T(4,128)}, bf16[2,192,3072]{2,1,0:T(8,128)(2,1)}, /*index=5*/bf16[2,192,3072]{2,1,0:T(8,128)(2,1)}) custom-call(s32[1]{0:T(128)} %bitcast.refs_0_, s32[16]{0:T(128)} %refs_1_.6, f32[2048,768]{1,0:T(8,128)} %get-tuple-element.83.refs_2_.refs_3_, ...), custom_call_target="tpu_custom_call" | custom-call | flops 28991029248 | bytes 67679232 | tf_op jit(solution)/shard_map/mlp_forward/pallas_call | solution.py:120
  157.1 4.5 %collective-permute-done.9 = bf16[2,192,3072]{2,1,0:T(8,128)(2,1)S(1)} collective-permute-done((bf16[2,192,3072]{2,1,0:T(8,128)(2,1)}, bf16[2,192,3072]{2,1,0:T(8,128)(2,1)S(1)}, u32[]{:S(2)}, u32[]{:S(2)}) %collective-permute-start.9) | collective-permute-done | bytes 2359328 | tf_op jit(solution)/shard_map/ppermute | solution.py:945
  161.6 4.0 %add_convert_fusion.1.refs_9_ = bf16[2,192,3072]{2,1,0:T(8,128)(2,1)} fusion(bf16[2,192,3072]{2,1,0:T(8,128)(2,1)S(1)} %collective-permute-done.9, bf16[2,192,3072]{2,1,0:T(8,128)(2,1)} %get-tuple-element.89), kind=kLoop, calls=%fused_computation.1 | loop fusion | flops 4718592 | bytes 7077888 | tf_op jit(solution)/shard_map/convert_element_type | solution.py:749
  165.6 4.6 %all-to-all-start = ((bf16[16,24,3072]{2,1,0:T(8,128)(2,1)}), bf16[16,24,3072]{2,1,0:T(8,128)(2,1)}, u32[]{:S(2)}, u32[]{:S(2)}) async-start(bf16[16,24,3072]{2,1,0:T(8,128)(2,1)} %bitcast.24), calls=%async_computation | async-start | bytes 4718592 | tf_op jit(solution)/shard_map/all_to_all | solution.py:949
  170.3 43.8 %mlp_backward.1 = (f32[2048,768]{1,0:T(8,128)}, bf16[2048,768]{1,0:T(8,128)(2,1)}, f32[3,768]{1,0:T(4,128)}, f32[1,3072]{1,0:T(1,128)}, bf16[2,192,3072]{2,1,0:T(8,128)(2,1)}, /*index=5*/bf16[2,192,3072]{2,1,0:T(8,128)(2,1)}) custom-call(s32[1]{0:T(128)} %bitcast.refs_0_, f32[2048,768]{1,0:T(8,128)} %get-tuple-element.85.refs_1_, ...), custom_call_target="tpu_custom_call" | custom-call | flops 28991029248 | bytes 75031552 | tf_op jit(solution)/shard_map/mlp_backward/pallas_call | solution.py:120
  214.5 7.0 %weight_grad.1 = (bf16[2,192,768]{2,1,0:T(8,128)(2,1)}, bf16[2,192,768]{2,1,0:T(8,128)(2,1)}) custom-call(s32[1]{0:T(128)} %bitcast.refs_0_, bf16[2048,768]{1,0:T(8,128)(2,1)} %get-tuple-element.91.refs_1_.refs_0_, bf16[2048,768]{1,0:T(8,128)(2,1)} %get-tuple-element.96.refs_2_, bf16[2,192,3072]{2,1,0:T(8,128)(2,1)} %get-tuple-element.99.refs_3_), custom_call_target="tpu_custom_call" | custom-call | flops 2415919104 | bytes 7471104 | tf_op jit(solution)/shard_map/weight_grad/pallas_call | solution.py:120
  221.5 4.0 %add_convert_fusion.refs_6_ = bf16[2,192,3072]{2,1,0:T(8,128)(2,1)} fusion(bf16[2,192,3072]{2,1,0:T(8,128)(2,1)} %collective-permute-done.10, bf16[2,192,3072]{2,1,0:T(8,128)(2,1)S(1)} %copy-done.1), kind=kLoop, calls=%fused_computation | loop fusion | flops 4718592 | bytes 7077888 | tf_op jit(solution)/shard_map/convert_element_type | solution.py:749
  225.5 6.6 %all-to-all-start.2 = ((bf16[16,24,3072]{2,1,0:T(8,128)(2,1)}), bf16[16,24,3072]{2,1,0:T(8,128)(2,1)S(1)}, u32[]{:S(2)}, u32[]{:S(2)}) async-start(bf16[16,24,3072]{2,1,0:T(8,128)(2,1)} %bitcast.33), calls=%async_computation.2 | async-start | bytes 4718592 | tf_op jit(solution)/shard_map/all_to_all | solution.py:949
  232.1 27.5 %attention_backward.1 = (bf16[2048,2304]{1,0:T(8,128)(2,1)}, f32[2,768]{1,0:T(2,128)}, f32[24,3072]{1,0:T(8,128)}) custom-call(bf16[2048,768]{1,0:T(8,128)(2,1)} %get-tuple-element.91.refs_1_.refs_0_, bf16[2048,2304]{1,0:T(8,128)(2,1)} %get-tuple-element.92.refs_1_, f32[2048,1536]{1,0:T(8,128)} %get-tuple-element.93.refs_2_, ...), custom_call_target="tpu_custom_call" | custom-call | flops 19327352832 | bytes 38443008 | tf_op jit(solution)/shard_map/attention_backward/pallas_call | solution.py:120
  261.6 13.2 %qkv_grad.1 = (bf16[2,192,1664]{2,1,0:T(8,128)(2,1)}, bf16[2,192,1664]{2,1,0:T(8,128)(2,1)}, bf16[2,192,768]{2,1,0:T(8,128)(2,1)}, bf16[2,192,768]{2,1,0:T(8,128)(2,1)}) custom-call(s32[1]{0:T(128)} %bitcast.refs_0_, bf16[2048,768]{1,0:T(8,128)(2,1)} %refs_1_.7, bf16[2048,2304]{1,0:T(8,128)(2,1)} %get-tuple-element.101.refs_2_.refs_0_, ...), custom_call_target="tpu_custom_call" | custom-call | flops 7247757312 | bytes 16711680 | tf_op jit(solution)/shard_map/qkv_grad/pallas_call | solution.py:120
  275.5 3.3 collective-permute-done.13
  280.5 4.1 %plane_split.1 = (bf16[2,192,1664]{2,1,0:T(8,128)(2,1)}, f32[96,1536]{1,0:T(8,128)}, bf16[96,1536]{1,0:T(8,128)(2,1)}, bf16[96,1536]{1,0:T(8,128)(2,1)}, bf16[96,1536]{1,0:T(8,128)(2,1)}) custom-call(s32[1]{0:T(128)} %bitcast.25.refs_0_, bf16[2,192,1664]{2,1,0:T(8,128)(2,1)} %get-tuple-element.108.refs_1_, ...), custom_call_target="tpu_custom_call" | custom-call | bytes 7667712 | tf_op jit(solution)/shard_map/plane_split/pallas_call | solution.py:120
  284.9 6.7 %all-to-all-start.1 = ((bf16[16,24,1664]{2,1,0:T(8,128)(2,1)}), bf16[16,24,1664]{2,1,0:T(8,128)(2,1)}, u32[]{:S(2)}, u32[]{:S(2)}) async-start(bf16[16,24,1664]{2,1,0:T(8,128)(2,1)} %bitcast.59), calls=%async_computation.1 | async-start | bytes 2555904 | tf_op jit(solution)/shard_map/all_to_all | solution.py:949
  291.7 1.9 collective-permute-start.14
  293.6 1.5 collective-permute-start.15
  295.2 13.4 %grad_tokens.1.refs_5_.refs_1_ = bf16[2048,768]{1,0:T(8,128)(2,1)} custom-call(bf16[2048,2304]{1,0:T(8,128)(2,1)} %get-tuple-element.101.refs_2_.refs_0_, f32[2048,768]{1,0:T(8,128)} %get-tuple-element.102.refs_1_, bf16[768,2304]{1,0:T(8,128)(2,1)} %get-tuple-element.103.refs_2_, bf16[2,192,1664]{2,1,0:T(8,128)(2,1)} %get-tuple-element.113.refs_3_, ...), custom_call_target="tpu_custom_call" | custom-call | flops 7247757312 | bytes 22413312 | tf_op jit(solution)/shard_map/grad_tokens/pallas_call | solution.py:120
  308.9 2.9 collective-permute-done.15.refs_3_
  311.9 11.6 %collective-permute-done.16.refs_4_ = bf16[96,1536]{1,0:T(8,128)(2,1)S(1)} collective-permute-done((bf16[96,1536]{1,0:T(8,128)(2,1)S(1)}, bf16[96,1536]{1,0:T(8,128)(2,1)S(1)}, u32[]{:S(2)}, u32[]{:S(2)}) %collective-permute-start.16) | collective-permute-done | bytes 294944 | tf_op jit(solution)/shard_map/ppermute | solution.py:743
  324.2 2.2 line_split.1
  326.7 3.2 collective-permute-start.18
  329.9 0.9 collective-permute-start.19
  330.8 2.7 fold_pieces.1.refs_5_.refs_3_
  333.5 1.6 collective-permute-done.18.refs_3_
  335.1 1.3 collective-permute-done.19.refs_4_
  337.0 2.7 fold_with_squares.1
  339.7 1.0 slice.44
  340.7 0.9 slice.45
  341.6 2.5 all-to-all-start.3
  344.8 6.3 %all-to-all-done.3 = f32[32,1,128]{2,1,0:T(1,128)S(1)} async-done(((f32[32,1,128]{2,1,0:T(1,128)}), f32[32,1,128]{2,1,0:T(1,128)S(1)}, u32[]{:S(2)}, u32[]{:S(2)}) %all-to-all-start.3) | async-done | bytes 16416 | tf_op jit(solution)/shard_map/all_to_all | solution.py:1015
  351.8 4.3 %update_weights.1 = (f32[24,2304]{1,0:T(8,128)}, f32[24,2304]{1,0:T(8,128)}, f32[24,2304]{1,0:T(8,128)}, bf16[24,2304]{1,0:T(8,128)(2,1)}, f32[24,768]{1,0:T(8,1...) custom-call(f32[32,128]{1,0:T(8,128)} %bitcast.73, ...), custom_call_target="tpu_custom_call" | custom-call | bytes 6726144 | tf_op jit(solution)/shard_map/update_weights/pallas_call | solution.py:120
  (110 shorter events, 14.8 us)
Async XLA Ops:
  7.2 100.1 %all-gather.2.cloned.1.call-start = ((), (), s32[]{:S(2)}) async-start(), calls=%async_computation.4 | async-start | bytes 9732096 | tf_op jit(solution)/shard_map/all_gather | solution.py:899
  11.7 9.3 %collective-permute-start = (bf16[24,3200]{1,0:T(8,128)(2,1)S(1)}, bf16[24,3200]{1,0:T(8,128)(2,1)S(1)}, u32[]{:S(2)}, u32[]{:S(2)}) collective-permute-start(bf16[24,3200]{1,0:T(8,128)(2,1)S(1)} %fusion.6), channel_id=1, source_target_pairs={{0,2},{2,0},{4,6},{6,4},{1,3},{3,1},{5,7},{7,5},{8,10},{10,8},{12,... | collective-permute-start | bytes 460808 | tf_op jit(solution)/shard_map/ppermute | solution.py:845
  14.8 17.3 %collective-permute-start.1 = (bf16[24,3200]{1,0:T(8,128)(2,1)S(1)}, bf16[24,3200]{1,0:T(8,128)(2,1)S(1)}, u32[]{:S(2)}, u32[]{:S(2)}) collective-permute-start(bf16[24,3200]{1,0:T(8,128)(2,1)S(1)} %fusion.6), channel_id=1, source_target_pairs={{0,4},{2,6},{4,0},{6,2},{1,5},{3,7},{5,1},{7,3},{8,12},{10,14},{12... | collective-permute-start | bytes 460808 | tf_op jit(solution)/shard_map/ppermute | solution.py:845
  17.4 14.7 %collective-permute-start.2 = (bf16[24,3200]{1,0:T(8,128)(2,1)S(1)}, bf16[24,3200]{1,0:T(8,128)(2,1)S(1)}, u32[]{:S(2)}, u32[]{:S(2)}) collective-permute-start(bf16[24,3200]{1,0:T(8,128)(2,1)S(1)} %fusion.6), channel_id=1, source_target_pairs={{0,6},{2,4},{4,2},{6,0},{1,7},{3,5},{5,3},{7,1},{8,14},{10,12},{12... | collective-permute-start | bytes 460808 | tf_op jit(solution)/shard_map/ppermute | solution.py:845
  32.5 8.7 %collective-permute-start.3 = (bf16[4,24,1536]{2,1,0:T(8,128)(2,1)S(1)}, bf16[4,24,1536]{2,1,0:T(8,128)(2,1)S(1)}, u32[]{:S(2)}, u32[]{:S(2)}) collective-permute-start(bf16[4,24,1536]{2,1,0:T(8,128)(2,1)S(1)} %get-tuple-element.150), channel_id=1, source_target_pairs={{0,1},{1,0},{2,3},{3,2},{4,5},{5,4},{6,7},{7,6},{8,9},{9,8},{10,11... | collective-permute-start | bytes 884744 | tf_op jit(solution)/shard_map/ppermute | solution.py:845
  34.1 10.5 %collective-permute-start.6 = (bf16[4,24,1664]{2,1,0:T(8,128)(2,1)S(1)}, bf16[4,24,1664]{2,1,0:T(8,128)(2,1)S(1)}, u32[]{:S(2)}, u32[]{:S(2)}) collective-permute-start(bf16[4,24,1664]{2,1,0:T(8,128)(2,1)S(1)} %get-tuple-element.148), channel_id=1, source_target_pairs={{0,16},{16,0},{1,17},{17,1},{2,18},{18,2},{3,19},{19,3},{4,20},{20... | collective-permute-start | bytes 958472 | tf_op jit(solution)/shard_map/ppermute | solution.py:845
  41.4 18.9 %collective-permute-start.4 = (bf16[4,2,24,1536]{3,2,0,1:T(8,128)(2,1)S(1)}, bf16[4,2,24,1536]{3,2,0,1:T(8,128)(2,1)S(1)}, u32[]{:S(2)}, u32[]{:S(2)}) collective-permute-start(bf16[4,2,24,1536]{3,2,0,1:T(8,128)(2,1)S(1)} %get-tuple-element.152), channel_id=1, source_target_pairs={{0,16},{16,0},{1,17},{17,1},{2,18},{18,2},{3,19},{19,3},{4,20},{20... | collective-permute-start | bytes 1769480 | tf_op jit(solution)/shard_map/ppermute | solution.py:845
  44.8 15.6 %collective-permute-start.7 = (bf16[2,4,24,1664]{3,2,1,0:T(8,128)(2,1)S(1)}, bf16[2,4,24,1664]{3,2,1,0:T(8,128)(2,1)S(1)}, u32[]{:S(2)}, u32[]{:S(2)}) collective-permute-start(bf16[2,4,24,1664]{3,2,1,0:T(8,128)(2,1)S(1)} %reverse_select_fusion.2), channel_id=1, source_target_pairs={{0,1},{1,0},{2,3},{3,2},{4,5},{5,4},{6,7},{7,6},{8,9},{9,8},{10,11... | collective-permute-start | bytes 1916936 | tf_op jit(solution)/shard_map/ppermute | solution.py:845
  60.8 1.0 copy-start.2
  60.8 3.2 collective-permute-start.8
  61.2 5.1 %copy-start.3 = (bf16[2,4,2,24,1536]{4,3,2,1,0:T(8,128)(2,1)}, bf16[2,4,2,24,1536]{4,3,2,1,0:T(8,128)(2,1)S(1)}, u32[]{:S(2)}) copy-start(bf16[2,4,2,24,1536]{4,3,2,1,0:T(8,128)(2,1)S(1)} %copy.47) | copy-start | bytes 3538948
  61.2 5.1 %collective-permute-start.5 = (bf16[2,192,1536]{2,1,0:T(8,128)(2,1)S(1)}, bf16[2,192,1536]{2,1,0:T(8,128)(2,1)}, u32[]{:S(2)}, u32[]{:S(2)}) collective-permute-start(bf16[2,192,1536]{2,1,0:T(8,128)(2,1)S(1)} %bitcast.60), channel_id=1, source_target_pairs={{0,8},{8,0},{1,9},{9,1},{2,10},{10,2},{3,11},{11,3},{4,12},{12,4},... | collective-permute-start | bytes 3538952 | tf_op jit(solution)/shard_map/ppermute | solution.py:920
  156.9 4.7 %collective-permute-start.9 = (bf16[2,192,3072]{2,1,0:T(8,128)(2,1)}, bf16[2,192,3072]{2,1,0:T(8,128)(2,1)S(1)}, u32[]{:S(2)}, u32[]{:S(2)}) collective-permute-start(bf16[2,192,3072]{2,1,0:T(8,128)(2,1)} %get-tuple-element.90), channel_id=1, source_target_pairs={{0,8},{8,0},{1,9},{9,1},{2,10},{10,2},{3,11},{11,3},{4,12},{12,4},... | collective-permute-start | bytes 7077896 | tf_op jit(solution)/shard_map/ppermute | solution.py:945
  165.6 59.9 %all-to-all-start = ((bf16[16,24,3072]{2,1,0:T(8,128)(2,1)}), bf16[16,24,3072]{2,1,0:T(8,128)(2,1)}, u32[]{:S(2)}, u32[]{:S(2)}) async-start(bf16[16,24,3072]{2,1,0:T(8,128)(2,1)} %bitcast.24), calls=%async_computation | async-start | bytes 4718592 | tf_op jit(solution)/shard_map/all_to_all | solution.py:949
  170.3 44.1 %copy-start.15 = (f32[3,768]{1,0:T(4,128)S(1)}, f32[3,768]{1,0:T(4,128)}, u32[]{:S(2)}) copy-start(f32[3,768]{1,0:T(4,128)} %get-tuple-element.107) | copy-start | bytes 27652
  214.1 7.4 %collective-permute-start.10 = (bf16[2,192,3072]{2,1,0:T(8,128)(2,1)}, bf16[2,192,3072]{2,1,0:T(8,128)(2,1)}, u32[]{:S(2)}, u32[]{:S(2)}) collective-permute-start(bf16[2,192,3072]{2,1,0:T(8,128)(2,1)} %get-tuple-element.100), channel_id=1, source_target_pairs={{0,8},{8,0},{1,9},{9,1},{2,10},{10,2},{3,11},{11,3},{4,12},{12,4},... | collective-permute-start | bytes 7077896 | tf_op jit(solution)/shard_map/ppermute | solution.py:945
  214.4 7.0 %copy-start.16 = (f32[3,768]{1,0:T(4,128)S(1)}, f32[3,768]{1,0:T(4,128)}, u32[]{:S(2)}) copy-start(f32[3,768]{1,0:T(4,128)} %get-tuple-element.105) | copy-start | bytes 27652
  214.4 7.1 %copy-start.1 = (bf16[2,192,3072]{2,1,0:T(8,128)(2,1)S(1)}, bf16[2,192,3072]{2,1,0:T(8,128)(2,1)}, u32[]{:S(2)}) copy-start(bf16[2,192,3072]{2,1,0:T(8,128)(2,1)} %get-tuple-element.99.refs_3_) | copy-start | bytes 7077892
  225.5 59.4 %all-to-all-start.2 = ((bf16[16,24,3072]{2,1,0:T(8,128)(2,1)}), bf16[16,24,3072]{2,1,0:T(8,128)(2,1)S(1)}, u32[]{:S(2)}, u32[]{:S(2)}) async-start(bf16[16,24,3072]{2,1,0:T(8,128)(2,1)} %bitcast.33), calls=%async_computation.2 | async-start | bytes 4718592 | tf_op jit(solution)/shard_map/all_to_all | solution.py:949
  232.1 28.3 %copy-start.13 = (f32[1,3072]{1,0:T(1,128)S(1)}, f32[1,3072]{1,0:T(1,128)}, u32[]{:S(2)}) copy-start(f32[1,3072]{1,0:T(1,128)} %get-tuple-element.106) | copy-start | bytes 36868
  274.8 4.9 %collective-permute-start.11 = (bf16[2,192,1664]{2,1,0:T(8,128)(2,1)}, bf16[2,192,1664]{2,1,0:T(8,128)(2,1)}, u32[]{:S(2)}, u32[]{:S(2)}) collective-permute-start(bf16[2,192,1664]{2,1,0:T(8,128)(2,1)} %get-tuple-element.109), channel_id=1, source_target_pairs={{0,8},{8,0},{1,9},{9,1},{2,10},{10,2},{3,11},{11,3},{4,12},{12,4},... | collective-permute-start | bytes 3833864 | tf_op jit(solution)/shard_map/ppermute | solution.py:945
  275.0 3.9 %collective-permute-start.13 = (bf16[2,192,768]{2,1,0:T(8,128)(2,1)}, bf16[2,192,768]{2,1,0:T(8,128)(2,1)S(1)}, u32[]{:S(2)}, u32[]{:S(2)}) collective-permute-start(bf16[2,192,768]{2,1,0:T(8,128)(2,1)} %get-tuple-element.112), channel_id=1, source_target_pairs={{0,8},{8,0},{1,9},{9,1},{2,10},{10,2},{3,11},{11,3},{4,12},{12,4},... | collective-permute-start | bytes 1769480 | tf_op jit(solution)/shard_map/ppermute | solution.py:945
  275.3 4.4 %collective-permute-start.12 = (bf16[2,192,768]{2,1,0:T(8,128)(2,1)}, bf16[2,192,768]{2,1,0:T(8,128)(2,1)S(1)}, u32[]{:S(2)}, u32[]{:S(2)}) collective-permute-start(bf16[2,192,768]{2,1,0:T(8,128)(2,1)} %get-tuple-element.111), channel_id=1, source_target_pairs={{0,8},{8,0},{1,9},{9,1},{2,10},{10,2},{3,11},{11,3},{4,12},{12,4},... | collective-permute-start | bytes 1769480 | tf_op jit(solution)/shard_map/ppermute | solution.py:945
  278.8 0.9 copy-start.4
  279.7 0.8 copy-start.5
  284.7 8.9 %copy-start.20 = (bf16[96,1536]{1,0:T(8,128)(2,1)S(1)}, bf16[96,1536]{1,0:T(8,128)(2,1)}, u32[]{:S(2)}) copy-start(bf16[96,1536]{1,0:T(8,128)(2,1)} %get-tuple-element.116) | copy-start | bytes 884740
  284.7 10.4 %copy-start.19 = (bf16[96,1536]{1,0:T(8,128)(2,1)S(1)}, bf16[96,1536]{1,0:T(8,128)(2,1)}, u32[]{:S(2)}) copy-start(bf16[96,1536]{1,0:T(8,128)(2,1)} %get-tuple-element.117) | copy-start | bytes 884740
  284.9 23.7 %copy-start = (bf16[16,24,3072]{2,1,0:T(8,128)(2,1)}, bf16[16,24,3072]{2,1,0:T(8,128)(2,1)S(1)}, u32[]{:S(2)}) copy-start(bf16[16,24,3072]{2,1,0:T(8,128)(2,1)S(1)} %all-to-all-done.2.refs_0_) | copy-start | bytes 7077892
  284.9 51.5 %all-to-all-start.1 = ((bf16[16,24,1664]{2,1,0:T(8,128)(2,1)}), bf16[16,24,1664]{2,1,0:T(8,128)(2,1)}, u32[]{:S(2)}, u32[]{:S(2)}) async-start(bf16[16,24,1664]{2,1,0:T(8,128)(2,1)} %bitcast.59), calls=%async_computation.1 | async-start | bytes 2555904 | tf_op jit(solution)/shard_map/all_to_all | solution.py:949
  291.7 17.3 %collective-permute-start.14 = (bf16[96,1536]{1,0:T(8,128)(2,1)}, bf16[96,1536]{1,0:T(8,128)(2,1)S(1)}, u32[]{:S(2)}, u32[]{:S(2)}) collective-permute-start(bf16[96,1536]{1,0:T(8,128)(2,1)} %get-tuple-element.115), channel_id=1, source_target_pairs={{0,1},{1,0},{16,17},{17,16},{2,3},{3,2},{18,19},{19,18},{4,5},{5,4... | collective-permute-start | bytes 884744 | tf_op jit(solution)/shard_map/ppermute | solution.py:743
  293.6 18.3 %collective-permute-start.15 = (bf16[96,1536]{1,0:T(8,128)(2,1)S(1)}, bf16[96,1536]{1,0:T(8,128)(2,1)S(1)}, u32[]{:S(2)}, u32[]{:S(2)}) collective-permute-start(bf16[96,1536]{1,0:T(8,128)(2,1)S(1)} %copy-done.20), channel_id=1, source_target_pairs={{0,16},{1,17},{16,0},{17,1},{2,18},{3,19},{18,2},{19,3},{4,20},{5,... | collective-permute-start | bytes 884744 | tf_op jit(solution)/shard_map/ppermute | solution.py:743
  295.0 28.4 %collective-permute-start.16 = (bf16[96,1536]{1,0:T(8,128)(2,1)S(1)}, bf16[96,1536]{1,0:T(8,128)(2,1)S(1)}, u32[]{:S(2)}, u32[]{:S(2)}) collective-permute-start(bf16[96,1536]{1,0:T(8,128)(2,1)S(1)} %copy-done.19), channel_id=1, source_target_pairs={{0,17},{1,16},{16,1},{17,0},{2,19},{3,18},{18,3},{19,2},{4,21},{5,... | collective-permute-start | bytes 884744 | tf_op jit(solution)/shard_map/ppermute | solution.py:743
  308.9 14.5 %copy-start.6 = (bf16[96,1536]{1,0:T(8,128)(2,1)}, bf16[96,1536]{1,0:T(8,128)(2,1)S(1)}, u32[]{:S(2)}) copy-start(bf16[96,1536]{1,0:T(8,128)(2,1)S(1)} %collective-permute-done.14.refs_2_) | copy-start | bytes 884740
  311.9 11.6 %copy-start.7 = (bf16[96,1536]{1,0:T(8,128)(2,1)}, bf16[96,1536]{1,0:T(8,128)(2,1)S(1)}, u32[]{:S(2)}) copy-start(bf16[96,1536]{1,0:T(8,128)(2,1)S(1)} %collective-permute-done.15.refs_3_) | copy-start | bytes 884740
  323.4 0.7 copy-start.8
  326.4 7.1 %collective-permute-start.17 = (bf16[24,1536]{1,0:T(8,128)(2,1)}, bf16[24,1536]{1,0:T(8,128)(2,1)S(1)}, u32[]{:S(2)}, u32[]{:S(2)}) collective-permute-start(bf16[24,1536]{1,0:T(8,128)(2,1)} %get-tuple-element.119), channel_id=1, source_target_pairs={{0,2},{2,0},{4,6},{6,4},{1,3},{3,1},{5,7},{7,5},{8,10},{10,8},{12,... | collective-permute-start | bytes 221192 | tf_op jit(solution)/shard_map/ppermute | solution.py:743
  326.7 8.3 %collective-permute-start.18 = (bf16[24,1536]{1,0:T(8,128)(2,1)}, bf16[24,1536]{1,0:T(8,128)(2,1)S(1)}, u32[]{:S(2)}, u32[]{:S(2)}) collective-permute-start(bf16[24,1536]{1,0:T(8,128)(2,1)} %get-tuple-element.120), channel_id=1, source_target_pairs={{0,4},{2,6},{4,0},{6,2},{1,5},{3,7},{5,1},{7,3},{8,12},{10,14},{12... | collective-permute-start | bytes 221192 | tf_op jit(solution)/shard_map/ppermute | solution.py:743
  329.9 6.5 %collective-permute-start.19 = (bf16[24,1536]{1,0:T(8,128)(2,1)}, bf16[24,1536]{1,0:T(8,128)(2,1)S(1)}, u32[]{:S(2)}, u32[]{:S(2)}) collective-permute-start(bf16[24,1536]{1,0:T(8,128)(2,1)} %get-tuple-element.121), channel_id=1, source_target_pairs={{0,6},{2,4},{4,2},{6,0},{1,7},{3,5},{5,3},{7,1},{8,14},{10,12},{12... | collective-permute-start | bytes 221192 | tf_op jit(solution)/shard_map/ppermute | solution.py:743
  333.5 2.9 copy-start.9
  335.1 1.3 copy-start.10
  336.4 0.6 copy-start.11
  339.7 17.8 %copy-start.14 = (f32[288]{0:T(512)S(1)}, f32[288]{0:T(512)}, u32[]{:S(2)}) copy-start(f32[288]{0:T(512)} %param.25) | copy-start | bytes 3460
  339.7 17.8 %copy-start.17 = (f32[288]{0:T(512)S(1)}, f32[288]{0:T(512)}, u32[]{:S(2)}) copy-start(f32[288]{0:T(512)} %param.34) | copy-start | bytes 3460
  339.7 17.8 %copy-start.18 = (f32[288]{0:T(512)S(1)}, f32[288]{0:T(512)}, u32[]{:S(2)}) copy-start(f32[288]{0:T(512)} %param.35) | copy-start | bytes 3460
  341.6 9.6 %all-to-all-start.3 = ((f32[32,1,128]{2,1,0:T(1,128)}), f32[32,1,128]{2,1,0:T(1,128)S(1)}, u32[]{:S(2)}, u32[]{:S(2)}) async-start(f32[32,1,128]{2,1,0:T(1,128)} %bitcast.74), calls=%async_computation.3 | async-start | bytes 32768 | tf_op jit(solution)/shard_map/all_to_all | solution.py:1015
  351.2 0.6 copy-start.12
Sparse Core Ops, SparseCore 0:
  11.5 95.7 all-gather.1

commit v5 on v4

--- a/solution.py
+++ b/solution.py
@@ -522,7 +522,7 @@
         sums_out[...] = jnp.sum(sums[...], axis=1)
 
 
-def attention_backward(first_low, joined, probs, w_out, pieces, after=(), block=256):
+def attention_backward(first_low, joined, probs, w_out, pieces, after=(), block=512):
     rows, width = first_low.shape
     steps = rows // block
     count, own_rows, columns = pieces.shape
@@ -812,11 +812,10 @@
     grad_norm = jnp.sqrt(jnp.sum(squares[:, :1], axis=0, keepdims=True))
     factor = CLIP_LIMIT / jnp.maximum(grad_norm, CLIP_LIMIT)
     norm_out[...] = jnp.broadcast_to(grad_norm, norm_out.shape)
-    for index, (source, low, high) in enumerate(places):
+    for index, parts in enumerate(places):
         weight, first, second = (ref[...] for ref in states[3 * index : 3 * index + 3])
-        fresh = adam_update(
-            weight, first, second, totals[source][:, low:high] * factor, RATE_MATRIX, DECAY
-        )
+        grad = jnp.concatenate([totals[source][:, low:high] for source, low, high in parts], axis=1)
+        fresh = adam_update(weight, first, second, grad * factor, RATE_MATRIX, DECAY)
         for target, value in zip(results[4 * index : 4 * index + 4], fresh):
             target[...] = value
 
@@ -1008,15 +1007,18 @@
     sum_front, *sum_last, spread = fold_with_squares(
         peer_sum(front), last, [sum_up, sum_down], device_count
     )
-    cut = 2 * width + LANES
     if order is None:
-        sum_last = [sum_front[:, cut:]]
-    sum_qkv = jnp.concatenate([sum_front[:, : 2 * width], sum_last[0][:, :width]], axis=1)
+        sum_last = [sum_front[:, 2 * width + LANES :]]
     squares = lax.all_to_all(spread, ALL, 0, 0, tiled=True)
     *updated, norm_row = update_weights(
         squares,
-        [sum_qkv, sum_last[0], sum_up, sum_down],
-        ((0, 0, 3 * width), (1, width, 2 * width), (2, 0, hidden), (3, 0, hidden)),
+        [sum_front, sum_last[0], sum_up, sum_down],
+        (
+            ((0, 0, 2 * width), (1, 0, width)),
+            ((1, width, 2 * width),),
+            ((2, 0, hidden),),
+            ((3, 0, hidden),),
+        ),
         [
             *(w_qkv, first_qkv, second_qkv),
             *(w_out, first_out, second_out),

time: 366 us -> 363 us (level)
  blocking collectives: 0 us -> 10.4 us
  waiting for transfers between devices: 80.7 us -> 75.4 us
    all_to_all x0 -> x1, blocking collectives: none -> 10.4 us  [body(): squares = lax.all_to_all(spread, ALL, 0, 0, tiled=True)]
    all_to_all x1 -> x0, waiting for transfers between devices: 6.35 us -> none  [body(): squares = lax.all_to_all(spread, ALL, 0, 0, tiled=True)]
  transfers between devices with their start and end apart: 25 -> 24, of which waited for: 17 -> 16; matrix products, arithmetic and copies ran while one was open for 4% -> 4% of each run, Pallas kernels for 40% -> 40%
where the time goes in v5:
time: 363 us; the launch traced here: 362 us
  Pallas kernels  203 us (56%)
  waiting for transfers between devices  75.4 us (21%)
  starting transfers between devices  38.1 us (10%)
  between operations  15.2 us (4%)
  other arithmetic  13.4 us (4%)
  blocking collectives  10.4 us (3%)
  local copies, waits for them, and re-layouts  7.01 us (2%)
    pallas_call x13, Pallas kernels, call_kernel(): pl.pallas_call(wrapped, grid_spec=pltpu.PrefetchScalarGridSpec(num_scalar...  203 us
    ppermute x7, waiting for transfers between devices, gather_axis(): lax.ppermute(value, axis, [(place, place ^ step) for place in range(size)])  36.6 us
    ppermute x6, waiting for transfers between devices, trade(): lax.ppermute(parts[step], axis, [(place, place ^ step) for place in range...  17.6 us
    all_to_all x3, starting transfers between devices, peer_sum(): pieces = lax.all_to_all(both.reshape(-1, columns), PEERS, 0, 0, tiled=True)  17.3 us
    ppermute x7, starting transfers between devices, gather_axis(): lax.ppermute(value, axis, [(place, place ^ step) for place in range(size)])  11.1 us
    all_to_all x1, blocking collectives, body(): squares = lax.all_to_all(spread, ALL, 0, 0, tiled=True)  10.4 us
    all_gather x1, waiting for transfers between devices, body(): packed = lax.all_gather(back, ALL, axis=0, tiled=True)  9.04 us
    ppermute x5, waiting for transfers between devices, swap_cores(): return (keep, lax.ppermute(send, 'core', swap))  8.77 us
  transfers between devices with their start and end apart: 24, of which 16 were waited for; matrix products, arithmetic and copies ran while one was open for 4% of the time, Pallas kernels for 40%

profile of v5, /device:TPU:0, one launch (start us, length us, event | category | flops | bytes accessed | tf_op | source)
XLA Modules:
  0.0 362.4 jit_solution(9431986258310404411)
XLA Ops:
  7.2 1.8 pack_rows.1
  9.1 1.0 convert_element_type.39
  10.0 0.9 convert_element_type.41
  11.7 3.1 collective-permute-start
  14.8 2.6 collective-permute-start.1
  17.4 3.5 collective-permute-done
  21.0 11.1 %collective-permute-done.1 = bf16[24,3200]{1,0:T(8,128)(2,1)S(1)} collective-permute-done((bf16[24,3200]{1,0:T(8,128)(2,1)S(1)}, bf16[24,3200]{1,0:T(8,128)(2,1)S(1)}, u32[]{:S(2)}, u32[]{:S(2)}) %collective-permute-start.1) | collective-permute-done | bytes 153632 | tf_op jit(solution)/shard_map/ppermute | solution.py:844
  32.5 1.6 collective-permute-start.3
  34.1 1.6 collective-permute-start.6
  35.7 5.5 %collective-permute-done.3 = bf16[4,24,1536]{2,1,0:T(8,128)(2,1)S(1)} collective-permute-done((bf16[4,24,1536]{2,1,0:T(8,128)(2,1)S(1)}, bf16[4,24,1536]{2,1,0:T(8,128)(2,1)S(1)}, u32[]{:S(2)}, u32[]{:S(2)}) %collective-permute-start.3) | collective-permute-done | bytes 294944 | tf_op jit(solution)/shard_map/ppermute | solution.py:844
  41.4 1.5 collective-permute-start.4
  42.9 1.8 collective-permute-done.6
  45.7 14.6 %collective-permute-done.4 = bf16[4,2,24,1536]{3,2,0,1:T(8,128)(2,1)S(1)} collective-permute-done((bf16[4,2,24,1536]{3,2,0,1:T(8,128)(2,1)S(1)}, bf16[4,2,24,1536]{3,2,0,1:T(8,128)(2,1)S(1)}, u32[]{:S(2)}, u32[]{:S(2)}) %collective-permute-start.4) | collective-permute-done | bytes 589856 | tf_op jit(solution)/shard_map/ppermute | solution.py:844
  62.0 2.0 collective-permute-done.8.refs_6_
  64.0 0.9 slice_bitcast_fusion
  65.4 0.9 reshape.178.refs_7_.refs_6_.refs_8_
  66.3 31.9 %attention_forward.1 = (bf16[2048,2304]{1,0:T(8,128)(2,1)}, f32[2048,1536]{1,0:T(8,128)}, bf16[2048,768]{1,0:T(8,128)(2,1)}, f32[2048,768]{1,0:T(8,128)}, f32[20...) custom-call(s32[1]{0:T(128)} %bitcast.refs_0_, s32[16]{0:T(128)} %refs_1_.6, ...), custom_call_target="tpu_custom_call" | custom-call | flops 14495514624 | bytes 48467968 | tf_op jit(solution)/shard_map/attention_forward/pallas_call | solution.py:120
  98.2 9.0 %all-gather.2.cloned.1.call-done.refs_4_.refs_5_.refs_6_.refs_7_ = bf16[768,6144]{1,0:T(8,128)(2,1)} async-done(((bf16[24,6144]{1,0:T(8,128)(2,1)}), bf16[768,6144]{1,0:T(8,128)(2,1)}) %all-gather.2.cloned.1.call-update) | async-done | bytes 9437200 | tf_op jit(solution)/shard_map/all_gather | solution.py:898
  107.3 49.6 %mlp_forward.1 = (bf16[2048,768]{1,0:T(8,128)(2,1)}, f32[2048,3072]{1,0:T(8,128)}, f32[2048,768]{1,0:T(8,128)}, f32[3,768]{1,0:T(4,128)}, bf16[2,192,3072]{2,1,0:T(8,128)(2,1)}, /*index=5*/bf16[2,192,3072]{2,1,0:T(8,128)(2,1)}) custom-call(s32[1]{0:T(128)} %bitcast.refs_0_, s32[16]{0:T(128)} %refs_1_.6, f32[2048,768]{1,0:T(8,128)} %get-tuple-element.83.refs_2_.refs_3_, ...), custom_call_target="tpu_custom_call" | custom-call | flops 28991029248 | bytes 67679232 | tf_op jit(solution)/shard_map/mlp_forward/pallas_call | solution.py:120
  157.1 4.6 %collective-permute-done.9 = bf16[2,192,3072]{2,1,0:T(8,128)(2,1)S(1)} collective-permute-done((bf16[2,192,3072]{2,1,0:T(8,128)(2,1)}, bf16[2,192,3072]{2,1,0:T(8,128)(2,1)S(1)}, u32[]{:S(2)}, u32[]{:S(2)}) %collective-permute-start.9) | collective-permute-done | bytes 2359328 | tf_op jit(solution)/shard_map/ppermute | solution.py:944
  161.6 4.0 %add_convert_fusion.1.refs_9_ = bf16[2,192,3072]{2,1,0:T(8,128)(2,1)} fusion(bf16[2,192,3072]{2,1,0:T(8,128)(2,1)S(1)} %collective-permute-done.9, bf16[2,192,3072]{2,1,0:T(8,128)(2,1)} %get-tuple-element.89), kind=kLoop, calls=%fused_computation.1 | loop fusion | flops 4718592 | bytes 7077888 | tf_op jit(solution)/shard_map/convert_element_type | solution.py:749
  165.6 4.6 %all-to-all-start = ((bf16[16,24,3072]{2,1,0:T(8,128)(2,1)}), bf16[16,24,3072]{2,1,0:T(8,128)(2,1)}, u32[]{:S(2)}, u32[]{:S(2)}) async-start(bf16[16,24,3072]{2,1,0:T(8,128)(2,1)} %bitcast.24), calls=%async_computation | async-start | bytes 4718592 | tf_op jit(solution)/shard_map/all_to_all | solution.py:948
  170.3 43.8 %mlp_backward.1 = (f32[2048,768]{1,0:T(8,128)}, bf16[2048,768]{1,0:T(8,128)(2,1)}, f32[3,768]{1,0:T(4,128)}, f32[1,3072]{1,0:T(1,128)}, bf16[2,192,3072]{2,1,0:T(8,128)(2,1)}, /*index=5*/bf16[2,192,3072]{2,1,0:T(8,128)(2,1)}) custom-call(s32[1]{0:T(128)} %bitcast.refs_0_, f32[2048,768]{1,0:T(8,128)} %get-tuple-element.85.refs_1_, ...), custom_call_target="tpu_custom_call" | custom-call | flops 28991029248 | bytes 75031552 | tf_op jit(solution)/shard_map/mlp_backward/pallas_call | solution.py:120
  214.4 7.0 %weight_grad.1 = (bf16[2,192,768]{2,1,0:T(8,128)(2,1)}, bf16[2,192,768]{2,1,0:T(8,128)(2,1)}) custom-call(s32[1]{0:T(128)} %bitcast.refs_0_, bf16[2048,768]{1,0:T(8,128)(2,1)} %get-tuple-element.91.refs_1_.refs_0_, bf16[2048,768]{1,0:T(8,128)(2,1)} %get-tuple-element.96.refs_2_, bf16[2,192,3072]{2,1,0:T(8,128)(2,1)} %get-tuple-element.99.refs_3_), custom_call_target="tpu_custom_call" | custom-call | flops 2415919104 | bytes 7471104 | tf_op jit(solution)/shard_map/weight_grad/pallas_call | solution.py:120
  221.4 4.0 %add_convert_fusion.refs_6_ = bf16[2,192,3072]{2,1,0:T(8,128)(2,1)} fusion(bf16[2,192,3072]{2,1,0:T(8,128)(2,1)} %collective-permute-done.10, bf16[2,192,3072]{2,1,0:T(8,128)(2,1)S(1)} %copy-done.1), kind=kLoop, calls=%fused_computation | loop fusion | flops 4718592 | bytes 7077888 | tf_op jit(solution)/shard_map/convert_element_type | solution.py:749
  225.4 6.7 %all-to-all-start.2 = ((bf16[16,24,3072]{2,1,0:T(8,128)(2,1)}), bf16[16,24,3072]{2,1,0:T(8,128)(2,1)S(1)}, u32[]{:S(2)}, u32[]{:S(2)}) async-start(bf16[16,24,3072]{2,1,0:T(8,128)(2,1)} %bitcast.33), calls=%async_computation.2 | async-start | bytes 4718592 | tf_op jit(solution)/shard_map/all_to_all | solution.py:948
  232.1 26.4 %attention_backward.1 = (bf16[2048,2304]{1,0:T(8,128)(2,1)}, f32[2,768]{1,0:T(2,128)}, f32[24,3072]{1,0:T(8,128)}) custom-call(bf16[2048,768]{1,0:T(8,128)(2,1)} %get-tuple-element.91.refs_1_.refs_0_, bf16[2048,2304]{1,0:T(8,128)(2,1)} %get-tuple-element.92.refs_1_, f32[2048,1536]{1,0:T(8,128)} %get-tuple-element.93.refs_2_, ...), custom_call_target="tpu_custom_call" | custom-call | flops 19327352832 | bytes 38443008 | tf_op jit(solution)/shard_map/attention_backward/pallas_call | solution.py:120
  260.5 13.2 %qkv_grad.1 = (bf16[2,192,1664]{2,1,0:T(8,128)(2,1)}, bf16[2,192,1664]{2,1,0:T(8,128)(2,1)}, bf16[2,192,768]{2,1,0:T(8,128)(2,1)}, bf16[2,192,768]{2,1,0:T(8,128)(2,1)}) custom-call(s32[1]{0:T(128)} %bitcast.refs_0_, bf16[2048,768]{1,0:T(8,128)(2,1)} %refs_1_.7, bf16[2048,2304]{1,0:T(8,128)(2,1)} %get-tuple-element.101.refs_2_.refs_0_, ...), custom_call_target="tpu_custom_call" | custom-call | flops 7247757312 | bytes 16711680 | tf_op jit(solution)/shard_map/qkv_grad/pallas_call | solution.py:120
  274.4 3.3 collective-permute-done.13
  277.7 0.8 collective-permute-done.12
  278.6 0.8 copy-done.5
  279.4 4.2 %plane_split.1 = (bf16[2,192,1664]{2,1,0:T(8,128)(2,1)}, f32[96,1536]{1,0:T(8,128)}, bf16[96,1536]{1,0:T(8,128)(2,1)}, bf16[96,1536]{1,0:T(8,128)(2,1)}, bf16[96,1536]{1,0:T(8,128)(2,1)}) custom-call(s32[1]{0:T(128)} %bitcast.25.refs_0_, bf16[2,192,1664]{2,1,0:T(8,128)(2,1)} %get-tuple-element.108.refs_1_, ...), custom_call_target="tpu_custom_call" | custom-call | bytes 7667712 | tf_op jit(solution)/shard_map/plane_split/pallas_call | solution.py:120
  283.6 1.3 all-to-all-done.2.refs_0_
  284.9 6.0 %all-to-all-start.1 = ((bf16[16,24,1664]{2,1,0:T(8,128)(2,1)}), bf16[16,24,1664]{2,1,0:T(8,128)(2,1)}, u32[]{:S(2)}, u32[]{:S(2)}) async-start(bf16[16,24,1664]{2,1,0:T(8,128)(2,1)} %bitcast.59), calls=%async_computation.1 | async-start | bytes 2555904 | tf_op jit(solution)/shard_map/all_to_all | solution.py:948
  290.9 1.9 collective-permute-start.14
  292.8 1.5 collective-permute-start.15
  294.5 13.4 %grad_tokens.1.refs_5_.refs_1_ = bf16[2048,768]{1,0:T(8,128)(2,1)} custom-call(bf16[2048,2304]{1,0:T(8,128)(2,1)} %get-tuple-element.101.refs_2_.refs_0_, f32[2048,768]{1,0:T(8,128)} %get-tuple-element.102.refs_1_, bf16[768,2304]{1,0:T(8,128)(2,1)} %get-tuple-element.103.refs_2_, bf16[2,192,1664]{2,1,0:T(8,128)(2,1)} %get-tuple-element.113.refs_3_, ...), custom_call_target="tpu_custom_call" | custom-call | flops 7247757312 | bytes 22413312 | tf_op jit(solution)/shard_map/grad_tokens/pallas_call | solution.py:120
  307.9 3.1 collective-permute-done.15.refs_3_
  311.0 11.6 %collective-permute-done.16.refs_4_ = bf16[96,1536]{1,0:T(8,128)(2,1)S(1)} collective-permute-done((bf16[96,1536]{1,0:T(8,128)(2,1)S(1)}, bf16[96,1536]{1,0:T(8,128)(2,1)S(1)}, u32[]{:S(2)}, u32[]{:S(2)}) %collective-permute-start.16) | collective-permute-done | bytes 294944 | tf_op jit(solution)/shard_map/ppermute | solution.py:743
  323.3 2.2 line_split.1
  325.9 3.2 collective-permute-start.18
  329.0 0.9 collective-permute-start.19
  329.9 2.7 fold_pieces.1.refs_5_.refs_3_
  332.6 1.4 collective-permute-done.18.refs_3_
  334.1 1.4 collective-permute-done.19.refs_4_
  336.1 2.7 fold_with_squares.1
  338.8 10.4 %all_to_all.38 = f32[32,1,128]{2,1,0:T(1,128)} all-to-all(f32[32,1,128]{2,1,0:T(1,128)} %bitcast.74), channel_id=1, replica_groups=mesh['hi'=2,'core'=2,'zed'=4,'low'=2] {'hi','core','zed','low'}, dimensions={0} | all-to-all | bytes 32768 | tf_op jit(solution)/shard_map/all_to_all | solution.py:1012
  349.2 4.2 %update_weights.1 = (f32[24,2304]{1,0:T(8,128)}, f32[24,2304]{1,0:T(8,128)}, f32[24,2304]{1,0:T(8,128)}, bf16[24,2304]{1,0:T(8,128)(2,1)}, f32[24,768]{1,0:T(8,1...) custom-call(f32[32,128]{1,0:T(8,128)} %bitcast.73, ...), custom_call_target="tpu_custom_call" | custom-call | bytes 6664704 | tf_op jit(solution)/shard_map/update_weights/pallas_call | solution.py:120
  (106 shorter events, 11.1 us)
Async XLA Ops:
  7.2 100.1 %all-gather.2.cloned.1.call-start = ((), (), s32[]{:S(2)}) async-start(), calls=%async_computation.4 | async-start | bytes 9732096 | tf_op jit(solution)/shard_map/all_gather | solution.py:898
  11.7 9.3 %collective-permute-start = (bf16[24,3200]{1,0:T(8,128)(2,1)S(1)}, bf16[24,3200]{1,0:T(8,128)(2,1)S(1)}, u32[]{:S(2)}, u32[]{:S(2)}) collective-permute-start(bf16[24,3200]{1,0:T(8,128)(2,1)S(1)} %fusion.6), channel_id=1, source_target_pairs={{0,2},{2,0},{4,6},{6,4},{1,3},{3,1},{5,7},{7,5},{8,10},{10,8},{12,... | collective-permute-start | bytes 460808 | tf_op jit(solution)/shard_map/ppermute | solution.py:844
  14.8 17.3 %collective-permute-start.1 = (bf16[24,3200]{1,0:T(8,128)(2,1)S(1)}, bf16[24,3200]{1,0:T(8,128)(2,1)S(1)}, u32[]{:S(2)}, u32[]{:S(2)}) collective-permute-start(bf16[24,3200]{1,0:T(8,128)(2,1)S(1)} %fusion.6), channel_id=1, source_target_pairs={{0,4},{2,6},{4,0},{6,2},{1,5},{3,7},{5,1},{7,3},{8,12},{10,14},{12... | collective-permute-start | bytes 460808 | tf_op jit(solution)/shard_map/ppermute | solution.py:844
  17.4 14.7 %collective-permute-start.2 = (bf16[24,3200]{1,0:T(8,128)(2,1)S(1)}, bf16[24,3200]{1,0:T(8,128)(2,1)S(1)}, u32[]{:S(2)}, u32[]{:S(2)}) collective-permute-start(bf16[24,3200]{1,0:T(8,128)(2,1)S(1)} %fusion.6), channel_id=1, source_target_pairs={{0,6},{2,4},{4,2},{6,0},{1,7},{3,5},{5,3},{7,1},{8,14},{10,12},{12... | collective-permute-start | bytes 460808 | tf_op jit(solution)/shard_map/ppermute | solution.py:844
  32.5 8.7 %collective-permute-start.3 = (bf16[4,24,1536]{2,1,0:T(8,128)(2,1)S(1)}, bf16[4,24,1536]{2,1,0:T(8,128)(2,1)S(1)}, u32[]{:S(2)}, u32[]{:S(2)}) collective-permute-start(bf16[4,24,1536]{2,1,0:T(8,128)(2,1)S(1)} %get-tuple-element.150), channel_id=1, source_target_pairs={{0,1},{1,0},{2,3},{3,2},{4,5},{5,4},{6,7},{7,6},{8,9},{9,8},{10,11... | collective-permute-start | bytes 884744 | tf_op jit(solution)/shard_map/ppermute | solution.py:844
  34.1 10.5 %collective-permute-start.6 = (bf16[4,24,1664]{2,1,0:T(8,128)(2,1)S(1)}, bf16[4,24,1664]{2,1,0:T(8,128)(2,1)S(1)}, u32[]{:S(2)}, u32[]{:S(2)}) collective-permute-start(bf16[4,24,1664]{2,1,0:T(8,128)(2,1)S(1)} %get-tuple-element.148), channel_id=1, source_target_pairs={{0,16},{16,0},{1,17},{17,1},{2,18},{18,2},{3,19},{19,3},{4,20},{20... | collective-permute-start | bytes 958472 | tf_op jit(solution)/shard_map/ppermute | solution.py:844
  41.4 18.9 %collective-permute-start.4 = (bf16[4,2,24,1536]{3,2,0,1:T(8,128)(2,1)S(1)}, bf16[4,2,24,1536]{3,2,0,1:T(8,128)(2,1)S(1)}, u32[]{:S(2)}, u32[]{:S(2)}) collective-permute-start(bf16[4,2,24,1536]{3,2,0,1:T(8,128)(2,1)S(1)} %get-tuple-element.152), channel_id=1, source_target_pairs={{0,16},{16,0},{1,17},{17,1},{2,18},{18,2},{3,19},{19,3},{4,20},{20... | collective-permute-start | bytes 1769480 | tf_op jit(solution)/shard_map/ppermute | solution.py:844
  44.8 15.6 %collective-permute-start.7 = (bf16[2,4,24,1664]{3,2,1,0:T(8,128)(2,1)S(1)}, bf16[2,4,24,1664]{3,2,1,0:T(8,128)(2,1)S(1)}, u32[]{:S(2)}, u32[]{:S(2)}) collective-permute-start(bf16[2,4,24,1664]{3,2,1,0:T(8,128)(2,1)S(1)} %reverse_select_fusion.2), channel_id=1, source_target_pairs={{0,1},{1,0},{2,3},{3,2},{4,5},{5,4},{6,7},{7,6},{8,9},{9,8},{10,11... | collective-permute-start | bytes 1916936 | tf_op jit(solution)/shard_map/ppermute | solution.py:844
  60.8 1.0 copy-start.2
  60.8 3.2 collective-permute-start.8
  61.2 5.1 %copy-start.3 = (bf16[2,4,2,24,1536]{4,3,2,1,0:T(8,128)(2,1)}, bf16[2,4,2,24,1536]{4,3,2,1,0:T(8,128)(2,1)S(1)}, u32[]{:S(2)}) copy-start(bf16[2,4,2,24,1536]{4,3,2,1,0:T(8,128)(2,1)S(1)} %copy.47) | copy-start | bytes 3538948
  61.2 5.1 %collective-permute-start.5 = (bf16[2,192,1536]{2,1,0:T(8,128)(2,1)S(1)}, bf16[2,192,1536]{2,1,0:T(8,128)(2,1)}, u32[]{:S(2)}, u32[]{:S(2)}) collective-permute-start(bf16[2,192,1536]{2,1,0:T(8,128)(2,1)S(1)} %bitcast.60), channel_id=1, source_target_pairs={{0,8},{8,0},{1,9},{9,1},{2,10},{10,2},{3,11},{11,3},{4,12},{12,4},... | collective-permute-start | bytes 3538952 | tf_op jit(solution)/shard_map/ppermute | solution.py:919
  156.9 4.7 %collective-permute-start.9 = (bf16[2,192,3072]{2,1,0:T(8,128)(2,1)}, bf16[2,192,3072]{2,1,0:T(8,128)(2,1)S(1)}, u32[]{:S(2)}, u32[]{:S(2)}) collective-permute-start(bf16[2,192,3072]{2,1,0:T(8,128)(2,1)} %get-tuple-element.90), channel_id=1, source_target_pairs={{0,8},{8,0},{1,9},{9,1},{2,10},{10,2},{3,11},{11,3},{4,12},{12,4},... | collective-permute-start | bytes 7077896 | tf_op jit(solution)/shard_map/ppermute | solution.py:944
  165.6 59.7 %all-to-all-start = ((bf16[16,24,3072]{2,1,0:T(8,128)(2,1)}), bf16[16,24,3072]{2,1,0:T(8,128)(2,1)}, u32[]{:S(2)}, u32[]{:S(2)}) async-start(bf16[16,24,3072]{2,1,0:T(8,128)(2,1)} %bitcast.24), calls=%async_computation | async-start | bytes 4718592 | tf_op jit(solution)/shard_map/all_to_all | solution.py:948
  170.2 44.0 %copy-start.14 = (f32[3,768]{1,0:T(4,128)S(1)}, f32[3,768]{1,0:T(4,128)}, u32[]{:S(2)}) copy-start(f32[3,768]{1,0:T(4,128)} %get-tuple-element.107) | copy-start | bytes 27652
  214.1 7.3 %collective-permute-start.10 = (bf16[2,192,3072]{2,1,0:T(8,128)(2,1)}, bf16[2,192,3072]{2,1,0:T(8,128)(2,1)}, u32[]{:S(2)}, u32[]{:S(2)}) collective-permute-start(bf16[2,192,3072]{2,1,0:T(8,128)(2,1)} %get-tuple-element.100), channel_id=1, source_target_pairs={{0,8},{8,0},{1,9},{9,1},{2,10},{10,2},{3,11},{11,3},{4,12},{12,4},... | collective-permute-start | bytes 7077896 | tf_op jit(solution)/shard_map/ppermute | solution.py:944
  214.3 7.0 %copy-start.15 = (f32[3,768]{1,0:T(4,128)S(1)}, f32[3,768]{1,0:T(4,128)}, u32[]{:S(2)}) copy-start(f32[3,768]{1,0:T(4,128)} %get-tuple-element.105) | copy-start | bytes 27652
  214.3 7.0 %copy-start.1 = (bf16[2,192,3072]{2,1,0:T(8,128)(2,1)S(1)}, bf16[2,192,3072]{2,1,0:T(8,128)(2,1)}, u32[]{:S(2)}) copy-start(bf16[2,192,3072]{2,1,0:T(8,128)(2,1)} %get-tuple-element.99.refs_3_) | copy-start | bytes 7077892
  225.4 59.5 %all-to-all-start.2 = ((bf16[16,24,3072]{2,1,0:T(8,128)(2,1)}), bf16[16,24,3072]{2,1,0:T(8,128)(2,1)S(1)}, u32[]{:S(2)}, u32[]{:S(2)}) async-start(bf16[16,24,3072]{2,1,0:T(8,128)(2,1)} %bitcast.33), calls=%async_computation.2 | async-start | bytes 4718592 | tf_op jit(solution)/shard_map/all_to_all | solution.py:948
  232.1 27.1 %copy-start.12 = (f32[1,3072]{1,0:T(1,128)S(1)}, f32[1,3072]{1,0:T(1,128)}, u32[]{:S(2)}) copy-start(f32[1,3072]{1,0:T(1,128)} %get-tuple-element.106) | copy-start | bytes 36868
  273.7 4.9 %collective-permute-start.11 = (bf16[2,192,1664]{2,1,0:T(8,128)(2,1)}, bf16[2,192,1664]{2,1,0:T(8,128)(2,1)}, u32[]{:S(2)}, u32[]{:S(2)}) collective-permute-start(bf16[2,192,1664]{2,1,0:T(8,128)(2,1)} %get-tuple-element.109), channel_id=1, source_target_pairs={{0,8},{8,0},{1,9},{9,1},{2,10},{10,2},{3,11},{11,3},{4,12},{12,4},... | collective-permute-start | bytes 3833864 | tf_op jit(solution)/shard_map/ppermute | solution.py:944
  273.9 3.9 %collective-permute-start.13 = (bf16[2,192,768]{2,1,0:T(8,128)(2,1)}, bf16[2,192,768]{2,1,0:T(8,128)(2,1)S(1)}, u32[]{:S(2)}, u32[]{:S(2)}) collective-permute-start(bf16[2,192,768]{2,1,0:T(8,128)(2,1)} %get-tuple-element.112), channel_id=1, source_target_pairs={{0,8},{8,0},{1,9},{9,1},{2,10},{10,2},{3,11},{11,3},{4,12},{12,4},... | collective-permute-start | bytes 1769480 | tf_op jit(solution)/shard_map/ppermute | solution.py:944
  274.2 4.4 %collective-permute-start.12 = (bf16[2,192,768]{2,1,0:T(8,128)(2,1)}, bf16[2,192,768]{2,1,0:T(8,128)(2,1)S(1)}, u32[]{:S(2)}, u32[]{:S(2)}) collective-permute-start(bf16[2,192,768]{2,1,0:T(8,128)(2,1)} %get-tuple-element.111), channel_id=1, source_target_pairs={{0,8},{8,0},{1,9},{9,1},{2,10},{10,2},{3,11},{11,3},{4,12},{12,4},... | collective-permute-start | bytes 1769480 | tf_op jit(solution)/shard_map/ppermute | solution.py:944
  277.7 0.9 copy-start.4
  278.6 0.8 copy-start.5
  283.6 7.3 %copy-start.20 = (bf16[96,1536]{1,0:T(8,128)(2,1)S(1)}, bf16[96,1536]{1,0:T(8,128)(2,1)}, u32[]{:S(2)}) copy-start(bf16[96,1536]{1,0:T(8,128)(2,1)} %get-tuple-element.115) | copy-start | bytes 884740
  283.6 9.3 %copy-start.19 = (bf16[96,1536]{1,0:T(8,128)(2,1)S(1)}, bf16[96,1536]{1,0:T(8,128)(2,1)}, u32[]{:S(2)}) copy-start(bf16[96,1536]{1,0:T(8,128)(2,1)} %get-tuple-element.116) | copy-start | bytes 884740
  283.6 10.7 %copy-start.18 = (bf16[96,1536]{1,0:T(8,128)(2,1)S(1)}, bf16[96,1536]{1,0:T(8,128)(2,1)}, u32[]{:S(2)}) copy-start(bf16[96,1536]{1,0:T(8,128)(2,1)} %get-tuple-element.117) | copy-start | bytes 884740
  284.9 22.9 %copy-start = (bf16[16,24,3072]{2,1,0:T(8,128)(2,1)}, bf16[16,24,3072]{2,1,0:T(8,128)(2,1)S(1)}, u32[]{:S(2)}) copy-start(bf16[16,24,3072]{2,1,0:T(8,128)(2,1)S(1)} %all-to-all-done.2.refs_0_) | copy-start | bytes 7077892
  284.9 50.6 %all-to-all-start.1 = ((bf16[16,24,1664]{2,1,0:T(8,128)(2,1)}), bf16[16,24,1664]{2,1,0:T(8,128)(2,1)}, u32[]{:S(2)}, u32[]{:S(2)}) async-start(bf16[16,24,1664]{2,1,0:T(8,128)(2,1)} %bitcast.59), calls=%async_computation.1 | async-start | bytes 2555904 | tf_op jit(solution)/shard_map/all_to_all | solution.py:948
  290.9 17.0 %collective-permute-start.14 = (bf16[96,1536]{1,0:T(8,128)(2,1)S(1)}, bf16[96,1536]{1,0:T(8,128)(2,1)S(1)}, u32[]{:S(2)}, u32[]{:S(2)}) collective-permute-start(bf16[96,1536]{1,0:T(8,128)(2,1)S(1)} %copy-done.20), channel_id=1, source_target_pairs={{0,1},{1,0},{16,17},{17,16},{2,3},{3,2},{18,19},{19,18},{4,5},{5,4... | collective-permute-start | bytes 884744 | tf_op jit(solution)/shard_map/ppermute | solution.py:743
  292.8 18.2 %collective-permute-start.15 = (bf16[96,1536]{1,0:T(8,128)(2,1)S(1)}, bf16[96,1536]{1,0:T(8,128)(2,1)S(1)}, u32[]{:S(2)}, u32[]{:S(2)}) collective-permute-start(bf16[96,1536]{1,0:T(8,128)(2,1)S(1)} %copy-done.19), channel_id=1, source_target_pairs={{0,16},{1,17},{16,0},{17,1},{2,18},{3,19},{18,2},{19,3},{4,20},{5,... | collective-permute-start | bytes 884744 | tf_op jit(solution)/shard_map/ppermute | solution.py:743
  294.3 28.3 %collective-permute-start.16 = (bf16[96,1536]{1,0:T(8,128)(2,1)S(1)}, bf16[96,1536]{1,0:T(8,128)(2,1)S(1)}, u32[]{:S(2)}, u32[]{:S(2)}) collective-permute-start(bf16[96,1536]{1,0:T(8,128)(2,1)S(1)} %copy-done.18), channel_id=1, source_target_pairs={{0,17},{1,16},{16,1},{17,0},{2,19},{3,18},{18,3},{19,2},{4,21},{5,... | collective-permute-start | bytes 884744 | tf_op jit(solution)/shard_map/ppermute | solution.py:743
  307.9 14.7 %copy-start.6 = (bf16[96,1536]{1,0:T(8,128)(2,1)}, bf16[96,1536]{1,0:T(8,128)(2,1)S(1)}, u32[]{:S(2)}) copy-start(bf16[96,1536]{1,0:T(8,128)(2,1)S(1)} %collective-permute-done.14.refs_2_) | copy-start | bytes 884740
  311.0 11.6 %copy-start.7 = (bf16[96,1536]{1,0:T(8,128)(2,1)}, bf16[96,1536]{1,0:T(8,128)(2,1)S(1)}, u32[]{:S(2)}) copy-start(bf16[96,1536]{1,0:T(8,128)(2,1)S(1)} %collective-permute-done.15.refs_3_) | copy-start | bytes 884740
  322.6 0.7 copy-start.8
  325.6 7.1 %collective-permute-start.17 = (bf16[24,1536]{1,0:T(8,128)(2,1)}, bf16[24,1536]{1,0:T(8,128)(2,1)S(1)}, u32[]{:S(2)}, u32[]{:S(2)}) collective-permute-start(bf16[24,1536]{1,0:T(8,128)(2,1)} %get-tuple-element.119), channel_id=1, source_target_pairs={{0,2},{2,0},{4,6},{6,4},{1,3},{3,1},{5,7},{7,5},{8,10},{10,8},{12,... | collective-permute-start | bytes 221192 | tf_op jit(solution)/shard_map/ppermute | solution.py:743
  325.9 8.2 %collective-permute-start.18 = (bf16[24,1536]{1,0:T(8,128)(2,1)}, bf16[24,1536]{1,0:T(8,128)(2,1)S(1)}, u32[]{:S(2)}, u32[]{:S(2)}) collective-permute-start(bf16[24,1536]{1,0:T(8,128)(2,1)} %get-tuple-element.120), channel_id=1, source_target_pairs={{0,4},{2,6},{4,0},{6,2},{1,5},{3,7},{5,1},{7,3},{8,12},{10,14},{12... | collective-permute-start | bytes 221192 | tf_op jit(solution)/shard_map/ppermute | solution.py:743
  329.0 6.5 %collective-permute-start.19 = (bf16[24,1536]{1,0:T(8,128)(2,1)}, bf16[24,1536]{1,0:T(8,128)(2,1)S(1)}, u32[]{:S(2)}, u32[]{:S(2)}) collective-permute-start(bf16[24,1536]{1,0:T(8,128)(2,1)} %get-tuple-element.121), channel_id=1, source_target_pairs={{0,6},{2,4},{4,2},{6,0},{1,7},{3,5},{5,3},{7,1},{8,14},{10,12},{12... | collective-permute-start | bytes 221192 | tf_op jit(solution)/shard_map/ppermute | solution.py:743
  332.6 2.9 copy-start.9
  334.1 1.4 copy-start.10
  335.5 0.6 copy-start.11
  338.8 16.2 %copy-start.13 = (f32[288]{0:T(512)S(1)}, f32[288]{0:T(512)}, u32[]{:S(2)}) copy-start(f32[288]{0:T(512)} %param.25) | copy-start | bytes 3460
  338.8 16.2 %copy-start.16 = (f32[288]{0:T(512)S(1)}, f32[288]{0:T(512)}, u32[]{:S(2)}) copy-start(f32[288]{0:T(512)} %param.34) | copy-start | bytes 3460
  338.8 16.2 %copy-start.17 = (f32[288]{0:T(512)S(1)}, f32[288]{0:T(512)}, u32[]{:S(2)}) copy-start(f32[288]{0:T(512)} %param.35) | copy-start | bytes 3460
Sparse Core Ops, SparseCore 0:
  11.5 95.7 all-gather.1

commit v6 on v5

--- a/solution.py
+++ b/solution.py
@@ -366,6 +366,21 @@
     )
 
 
+def weight_copies(packed, targets, chunk, sems):
+    copies, column = [], 0
+    for target in targets:
+        for place in range(0, target.shape[1], chunk):
+            copies.append(
+                pltpu.make_async_copy(
+                    packed.at[:, column : column + chunk],
+                    target.at[:, place : place + chunk],
+                    sems.at[len(copies)],
+                )
+            )
+            column += chunk
+    return copies
+
+
 def mlp_backward_body(
     tiles,
     core,
@@ -374,8 +389,7 @@
     normed_one,
     inverse_one,
     hidden_low,
-    w_up,
-    w_down,
+    packed,
     small,
     first_out,
     first_low_out,
@@ -388,19 +402,18 @@
     total,
     sums,
     wide_sums,
+    w_up,
+    w_down,
+    sems,
 ):
     step = pl.program_id(0)
-
-    @pl.when(step == 0)
-    def _():
-        sums[...] = jnp.zeros_like(sums)
-        wide_sums[...] = jnp.zeros_like(wide_sums)
-
-    @pl.when(step < tiles)
-    def _():
+    chunk = normed_one.shape[1]
+    copies = weight_copies(packed, (w_up, w_down), chunk, sems)
+    half = len(copies) // 2
+
+    def tile(arriving):
         rows, width = normed_one.shape
         hidden = slope.shape[1]
-        chunk = width
         at = small_places(width, hidden)
         place = pl.ds(pl.multiple_of(step * rows, rows), rows)
         hidden_all[place, :] = hidden_low[...]
@@ -409,6 +422,9 @@
         grad_hidden = incoming
         for piece in range(hidden // chunk):
             columns = slice(piece * chunk, (piece + 1) * chunk)
+            if arriving:
+                copies[half + piece].wait()
+                copies[piece].wait()
             grad_pre = dot_nn(incoming_low, w_down[:, columns]) * slope[:, columns]
             wide_sums[:, columns] += fold_rows(grad_pre)
             grad_low = grad_pre.astype(BF16)
@@ -424,6 +440,19 @@
         first_low_out[...] = grad_first.astype(BF16)
         sums[2] += fold_rows(grad_first)
 
+    @pl.when(step == 0)
+    def _():
+        for piece in range(half):
+            copies[half + piece].start()
+            copies[piece].start()
+        sums[...] = jnp.zeros_like(sums)
+        wide_sums[...] = jnp.zeros_like(wide_sums)
+        tile(True)
+
+    @pl.when((step > 0) & (step < tiles))
+    def _():
+        tile(False)
+
     @pl.when(step == tiles)
     def _():
         sums_out[...] = jnp.sum(sums[...], axis=1)
@@ -444,15 +473,14 @@
         functools.partial(mlp_backward_body, tiles),
         "mlp_backward",
         (tiles + hidden // wide,),
-        [grad_second, slope, normed_one, inverse_one, hidden_low, packed, packed, small],
+        [grad_second, slope, normed_one, inverse_one, hidden_low, packed, small],
         [
             tile_spec(block, width, tiles),
             tile_spec(block, hidden, tiles),
             tile_spec(block, width, tiles),
             tile_spec(block, LANES, tiles),
             tile_spec(block, width, tiles),
-            held_spec(width, hidden),
-            held_spec(width, hidden, 1),
+            pl.BlockSpec(memory_space=pl.ANY),
             held_spec(1, small.shape[1]),
         ],
         [
@@ -478,6 +506,9 @@
             pltpu.VMEM((width, wide), F32),
             pltpu.VMEM((3, 8, width), F32),
             pltpu.VMEM((8, hidden), F32),
+            pltpu.VMEM((width, hidden), BF16),
+            pltpu.VMEM((width, hidden), BF16),
+            pltpu.SemaphoreType.DMA((2 * hidden // width,)),
         ],
         after=after,
         flops=6 * rows * width * hidden,
@@ -970,7 +1001,7 @@
     up = add_pairs([(keep, received)])
     out = swap_cores(out)
     joined_grad, sums_qv, sum_down = attention_backward(
-        first_low, joined, probs, whole_out, down, after=[out_done, up]
+        first_low, joined, probs, whole_out, down, after=[out_done, out[1], up]
     )
     up = peer_sum(up)
     grad_small = jnp.concatenate(

time: 363 us -> 363 us (level)
  no operation moved by 1% of the time
where the time goes in v6:
time: 363 us; the launch traced here: 362 us
  Pallas kernels  202 us (56%)
  waiting for transfers between devices  75.1 us (21%)
  starting transfers between devices  38.2 us (11%)
  between operations  15.2 us (4%)
  other arithmetic  13.4 us (4%)
  blocking collectives  10.4 us (3%)
  local copies, waits for them, and re-layouts  7.42 us (2%)
    pallas_call x13, Pallas kernels, call_kernel(): pl.pallas_call(wrapped, grid_spec=pltpu.PrefetchScalarGridSpec(num_scalar...  202 us
    ppermute x7, waiting for transfers between devices, gather_axis(): lax.ppermute(value, axis, [(place, place ^ step) for place in range(size)])  36.6 us
    ppermute x6, waiting for transfers between devices, trade(): lax.ppermute(parts[step], axis, [(place, place ^ step) for place in range...  17.7 us
    all_to_all x3, starting transfers between devices, peer_sum(): pieces = lax.all_to_all(both.reshape(-1, columns), PEERS, 0, 0, tiled=True)  17.3 us
    ppermute x7, starting transfers between devices, gather_axis(): lax.ppermute(value, axis, [(place, place ^ step) for place in range(size)])  11.1 us
    all_to_all x1, blocking collectives, body(): squares = lax.all_to_all(spread, ALL, 0, 0, tiled=True)  10.4 us
    all_gather x1, waiting for transfers between devices, body(): packed = lax.all_gather(back, ALL, axis=0, tiled=True)  9.04 us
    ppermute x5, waiting for transfers between devices, swap_cores(): return (keep, lax.ppermute(send, 'core', swap))  8.25 us
  transfers between devices with their start and end apart: 24, of which 16 were waited for; matrix products, arithmetic and copies ran while one was open for 4% of the time, Pallas kernels for 40%

profile of v6, /device:TPU:0, one launch (start us, length us, event | category | flops | bytes accessed | tf_op | source)
XLA Modules:
  0.0 362.1 jit_solution(4272827296164656915)
XLA Ops:
  7.2 1.8 pack_rows.1
  9.1 1.0 convert_element_type.39
  10.0 0.9 convert_element_type.41
  11.7 3.1 collective-permute-start
  14.8 2.6 collective-permute-start.1
  17.4 3.5 collective-permute-done
  21.0 11.1 %collective-permute-done.1 = bf16[24,3200]{1,0:T(8,128)(2,1)S(1)} collective-permute-done((bf16[24,3200]{1,0:T(8,128)(2,1)S(1)}, bf16[24,3200]{1,0:T(8,128)(2,1)S(1)}, u32[]{:S(2)}, u32[]{:S(2)}) %collective-permute-start.1) | collective-permute-done | bytes 153632 | tf_op jit(solution)/shard_map/ppermute | solution.py:875
  32.5 1.6 collective-permute-start.3
  34.1 1.6 collective-permute-start.6
  35.7 5.5 %collective-permute-done.3 = bf16[4,24,1536]{2,1,0:T(8,128)(2,1)S(1)} collective-permute-done((bf16[4,24,1536]{2,1,0:T(8,128)(2,1)S(1)}, bf16[4,24,1536]{2,1,0:T(8,128)(2,1)S(1)}, u32[]{:S(2)}, u32[]{:S(2)}) %collective-permute-start.3) | collective-permute-done | bytes 294944 | tf_op jit(solution)/shard_map/ppermute | solution.py:875
  41.4 1.5 collective-permute-start.4
  42.9 1.8 collective-permute-done.6
  45.7 14.6 %collective-permute-done.4 = bf16[4,2,24,1536]{3,2,0,1:T(8,128)(2,1)S(1)} collective-permute-done((bf16[4,2,24,1536]{3,2,0,1:T(8,128)(2,1)S(1)}, bf16[4,2,24,1536]{3,2,0,1:T(8,128)(2,1)S(1)}, u32[]{:S(2)}, u32[]{:S(2)}) %collective-permute-start.4) | collective-permute-done | bytes 589856 | tf_op jit(solution)/shard_map/ppermute | solution.py:875
  62.0 2.0 collective-permute-done.8.refs_6_
  64.0 0.9 slice_bitcast_fusion
  65.4 0.9 reshape.178.refs_7_.refs_6_
  66.3 31.9 %attention_forward.1 = (bf16[2048,2304]{1,0:T(8,128)(2,1)}, f32[2048,1536]{1,0:T(8,128)}, bf16[2048,768]{1,0:T(8,128)(2,1)}, f32[2048,768]{1,0:T(8,128)}, f32[20...) custom-call(s32[1]{0:T(128)} %bitcast.refs_0_, s32[16]{0:T(128)} %refs_1_.6, ...), custom_call_target="tpu_custom_call" | custom-call | flops 14495514624 | bytes 48467968 | tf_op jit(solution)/shard_map/attention_forward/pallas_call | solution.py:120
  98.2 9.0 %all-gather.2.cloned.1.call-done.refs_4_.refs_5_.refs_6_ = bf16[768,6144]{1,0:T(8,128)(2,1)} async-done(((bf16[24,6144]{1,0:T(8,128)(2,1)}), bf16[768,6144]{1,0:T(8,128)(2,1)}) %all-gather.2.cloned.1.call-update) | async-done | bytes 9437200 | tf_op jit(solution)/shard_map/all_gather | solution.py:929
  107.3 49.6 %mlp_forward.1 = (bf16[2048,768]{1,0:T(8,128)(2,1)}, f32[2048,3072]{1,0:T(8,128)}, f32[2048,768]{1,0:T(8,128)}, f32[3,768]{1,0:T(4,128)}, bf16[2,192,3072]{2,1,0:T(8,128)(2,1)}, /*index=5*/bf16[2,192,3072]{2,1,0:T(8,128)(2,1)}) custom-call(s32[1]{0:T(128)} %bitcast.refs_0_, s32[16]{0:T(128)} %refs_1_.6, f32[2048,768]{1,0:T(8,128)} %get-tuple-element.83.refs_2_.refs_3_, ...), custom_call_target="tpu_custom_call" | custom-call | flops 28991029248 | bytes 67679232 | tf_op jit(solution)/shard_map/mlp_forward/pallas_call | solution.py:120
  157.1 4.6 %collective-permute-done.9 = bf16[2,192,3072]{2,1,0:T(8,128)(2,1)S(1)} collective-permute-done((bf16[2,192,3072]{2,1,0:T(8,128)(2,1)}, bf16[2,192,3072]{2,1,0:T(8,128)(2,1)S(1)}, u32[]{:S(2)}, u32[]{:S(2)}) %collective-permute-start.9) | collective-permute-done | bytes 2359328 | tf_op jit(solution)/shard_map/ppermute | solution.py:975
  161.6 4.0 %add_convert_fusion.1.refs_8_ = bf16[2,192,3072]{2,1,0:T(8,128)(2,1)} fusion(bf16[2,192,3072]{2,1,0:T(8,128)(2,1)S(1)} %collective-permute-done.9, bf16[2,192,3072]{2,1,0:T(8,128)(2,1)} %get-tuple-element.89), kind=kLoop, calls=%fused_computation.1 | loop fusion | flops 4718592 | bytes 7077888 | tf_op jit(solution)/shard_map/convert_element_type | solution.py:780
  165.6 4.6 %all-to-all-start = ((bf16[16,24,3072]{2,1,0:T(8,128)(2,1)}), bf16[16,24,3072]{2,1,0:T(8,128)(2,1)}, u32[]{:S(2)}, u32[]{:S(2)}) async-start(bf16[16,24,3072]{2,1,0:T(8,128)(2,1)} %bitcast.24), calls=%async_computation | async-start | bytes 4718592 | tf_op jit(solution)/shard_map/all_to_all | solution.py:979
  170.3 43.2 %mlp_backward.1 = (f32[2048,768]{1,0:T(8,128)}, bf16[2048,768]{1,0:T(8,128)(2,1)}, f32[3,768]{1,0:T(4,128)}, f32[1,3072]{1,0:T(1,128)}, bf16[2,192,3072]{2,1,0:T(8,128)(2,1)}, /*index=5*/bf16[2,192,3072]{2,1,0:T(8,128)(2,1)}) custom-call(s32[1]{0:T(128)} %bitcast.refs_0_, f32[2048,768]{1,0:T(8,128)} %get-tuple-element.85.refs_1_, ...), custom_call_target="tpu_custom_call" | custom-call | flops 28991029248 | bytes 65594368 | tf_op jit(solution)/shard_map/mlp_backward/pallas_call | solution.py:120
  213.8 7.0 %weight_grad.1 = (bf16[2,192,768]{2,1,0:T(8,128)(2,1)}, bf16[2,192,768]{2,1,0:T(8,128)(2,1)}) custom-call(s32[1]{0:T(128)} %bitcast.refs_0_, bf16[2048,768]{1,0:T(8,128)(2,1)} %get-tuple-element.91.refs_1_.refs_0_, bf16[2048,768]{1,0:T(8,128)(2,1)} %get-tuple-element.96.refs_2_, bf16[2,192,3072]{2,1,0:T(8,128)(2,1)} %get-tuple-element.100.refs_3_), custom_call_target="tpu_custom_call" | custom-call | flops 2415919104 | bytes 7471104 | tf_op jit(solution)/shard_map/weight_grad/pallas_call | solution.py:120
  221.1 4.0 %add_convert_fusion.refs_7_ = bf16[2,192,3072]{2,1,0:T(8,128)(2,1)} fusion(bf16[2,192,3072]{2,1,0:T(8,128)(2,1)} %collective-permute-done.11, bf16[2,192,3072]{2,1,0:T(8,128)(2,1)S(1)} %copy-done.1), kind=kLoop, calls=%fused_computation | loop fusion | flops 4718592 | bytes 7077888 | tf_op jit(solution)/shard_map/convert_element_type | solution.py:780
  225.1 6.8 %all-to-all-start.2 = ((bf16[16,24,3072]{2,1,0:T(8,128)(2,1)}), bf16[16,24,3072]{2,1,0:T(8,128)(2,1)S(1)}, u32[]{:S(2)}, u32[]{:S(2)}) async-start(bf16[16,24,3072]{2,1,0:T(8,128)(2,1)} %bitcast.33), calls=%async_computation.2 | async-start | bytes 4718592 | tf_op jit(solution)/shard_map/all_to_all | solution.py:979
  232.0 0.9 copy-done.4
  232.8 26.4 %attention_backward.1 = (bf16[2048,2304]{1,0:T(8,128)(2,1)}, f32[2,768]{1,0:T(2,128)}, f32[24,3072]{1,0:T(8,128)}) custom-call(bf16[2048,768]{1,0:T(8,128)(2,1)} %get-tuple-element.91.refs_1_.refs_0_, bf16[2048,2304]{1,0:T(8,128)(2,1)} %get-tuple-element.92.refs_1_, f32[2048,1536]{1,0:T(8,128)} %get-tuple-element.93.refs_2_, ...), custom_call_target="tpu_custom_call" | custom-call | flops 19327352832 | bytes 38443008 | tf_op jit(solution)/shard_map/attention_backward/pallas_call | solution.py:120
  260.4 0.8 pad.9.refs_3_
  261.3 13.1 %qkv_grad.1 = (bf16[2,192,1664]{2,1,0:T(8,128)(2,1)}, bf16[2,192,1664]{2,1,0:T(8,128)(2,1)}, bf16[2,192,768]{2,1,0:T(8,128)(2,1)}, bf16[2,192,768]{2,1,0:T(8,128)(2,1)}) custom-call(s32[1]{0:T(128)} %bitcast.refs_0_, bf16[2048,768]{1,0:T(8,128)(2,1)} %refs_1_.7, bf16[2048,2304]{1,0:T(8,128)(2,1)} %get-tuple-element.102.refs_2_.refs_0_, ...), custom_call_target="tpu_custom_call" | custom-call | flops 7247757312 | bytes 16711680 | tf_op jit(solution)/shard_map/qkv_grad/pallas_call | solution.py:120
  274.9 3.2 collective-permute-done.13
  278.9 4.2 %plane_split.1 = (bf16[2,192,1664]{2,1,0:T(8,128)(2,1)}, f32[96,1536]{1,0:T(8,128)}, bf16[96,1536]{1,0:T(8,128)(2,1)}, bf16[96,1536]{1,0:T(8,128)(2,1)}, bf16[96,1536]{1,0:T(8,128)(2,1)}) custom-call(s32[1]{0:T(128)} %bitcast.25.refs_0_, bf16[2,192,1664]{2,1,0:T(8,128)(2,1)} %get-tuple-element.109.refs_1_, ...), custom_call_target="tpu_custom_call" | custom-call | bytes 7667712 | tf_op jit(solution)/shard_map/plane_split/pallas_call | solution.py:120
  283.1 1.5 all-to-all-done.2.refs_0_
  284.6 5.8 %all-to-all-start.1 = ((bf16[16,24,1664]{2,1,0:T(8,128)(2,1)}), bf16[16,24,1664]{2,1,0:T(8,128)(2,1)}, u32[]{:S(2)}, u32[]{:S(2)}) async-start(bf16[16,24,1664]{2,1,0:T(8,128)(2,1)} %bitcast.59), calls=%async_computation.1 | async-start | bytes 2555904 | tf_op jit(solution)/shard_map/all_to_all | solution.py:979
  290.5 1.9 collective-permute-start.14
  292.4 1.5 collective-permute-start.15
  294.0 13.4 %grad_tokens.1.refs_5_.refs_1_ = bf16[2048,768]{1,0:T(8,128)(2,1)} custom-call(bf16[2048,2304]{1,0:T(8,128)(2,1)} %get-tuple-element.102.refs_2_.refs_0_, f32[2048,768]{1,0:T(8,128)} %get-tuple-element.103.refs_1_, bf16[768,2304]{1,0:T(8,128)(2,1)} %get-tuple-element.104.refs_2_, bf16[2,192,1664]{2,1,0:T(8,128)(2,1)} %get-tuple-element.113.refs_3_, ...), custom_call_target="tpu_custom_call" | custom-call | flops 7247757312 | bytes 22413312 | tf_op jit(solution)/shard_map/grad_tokens/pallas_call | solution.py:120
  307.7 2.9 collective-permute-done.15.refs_3_
  310.7 11.6 %collective-permute-done.16.refs_4_ = bf16[96,1536]{1,0:T(8,128)(2,1)S(1)} collective-permute-done((bf16[96,1536]{1,0:T(8,128)(2,1)S(1)}, bf16[96,1536]{1,0:T(8,128)(2,1)S(1)}, u32[]{:S(2)}, u32[]{:S(2)}) %collective-permute-start.16) | collective-permute-done | bytes 294944 | tf_op jit(solution)/shard_map/ppermute | solution.py:774
  323.0 2.2 line_split.1
  325.5 3.2 collective-permute-start.18
  328.7 0.9 collective-permute-start.19
  329.6 2.7 fold_pieces.1.refs_5_.refs_3_
  332.3 1.6 collective-permute-done.18.refs_3_
  333.8 1.3 collective-permute-done.19.refs_4_
  335.8 2.7 fold_with_squares.1
  338.5 10.4 %all_to_all.38 = f32[32,1,128]{2,1,0:T(1,128)} all-to-all(f32[32,1,128]{2,1,0:T(1,128)} %bitcast.74), channel_id=1, replica_groups=mesh['hi'=2,'core'=2,'zed'=4,'low'=2] {'hi','core','zed','low'}, dimensions={0} | all-to-all | bytes 32768 | tf_op jit(solution)/shard_map/all_to_all | solution.py:1043
  348.9 4.2 %update_weights.1 = (f32[24,2304]{1,0:T(8,128)}, f32[24,2304]{1,0:T(8,128)}, f32[24,2304]{1,0:T(8,128)}, bf16[24,2304]{1,0:T(8,128)(2,1)}, f32[24,768]{1,0:T(8,1...) custom-call(f32[32,128]{1,0:T(8,128)} %bitcast.73, ...), custom_call_target="tpu_custom_call" | custom-call | bytes 6664704 | tf_op jit(solution)/shard_map/update_weights/pallas_call | solution.py:120
  (106 shorter events, 11.5 us)
Async XLA Ops:
  7.2 100.1 %all-gather.2.cloned.1.call-start = ((), (), s32[]{:S(2)}) async-start(), calls=%async_computation.4 | async-start | bytes 9732096 | tf_op jit(solution)/shard_map/all_gather | solution.py:929
  11.7 9.3 %collective-permute-start = (bf16[24,3200]{1,0:T(8,128)(2,1)S(1)}, bf16[24,3200]{1,0:T(8,128)(2,1)S(1)}, u32[]{:S(2)}, u32[]{:S(2)}) collective-permute-start(bf16[24,3200]{1,0:T(8,128)(2,1)S(1)} %fusion.6), channel_id=1, source_target_pairs={{0,2},{2,0},{4,6},{6,4},{1,3},{3,1},{5,7},{7,5},{8,10},{10,8},{12,... | collective-permute-start | bytes 460808 | tf_op jit(solution)/shard_map/ppermute | solution.py:875
  14.8 17.3 %collective-permute-start.1 = (bf16[24,3200]{1,0:T(8,128)(2,1)S(1)}, bf16[24,3200]{1,0:T(8,128)(2,1)S(1)}, u32[]{:S(2)}, u32[]{:S(2)}) collective-permute-start(bf16[24,3200]{1,0:T(8,128)(2,1)S(1)} %fusion.6), channel_id=1, source_target_pairs={{0,4},{2,6},{4,0},{6,2},{1,5},{3,7},{5,1},{7,3},{8,12},{10,14},{12... | collective-permute-start | bytes 460808 | tf_op jit(solution)/shard_map/ppermute | solution.py:875
  17.4 14.7 %collective-permute-start.2 = (bf16[24,3200]{1,0:T(8,128)(2,1)S(1)}, bf16[24,3200]{1,0:T(8,128)(2,1)S(1)}, u32[]{:S(2)}, u32[]{:S(2)}) collective-permute-start(bf16[24,3200]{1,0:T(8,128)(2,1)S(1)} %fusion.6), channel_id=1, source_target_pairs={{0,6},{2,4},{4,2},{6,0},{1,7},{3,5},{5,3},{7,1},{8,14},{10,12},{12... | collective-permute-start | bytes 460808 | tf_op jit(solution)/shard_map/ppermute | solution.py:875
  32.5 8.7 %collective-permute-start.3 = (bf16[4,24,1536]{2,1,0:T(8,128)(2,1)S(1)}, bf16[4,24,1536]{2,1,0:T(8,128)(2,1)S(1)}, u32[]{:S(2)}, u32[]{:S(2)}) collective-permute-start(bf16[4,24,1536]{2,1,0:T(8,128)(2,1)S(1)} %get-tuple-element.150), channel_id=1, source_target_pairs={{0,1},{1,0},{2,3},{3,2},{4,5},{5,4},{6,7},{7,6},{8,9},{9,8},{10,11... | collective-permute-start | bytes 884744 | tf_op jit(solution)/shard_map/ppermute | solution.py:875
  34.1 10.5 %collective-permute-start.6 = (bf16[4,24,1664]{2,1,0:T(8,128)(2,1)S(1)}, bf16[4,24,1664]{2,1,0:T(8,128)(2,1)S(1)}, u32[]{:S(2)}, u32[]{:S(2)}) collective-permute-start(bf16[4,24,1664]{2,1,0:T(8,128)(2,1)S(1)} %get-tuple-element.148), channel_id=1, source_target_pairs={{0,16},{16,0},{1,17},{17,1},{2,18},{18,2},{3,19},{19,3},{4,20},{20... | collective-permute-start | bytes 958472 | tf_op jit(solution)/shard_map/ppermute | solution.py:875
  41.4 18.9 %collective-permute-start.4 = (bf16[4,2,24,1536]{3,2,0,1:T(8,128)(2,1)S(1)}, bf16[4,2,24,1536]{3,2,0,1:T(8,128)(2,1)S(1)}, u32[]{:S(2)}, u32[]{:S(2)}) collective-permute-start(bf16[4,2,24,1536]{3,2,0,1:T(8,128)(2,1)S(1)} %get-tuple-element.152), channel_id=1, source_target_pairs={{0,16},{16,0},{1,17},{17,1},{2,18},{18,2},{3,19},{19,3},{4,20},{20... | collective-permute-start | bytes 1769480 | tf_op jit(solution)/shard_map/ppermute | solution.py:875
  44.8 15.6 %collective-permute-start.7 = (bf16[2,4,24,1664]{3,2,1,0:T(8,128)(2,1)S(1)}, bf16[2,4,24,1664]{3,2,1,0:T(8,128)(2,1)S(1)}, u32[]{:S(2)}, u32[]{:S(2)}) collective-permute-start(bf16[2,4,24,1664]{3,2,1,0:T(8,128)(2,1)S(1)} %reverse_select_fusion.2), channel_id=1, source_target_pairs={{0,1},{1,0},{2,3},{3,2},{4,5},{5,4},{6,7},{7,6},{8,9},{9,8},{10,11... | collective-permute-start | bytes 1916936 | tf_op jit(solution)/shard_map/ppermute | solution.py:875
  60.8 1.0 copy-start.2
  60.8 3.2 collective-permute-start.8
  61.2 5.1 %copy-start.3 = (bf16[2,4,2,24,1536]{4,3,2,1,0:T(8,128)(2,1)}, bf16[2,4,2,24,1536]{4,3,2,1,0:T(8,128)(2,1)S(1)}, u32[]{:S(2)}) copy-start(bf16[2,4,2,24,1536]{4,3,2,1,0:T(8,128)(2,1)S(1)} %copy.47) | copy-start | bytes 3538948
  61.2 5.1 %collective-permute-start.5 = (bf16[2,192,1536]{2,1,0:T(8,128)(2,1)S(1)}, bf16[2,192,1536]{2,1,0:T(8,128)(2,1)}, u32[]{:S(2)}, u32[]{:S(2)}) collective-permute-start(bf16[2,192,1536]{2,1,0:T(8,128)(2,1)S(1)} %bitcast.60), channel_id=1, source_target_pairs={{0,8},{8,0},{1,9},{9,1},{2,10},{10,2},{3,11},{11,3},{4,12},{12,4},... | collective-permute-start | bytes 3538952 | tf_op jit(solution)/shard_map/ppermute | solution.py:950
  156.9 4.7 %collective-permute-start.9 = (bf16[2,192,3072]{2,1,0:T(8,128)(2,1)}, bf16[2,192,3072]{2,1,0:T(8,128)(2,1)S(1)}, u32[]{:S(2)}, u32[]{:S(2)}) collective-permute-start(bf16[2,192,3072]{2,1,0:T(8,128)(2,1)} %get-tuple-element.90), channel_id=1, source_target_pairs={{0,8},{8,0},{1,9},{9,1},{2,10},{10,2},{3,11},{11,3},{4,12},{12,4},... | collective-permute-start | bytes 7077896 | tf_op jit(solution)/shard_map/ppermute | solution.py:975
  165.6 59.5 %all-to-all-start = ((bf16[16,24,3072]{2,1,0:T(8,128)(2,1)}), bf16[16,24,3072]{2,1,0:T(8,128)(2,1)}, u32[]{:S(2)}, u32[]{:S(2)}) async-start(bf16[16,24,3072]{2,1,0:T(8,128)(2,1)} %bitcast.24), calls=%async_computation | async-start | bytes 4718592 | tf_op jit(solution)/shard_map/all_to_all | solution.py:979
  170.2 43.4 %copy-start.14 = (f32[3,768]{1,0:T(4,128)S(1)}, f32[3,768]{1,0:T(4,128)}, u32[]{:S(2)}) copy-start(f32[3,768]{1,0:T(4,128)} %get-tuple-element.108) | copy-start | bytes 27652
  213.5 7.7 %collective-permute-start.11 = (bf16[2,192,3072]{2,1,0:T(8,128)(2,1)}, bf16[2,192,3072]{2,1,0:T(8,128)(2,1)}, u32[]{:S(2)}, u32[]{:S(2)}) collective-permute-start(bf16[2,192,3072]{2,1,0:T(8,128)(2,1)} %get-tuple-element.101), channel_id=1, source_target_pairs={{0,8},{8,0},{1,9},{9,1},{2,10},{10,2},{3,11},{11,3},{4,12},{12,4},... | collective-permute-start | bytes 7077896 | tf_op jit(solution)/shard_map/ppermute | solution.py:975
  213.7 7.4 %copy-start.15 = (f32[3,768]{1,0:T(4,128)S(1)}, f32[3,768]{1,0:T(4,128)}, u32[]{:S(2)}) copy-start(f32[3,768]{1,0:T(4,128)} %get-tuple-element.106) | copy-start | bytes 27652
  213.7 7.4 %copy-start.1 = (bf16[2,192,3072]{2,1,0:T(8,128)(2,1)S(1)}, bf16[2,192,3072]{2,1,0:T(8,128)(2,1)}, u32[]{:S(2)}) copy-start(bf16[2,192,3072]{2,1,0:T(8,128)(2,1)} %get-tuple-element.100.refs_3_) | copy-start | bytes 7077892
  220.7 11.2 %collective-permute-start.10 = (bf16[2,192,768]{2,1,0:T(8,128)(2,1)}, bf16[2,192,768]{2,1,0:T(8,128)(2,1)S(1)}, u32[]{:S(2)}, u32[]{:S(2)}) collective-permute-start(bf16[2,192,768]{2,1,0:T(8,128)(2,1)} %get-tuple-element.99), channel_id=1, source_target_pairs={{0,8},{8,0},{1,9},{9,1},{2,10},{10,2},{3,11},{11,3},{4,12},{12,4},... | collective-permute-start | bytes 1769480 | tf_op jit(solution)/shard_map/ppermute | solution.py:975
  225.1 59.5 %all-to-all-start.2 = ((bf16[16,24,3072]{2,1,0:T(8,128)(2,1)}), bf16[16,24,3072]{2,1,0:T(8,128)(2,1)S(1)}, u32[]{:S(2)}, u32[]{:S(2)}) async-start(bf16[16,24,3072]{2,1,0:T(8,128)(2,1)} %bitcast.33), calls=%async_computation.2 | async-start | bytes 4718592 | tf_op jit(solution)/shard_map/all_to_all | solution.py:979
  232.0 0.9 copy-start.4
  232.8 27.1 %copy-start.12 = (f32[1,3072]{1,0:T(1,128)S(1)}, f32[1,3072]{1,0:T(1,128)}, u32[]{:S(2)}) copy-start(f32[1,3072]{1,0:T(1,128)} %get-tuple-element.107) | copy-start | bytes 36868
  274.4 4.2 %collective-permute-start.12 = (bf16[2,192,1664]{2,1,0:T(8,128)(2,1)}, bf16[2,192,1664]{2,1,0:T(8,128)(2,1)}, u32[]{:S(2)}, u32[]{:S(2)}) collective-permute-start(bf16[2,192,1664]{2,1,0:T(8,128)(2,1)} %get-tuple-element.110), channel_id=1, source_target_pairs={{0,8},{8,0},{1,9},{9,1},{2,10},{10,2},{3,11},{11,3},{4,12},{12,4},... | collective-permute-start | bytes 3833864 | tf_op jit(solution)/shard_map/ppermute | solution.py:975
  274.4 3.7 %collective-permute-start.13 = (bf16[2,192,768]{2,1,0:T(8,128)(2,1)}, bf16[2,192,768]{2,1,0:T(8,128)(2,1)S(1)}, u32[]{:S(2)}, u32[]{:S(2)}) collective-permute-start(bf16[2,192,768]{2,1,0:T(8,128)(2,1)} %get-tuple-element.112), channel_id=1, source_target_pairs={{0,8},{8,0},{1,9},{9,1},{2,10},{10,2},{3,11},{11,3},{4,12},{12,4},... | collective-permute-start | bytes 1769480 | tf_op jit(solution)/shard_map/ppermute | solution.py:975
  278.1 0.8 copy-start.5
  283.1 7.4 %copy-start.20 = (bf16[96,1536]{1,0:T(8,128)(2,1)S(1)}, bf16[96,1536]{1,0:T(8,128)(2,1)}, u32[]{:S(2)}) copy-start(bf16[96,1536]{1,0:T(8,128)(2,1)} %get-tuple-element.115) | copy-start | bytes 884740
  283.1 9.3 %copy-start.19 = (bf16[96,1536]{1,0:T(8,128)(2,1)S(1)}, bf16[96,1536]{1,0:T(8,128)(2,1)}, u32[]{:S(2)}) copy-start(bf16[96,1536]{1,0:T(8,128)(2,1)} %get-tuple-element.116) | copy-start | bytes 884740
  283.1 10.8 %copy-start.18 = (bf16[96,1536]{1,0:T(8,128)(2,1)S(1)}, bf16[96,1536]{1,0:T(8,128)(2,1)}, u32[]{:S(2)}) copy-start(bf16[96,1536]{1,0:T(8,128)(2,1)} %get-tuple-element.117) | copy-start | bytes 884740
  284.6 22.8 %copy-start = (bf16[16,24,3072]{2,1,0:T(8,128)(2,1)}, bf16[16,24,3072]{2,1,0:T(8,128)(2,1)S(1)}, u32[]{:S(2)}) copy-start(bf16[16,24,3072]{2,1,0:T(8,128)(2,1)S(1)} %all-to-all-done.2.refs_0_) | copy-start | bytes 7077892
  284.6 50.5 %all-to-all-start.1 = ((bf16[16,24,1664]{2,1,0:T(8,128)(2,1)}), bf16[16,24,1664]{2,1,0:T(8,128)(2,1)}, u32[]{:S(2)}, u32[]{:S(2)}) async-start(bf16[16,24,1664]{2,1,0:T(8,128)(2,1)} %bitcast.59), calls=%async_computation.1 | async-start | bytes 2555904 | tf_op jit(solution)/shard_map/all_to_all | solution.py:979
  290.5 17.2 %collective-permute-start.14 = (bf16[96,1536]{1,0:T(8,128)(2,1)S(1)}, bf16[96,1536]{1,0:T(8,128)(2,1)S(1)}, u32[]{:S(2)}, u32[]{:S(2)}) collective-permute-start(bf16[96,1536]{1,0:T(8,128)(2,1)S(1)} %copy-done.20), channel_id=1, source_target_pairs={{0,1},{1,0},{16,17},{17,16},{2,3},{3,2},{18,19},{19,18},{4,5},{5,4... | collective-permute-start | bytes 884744 | tf_op jit(solution)/shard_map/ppermute | solution.py:774
  292.4 18.2 %collective-permute-start.15 = (bf16[96,1536]{1,0:T(8,128)(2,1)S(1)}, bf16[96,1536]{1,0:T(8,128)(2,1)S(1)}, u32[]{:S(2)}, u32[]{:S(2)}) collective-permute-start(bf16[96,1536]{1,0:T(8,128)(2,1)S(1)} %copy-done.19), channel_id=1, source_target_pairs={{0,16},{1,17},{16,0},{17,1},{2,18},{3,19},{18,2},{19,3},{4,20},{5,... | collective-permute-start | bytes 884744 | tf_op jit(solution)/shard_map/ppermute | solution.py:774
  293.9 28.3 %collective-permute-start.16 = (bf16[96,1536]{1,0:T(8,128)(2,1)S(1)}, bf16[96,1536]{1,0:T(8,128)(2,1)S(1)}, u32[]{:S(2)}, u32[]{:S(2)}) collective-permute-start(bf16[96,1536]{1,0:T(8,128)(2,1)S(1)} %copy-done.18), channel_id=1, source_target_pairs={{0,17},{1,16},{16,1},{17,0},{2,19},{3,18},{18,3},{19,2},{4,21},{5,... | collective-permute-start | bytes 884744 | tf_op jit(solution)/shard_map/ppermute | solution.py:774
  307.7 14.5 %copy-start.6 = (bf16[96,1536]{1,0:T(8,128)(2,1)}, bf16[96,1536]{1,0:T(8,128)(2,1)S(1)}, u32[]{:S(2)}) copy-start(bf16[96,1536]{1,0:T(8,128)(2,1)S(1)} %collective-permute-done.14.refs_2_) | copy-start | bytes 884740
  310.7 11.6 %copy-start.7 = (bf16[96,1536]{1,0:T(8,128)(2,1)}, bf16[96,1536]{1,0:T(8,128)(2,1)S(1)}, u32[]{:S(2)}) copy-start(bf16[96,1536]{1,0:T(8,128)(2,1)S(1)} %collective-permute-done.15.refs_3_) | copy-start | bytes 884740
  322.2 0.7 copy-start.8
  325.2 7.1 %collective-permute-start.17 = (bf16[24,1536]{1,0:T(8,128)(2,1)}, bf16[24,1536]{1,0:T(8,128)(2,1)S(1)}, u32[]{:S(2)}, u32[]{:S(2)}) collective-permute-start(bf16[24,1536]{1,0:T(8,128)(2,1)} %get-tuple-element.119), channel_id=1, source_target_pairs={{0,2},{2,0},{4,6},{6,4},{1,3},{3,1},{5,7},{7,5},{8,10},{10,8},{12,... | collective-permute-start | bytes 221192 | tf_op jit(solution)/shard_map/ppermute | solution.py:774
  325.5 8.3 %collective-permute-start.18 = (bf16[24,1536]{1,0:T(8,128)(2,1)}, bf16[24,1536]{1,0:T(8,128)(2,1)S(1)}, u32[]{:S(2)}, u32[]{:S(2)}) collective-permute-start(bf16[24,1536]{1,0:T(8,128)(2,1)} %get-tuple-element.120), channel_id=1, source_target_pairs={{0,4},{2,6},{4,0},{6,2},{1,5},{3,7},{5,1},{7,3},{8,12},{10,14},{12... | collective-permute-start | bytes 221192 | tf_op jit(solution)/shard_map/ppermute | solution.py:774
  328.7 6.5 %collective-permute-start.19 = (bf16[24,1536]{1,0:T(8,128)(2,1)}, bf16[24,1536]{1,0:T(8,128)(2,1)S(1)}, u32[]{:S(2)}, u32[]{:S(2)}) collective-permute-start(bf16[24,1536]{1,0:T(8,128)(2,1)} %get-tuple-element.121), channel_id=1, source_target_pairs={{0,6},{2,4},{4,2},{6,0},{1,7},{3,5},{5,3},{7,1},{8,14},{10,12},{12... | collective-permute-start | bytes 221192 | tf_op jit(solution)/shard_map/ppermute | solution.py:774
  332.3 2.9 copy-start.9
  333.8 1.3 copy-start.10
  335.2 0.6 copy-start.11
  338.5 16.2 %copy-start.13 = (f32[288]{0:T(512)S(1)}, f32[288]{0:T(512)}, u32[]{:S(2)}) copy-start(f32[288]{0:T(512)} %param.25) | copy-start | bytes 3460
  338.5 16.2 %copy-start.16 = (f32[288]{0:T(512)S(1)}, f32[288]{0:T(512)}, u32[]{:S(2)}) copy-start(f32[288]{0:T(512)} %param.34) | copy-start | bytes 3460
  338.5 16.2 %copy-start.17 = (f32[288]{0:T(512)S(1)}, f32[288]{0:T(512)}, u32[]{:S(2)}) copy-start(f32[288]{0:T(512)} %param.35) | copy-start | bytes 3460
Sparse Core Ops, SparseCore 0:
  11.5 95.7 all-gather.1
